TPU v7x, 256 devices: a whole 4x4x8 slice. The times are simulated.
256 devices in a mesh: src: 32 (over y_hi, z, core), tgt: 8 (over y_lo, x).
Axes of the slice: x: 4, y: 4 (y_hi: 2, y_lo: 2; y = y_hi * 2 + y_lo), z: 8, core: 2. Of those that a mesh axis runs over, the one named last changes fastest.
Arguments:
- source_cells: float32 [32, 32768], P(None, 'src'), may hold values from -2.6 to 2.6
- target_cells: float32 [32, 32768], P(None, 'tgt'), may hold values from -0.6 to 0.6
- start_potential: float32 [32768], P('tgt'), may hold values from -0.3 to 0.3
Outputs:
- source_potential: float32 [32768], P('src')
- target_potential: float32 [32768], P('tgt')
- source_image: float32 [32, 32768], P(None, 'src')
- target_image: float32 [32, 32768], P(None, 'tgt')
All inputs are finite; a program needn't handle non-finite values.
Results may differ from a plain program's by a relative error of at most 0.0003.
Values sent between devices are 32-bit elements; how exact they have to be, the bound alone decides.
No kernel may reach another device: no remote copies, remote signals or barrier semaphores. Data moves between devices by JAX's collectives and lax.ppermute only.
A program may use at most 64 MiB of HBM per device.

v0:
```python
import jax
import jax.numpy as jnp
from jax import lax
from jax.sharding import PartitionSpec as P

EPS = 0.05


def cross_cost(left, left_sq, right):
    cross = lax.dot_general(
        left,
        right,
        (((0,), (0,)), ((), ())),
        precision=lax.Precision.HIGHEST,
        preferred_element_type=jnp.float32,
    )
    return left_sq[:, None] + jnp.sum(right * right, 0)[None, :] - 2.0 * cross


def shards(source_cells, target_cells, start_potential):
    comps, src_rows = source_cells.shape
    tgt_rows = target_cells.shape[1]
    width = min(256, tgt_rows)
    blocks = tgt_rows // width
    total_src = src_rows * lax.axis_size("src")
    total_tgt = tgt_rows * lax.axis_size("tgt")
    src_sq = jnp.sum(source_cells * source_cells, 0)
    tgt_parts = target_cells.reshape(comps, blocks, width).transpose(1, 0, 2)
    start_parts = start_potential.reshape(blocks, width)

    def row_step(carry, pair):
        peak, mass = carry
        block, pots = pair
        scores = (pots[None, :] - cross_cost(source_cells, src_sq, block)) / EPS
        new_peak = jnp.maximum(peak, jnp.max(scores, 1))
        new_mass = mass * jnp.exp(peak - new_peak) + jnp.sum(jnp.exp(scores - new_peak[:, None]), 1)
        return ((new_peak, new_mass), None)

    row_init = (jnp.full((src_rows,), -1e30, jnp.float32), jnp.zeros((src_rows,), jnp.float32))
    (row_peak, row_mass), _ = lax.scan(row_step, row_init, (tgt_parts, start_parts))
    top = lax.pmax(row_peak, "tgt")
    row_mass = lax.psum(row_mass * jnp.exp(row_peak - top), "tgt")
    row_peak = top
    source_potential = -EPS * jnp.log(jnp.float32(total_src)) - EPS * (row_peak + jnp.log(row_mass))

    def column_step(block):
        scores = (source_potential[:, None] - cross_cost(source_cells, src_sq, block)) / EPS
        peak = jnp.max(scores, 0)
        return (peak, jnp.sum(jnp.exp(scores - peak[None, :]), 0))

    col_peak, col_mass = lax.map(column_step, tgt_parts)
    col_peak = col_peak.reshape(tgt_rows)
    col_mass = col_mass.reshape(tgt_rows)
    top = lax.pmax(col_peak, "src")
    col_mass = lax.psum(col_mass * jnp.exp(col_peak - top), "src")
    col_peak = top
    target_potential = -EPS * jnp.log(jnp.float32(total_tgt)) - EPS * (col_peak + jnp.log(col_mass))
    tgt_pots = target_potential.reshape(blocks, width)

    def image_step(carry, pair):
        src_numer, src_mass = carry
        block, pots = pair
        plan = jnp.exp(
            (source_potential[:, None] + pots[None, :] - cross_cost(source_cells, src_sq, block))
            / EPS
        )
        src_numer = src_numer + lax.dot_general(
            block,
            plan,
            (((1,), (1,)), ((), ())),
            precision=lax.Precision.HIGHEST,
            preferred_element_type=jnp.float32,
        )
        src_mass = src_mass + jnp.sum(plan, 1)
        tgt_numer = jnp.dot(
            source_cells, plan, precision=lax.Precision.HIGHEST, preferred_element_type=jnp.float32
        )
        return ((src_numer, src_mass), (tgt_numer, jnp.sum(plan, 0)))

    image_init = (jnp.zeros((comps, src_rows), jnp.float32), jnp.zeros((src_rows,), jnp.float32))
    (src_numer, src_mass), (tgt_numer, tgt_mass) = lax.scan(
        image_step, image_init, (tgt_parts, tgt_pots)
    )
    tgt_numer = tgt_numer.transpose(1, 0, 2).reshape(comps, tgt_rows)
    tgt_mass = tgt_mass.reshape(tgt_rows)
    src_numer, src_mass = lax.psum((src_numer, src_mass), "tgt")
    source_image = src_numer / src_mass[None, :]
    tgt_numer, tgt_mass = lax.psum((tgt_numer, tgt_mass), "src")
    target_image = tgt_numer / tgt_mass[None, :]
    return (source_potential, target_potential, source_image, target_image)


def solution(mesh):
    placed = (P(None, "src"), P(None, "tgt"), P("tgt"))
    return jax.shard_map(
        shards,
        mesh=mesh,
        in_specs=placed,
        out_specs=(P("src"), P("tgt"), P(None, "src"), P(None, "tgt")),
        check_vma=False,
    )
```

profile of v0, /device:TPU:32, one launch (start us, length us, event | category | flops | bytes accessed | tf_op | source)
XLA Modules:
  0.0 755.6 jit_solution(17000794373419457305)
XLA Ops:
  10.3 23.9 %while.43 = (s32[]{:T(128)}, f32[1024]{0:T(1024)S(1)}, f32[1024]{0:T(1024)S(1)}, f32[16,256]{1,0:T(8,128)S(1)}, f32[1024]{0:T(1024)S(1)}, /*index=5*/f32[16,32,2...) while((s32[]{:T(128)}, f32[1024]{0:T(1024)S(1)}, f32[1024]{0:T(1024)S(1)}, ...), condition=%wide.region_5.6_spmd.clone, body=%wide.region_1.5_spmd.clone.sunk | while | flops 102781696 | bytes 2356348 | solution.py:40
  13.4 1.2 fusion.59
  17.9 1.2 fusion.59
  25.3 1.2 fusion.59
  32.8 1.2 fusion.59
  34.3 19.7 %pmax.14 = f32[1024]{0:T(1024)S(1)} all-reduce(f32[1024]{0:T(1024)S(1)} %get-tuple-element.135), channel_id=1, replica_groups=mesh['src'=32,'tgt'=8] {'tgt'}, use_global_device_ids=true, to_apply=%region_6.7 | all-reduce | flops 1024 | bytes 8192 | tf_op jit(solution)/shard_map/pmax | solution.py:41
  54.0 16.0 %psum.42 = f32[1024]{0:T(1024)S(1)} all-reduce(f32[1024]{0:T(1024)S(1)} %exponential_multiply_fusion.1), channel_id=1, replica_groups=mesh['src'=32,'tgt'=8] {'tgt'}, use_global_device_ids=true, to_apply=%region_7.8 | all-reduce | flops 1024 | bytes 8192 | tf_op jit(solution)/shard_map/psum | solution.py:42
  70.0 28.2 %while.42 = (s32[]{:T(128)}, f32[16,256]{1,0:T(8,128)S(1)}, f32[16,256]{1,0:T(8,128)S(1)}, f32[1024]{0:T(1024)S(1)}, f32[1024]{0:T(1024)S(1)}, /*index=5*/f32[16...) while((s32[]{:T(128)}, f32[16,256]{1,0:T(8,128)S(1)}, f32[16,256]{1,0:T(8,128)S(1)}, ...), condition=%wide.region_12.13_spmd, body=%wide.region_8.12_spmd.sunk | while | flops 102776064 | bytes 2311285 | solution.py:51
  70.0 1.3 fusion.56
  71.8 1.3 fusion.56
  73.5 1.3 fusion.56
  75.3 1.3 fusion.56
  77.1 1.3 fusion.56
  78.8 1.3 fusion.56
  80.6 1.3 fusion.56
  82.3 1.3 fusion.56
  84.1 1.3 fusion.56
  85.9 1.3 fusion.56
  87.6 1.3 fusion.56
  89.4 1.3 fusion.56
  91.1 1.3 fusion.56
  92.9 1.3 fusion.56
  94.7 1.3 fusion.56
  96.4 1.3 fusion.56
  98.2 125.6 %pmax.15 = f32[4096]{0:T(1024)S(1)} all-reduce(f32[4096]{0:T(1024)S(1)} %bitcast.124), channel_id=1, replica_groups=mesh['src'=32,'tgt'=8] {'src'}, use_global_device_ids=true, to_apply=%region_13.14 | all-reduce | flops 4096 | bytes 32768 | tf_op jit(solution)/shard_map/pmax | solution.py:54
  223.8 128.5 %psum.43 = f32[4096]{0:T(1024)S(1)} all-reduce(f32[4096]{0:T(1024)S(1)} %exponential_multiply_fusion), channel_id=1, replica_groups=mesh['src'=32,'tgt'=8] {'src'}, use_global_device_ids=true, to_apply=%region_14.15 | all-reduce | flops 4096 | bytes 32768 | tf_op jit(solution)/shard_map/psum | solution.py:55
  352.9 52.6 %while.44 = (s32[]{:T(128)}, f32[32,1024]{1,0:T(8,128)S(1)}, f32[1024]{0:T(1024)S(1)}, f32[16,32,256]{2,1,0:T(8,128)S(1)}, f32[16,256]{1,0:T(8,128)S(1)}, /*inde...) while((s32[]{:T(128)}, f32[32,1024]{1,0:T(8,128)S(1)}, ...), condition=%wide.region_19.20_spmd.clone, body=%wide.region_15.19_spmd.clone.sunk | while | flops 304169472 | bytes 3834016 | solution.py:81
  353.0 1.4 fusion.67
  356.3 1.4 fusion.67
  359.6 1.4 fusion.67
  362.8 1.4 fusion.67
  366.1 1.4 fusion.67
  369.4 1.4 fusion.67
  372.7 1.4 fusion.67
  376.0 1.4 fusion.67
  379.3 1.4 fusion.67
  382.6 1.4 fusion.67
  385.9 1.4 fusion.67
  389.2 1.4 fusion.67
  392.5 1.4 fusion.67
  395.8 1.4 fusion.67
  399.1 1.4 fusion.67
  402.4 1.4 fusion.67
  407.2 18.0 %psum.45 = f32[1024]{0:T(1024)S(1)} all-reduce(f32[1024]{0:T(1024)S(1)} %get-tuple-element.140), channel_id=1, replica_groups=mesh['src'=32,'tgt'=8] {'tgt'}, use_global_device_ids=true, to_apply=%region_21.22 | all-reduce | flops 1024 | bytes 8192 | tf_op jit(solution)/shard_map/psum | solution.py:86
  425.2 128.5 %psum.47 = f32[4096]{0:T(1024)S(1)} all-reduce(f32[4096]{0:T(1024)S(1)} %bitcast.131), channel_id=1, replica_groups=mesh['src'=32,'tgt'=8] {'src'}, use_global_device_ids=true, to_apply=%region_23.24 | all-reduce | flops 4096 | bytes 32768 | tf_op jit(solution)/shard_map/psum | solution.py:88
  553.7 1.6 broadcast_divide_fusion.1
  555.3 191.6 %all-reduce.5.cloned.1.call-done = f32[32,4096]{1,0:T(8,128)} async-done(((f32[32,4096]{1,0:T(8,128)}), f32[32,4096]{1,0:T(8,128)}) %all-reduce.5.cloned.1.call-update) | async-done | bytes 524304 | tf_op jit(solution)/shard_map/psum | solution.py:88
  746.9 1.9 broadcast_divide_fusion
  (304 shorter events, 59.3 us)
Async XLA Ops:
  7.2 546.5 %all-reduce.3.cloned.1.call-start = ((), (), s32[]{:S(2)}) async-start(), calls=%async_computation | async-start | bytes 262144 | tf_op jit(solution)/shard_map/psum | solution.py:86
  7.3 0.9 copy-start.3
  9.4 0.9 copy-start
  352.3 0.6 copy-start.2
  405.6 0.7 copy-start.1
  405.6 0.7 copy-start.4
  406.3 340.6 %all-reduce.5.cloned.1.call-start = ((), (), s32[]{:S(2)}) async-start(), calls=%async_computation.1 | async-start | bytes 1048576 | tf_op jit(solution)/shard_map/psum | solution.py:88
Sparse Core Ops, SparseCore 0:
  406.4 76.6 all-reduce.2
  486.5 260.3 all-reduce.4
where the time goes:
time: 762 us; the launch traced here: 756 us
  blocking collectives  436 us (57%)
  waiting for transfers between devices  192 us (25%)
  matrix products  90.5 us (12%)
  between operations  14.2 us (2%)
  other arithmetic  14 us (2%)
    psum x1, waiting for transfers between devices, shards(): tgt_numer, tgt_mass = lax.psum((tgt_numer, tgt_mass), 'src')  192 us
    psum x1, blocking collectives, shards(): tgt_numer, tgt_mass = lax.psum((tgt_numer, tgt_mass), 'src')  128 us
    psum x1, blocking collectives, shards(): col_mass = lax.psum(col_mass * jnp.exp(col_peak - top), 'src')  128 us
    pmax x1, blocking collectives, shards(): top = lax.pmax(col_peak, 'src')  126 us
    dot_general x48, matrix products, cross_cost(): lax.dot_general(left, right, (((0,), (0,)), ((), ())), precision=lax.Prec...  63 us
    pmax x1, blocking collectives, shards(): top = lax.pmax(row_peak, 'tgt')  19.7 us
    psum x1, blocking collectives, shards(): src_numer, src_mass = lax.psum((src_numer, src_mass), 'tgt')  18 us
    dot_general x16, matrix products, image_step(): jnp.dot(source_cells, plan, precision=lax.Precision.HIGHEST, preferred_el...  16 us
  transfers between devices with their start and end apart: 2, of which 1 were waited for; matrix products, arithmetic and copies ran while one was open for 0% of the time, Pallas kernels for 0%

commit v1 on v0

v1 whole, which is shorter than its diff:
```python
import functools
import math

import jax
import jax.numpy as jnp
from jax import lax
from jax.experimental import pallas as pl
from jax.experimental.pallas import tpu as pltpu
from jax.sharding import PartitionSpec as P

EPS = 0.05
C2 = 1.4426950408889634 / EPS
LN = EPS * math.log(2.0)
BF = jnp.bfloat16
F32 = jnp.float32
K = 32
KD = 8 * K
VM = pl.BlockSpec(memory_space=pltpu.VMEM)
SM = pl.BlockSpec(memory_space=pltpu.SMEM)
LANES = 128


def thirds(v):
    hi = v.astype(BF)
    rest = v - hi.astype(F32)
    mid = rest.astype(BF)
    return hi, mid, (rest - mid.astype(F32)).astype(BF)


def left_rows(v):
    hi, mid, lo = thirds(v)
    return jnp.concatenate([hi, hi, hi, mid, mid, lo], 0)


def right_rows(v):
    hi, mid, lo = thirds(v)
    return jnp.concatenate([hi, mid, lo, hi, mid, hi], 0)


def bias_rows(b):
    hi, mid, lo = (part.astype(F32) for part in thirds(b))
    row = lax.broadcasted_iota(jnp.int32, (2 * K, b.shape[1]), 0)
    return jnp.where(row == 0, hi, jnp.where(row == 1, mid, jnp.where(row == 2, lo, 0.0))).astype(BF)


def halves(v):
    hi = v.astype(BF)
    return hi, (v - hi.astype(F32)).astype(BF)


def merge(logs, images):
    top = functools.reduce(jnp.maximum, logs)
    shares = [jnp.exp2(one - top) for one in logs]
    mass = functools.reduce(jnp.add, shares)
    image = functools.reduce(jnp.add, [w * i for w, i in zip(shares, images)])
    return top + jnp.log2(mass), image / mass


def row_sums(x_ref, y_ref, g_ref, out_ref, a_ref, b_ref, t_ref, m_ref, s_ref):
    ns, nt = x_ref.shape[1], y_ref.shape[1]
    rows_at_once = t_ref.shape[0]
    a_ref[...] = jnp.concatenate([left_rows(x_ref[...] * (2 * C2)), jnp.ones((2 * K, ns), BF)], 0).T
    y = y_ref[...]
    b_ref[0 : 6 * K, :] = right_rows(y)
    b_ref[6 * K : KD, :] = bias_rows((g_ref[...] - jnp.sum(y * y, 0, keepdims=True)) * C2)

    def block(r, _):
        rows = pl.ds(pl.multiple_of(r * rows_at_once, rows_at_once), rows_at_once)
        t_ref[...] = jnp.dot(a_ref[rows, :], b_ref[...], preferred_element_type=F32)
        cuts = [slice(c, c + LANES) for c in range(0, nt, LANES)]
        peak = functools.reduce(jnp.maximum, [t_ref[:, cut] for cut in cuts])
        m_ref[rows, :] = peak
        s_ref[rows, :] = functools.reduce(jnp.add, [jnp.exp2(t_ref[:, cut] - peak) for cut in cuts])
        return 0

    lax.fori_loop(0, ns // rows_at_once, block, 0)
    peak = m_ref[...].T
    top = jnp.max(peak, 0, keepdims=True)
    total = top + jnp.log2(jnp.sum(s_ref[...].T * jnp.exp2(peak - top), 0, keepdims=True))
    for d in range(out_ref.shape[0]):
        for k in range(ns // LANES):
            out_ref[d, k : k + 1, :] = total[:, k * LANES : (k + 1) * LANES]


def column_sums(log_n, core_ref, x_ref, y_ref, part_ref, pot_ref, keep_ref, send_ref, a_ref, b_ref, v_ref, t_ref):
    ns, nt = x_ref.shape[1], y_ref.shape[1]
    width = t_ref.shape[1]
    parts = part_ref[...]
    top = jnp.max(parts, 0)
    total = top + jnp.log2(jnp.sum(jnp.exp2(parts - top[None]), 0))
    total = jnp.concatenate([total[k : k + 1, :] for k in range(ns // LANES)], 1) + log_n
    x = x_ref[...]
    pot_ref[...] = jnp.sum(x * x, 0, keepdims=True) - LN * total
    a_ref[...] = jnp.concatenate([left_rows(x * (2 * C2)), bias_rows(-total)], 0).T
    b_ref[0 : 6 * K, :] = right_rows(y_ref[...])
    b_ref[6 * K : KD, :] = jnp.ones((2 * K, nt), BF)
    hi, lo = halves(x)
    v_ref[...] = jnp.concatenate([hi, lo, jnp.ones((K // 2, ns), BF)], 0)

    def work(out_ref, start, chunk):
        cols = pl.ds(pl.multiple_of(start + chunk * width, width), width)
        t_ref[...] = jnp.dot(a_ref[...], b_ref[:, cols], preferred_element_type=F32)
        peak = jnp.max(t_ref[...], 0, keepdims=True)
        hi, lo = halves(jnp.exp2(t_ref[...] - peak))
        sums = jnp.dot(v_ref[...], hi, preferred_element_type=F32) + jnp.dot(v_ref[...], lo, preferred_element_type=F32)
        mass = sums[2 * K : 2 * K + 1, :]
        image = (sums[0:K, :] + sums[K : 2 * K, :]) / mass
        logs = jnp.broadcast_to(peak + jnp.log2(mass), (8, width))
        per = width // LANES
        for k in range(per):
            out_ref[chunk * per + k, 0:K, :] = image[:, k * LANES : (k + 1) * LANES]
            out_ref[chunk * per + k, K : K + 8, :] = logs[:, k * LANES : (k + 1) * LANES]
        return 0

    core = core_ref[0]
    half = nt // 2
    lax.fori_loop(0, half // width, lambda c, _: work(send_ref, (1 - core) * half, c), 0)
    lax.fori_loop(0, half // width, lambda c, _: work(keep_ref, core * half, c), 0)


def merge_pair(one_ref, two_ref, out_ref):
    log, image = merge(
        [one_ref[:, K : K + 8, :][:, 0:1, :], two_ref[:, K : K + 8, :][:, 0:1, :]],
        [one_ref[:, 0:K, :], two_ref[:, 0:K, :]],
    )
    out_ref[:, 0:K, :] = image
    out_ref[:, K : K + 8, :] = jnp.broadcast_to(log, (out_ref.shape[0], 8, LANES))


def merge_chunk(part_ref, out_ref):
    n = part_ref.shape[0]
    log, image = merge([part_ref[d, K : K + 1, :] for d in range(n)], [part_ref[d, 0:K, :] for d in range(n)])
    for d in range(n):
        out_ref[d, 0:K, :] = image
        out_ref[d, K : K + 8, :] = jnp.broadcast_to(log, (8, LANES))


def row_images(
    log_n, core_ref, x_ref, y_ref, mine_ref, other_ref, pot_ref, img_ref, out_ref, a_ref, b_ref, v_ref, t_ref, o_ref, l_ref
):
    ns, nt = x_ref.shape[1], y_ref.shape[1]
    rows_at_once = t_ref.shape[0]
    core = core_ref[0]
    for side, ref in ((core, mine_ref), (1 - core, other_ref)):
        for q in range(ref.shape[0]):
            cols = pl.ds(pl.multiple_of(side * (nt // 2) + q * LANES, LANES), LANES)
            img_ref[:, cols] = ref[q, 0:K, :]
            l_ref[:, cols] = ref[q, K : K + 8, :]
    total = l_ref[0:1, :] + log_n
    y = y_ref[...]
    pot_ref[...] = jnp.sum(y * y, 0, keepdims=True) - LN * total
    a_ref[...] = jnp.concatenate([left_rows(x_ref[...] * (2 * C2)), jnp.ones((2 * K, ns), BF)], 0).T
    b_ref[0 : 6 * K, :] = right_rows(y)
    b_ref[6 * K : KD, :] = bias_rows(-total)
    hi, lo = halves(y)
    v_ref[...] = jnp.concatenate([hi, lo, jnp.ones((2 * K, nt), BF)], 0)
    by_last = (((1,), (1,)), ((), ()))

    def block(r, _):
        rows = pl.ds(pl.multiple_of(r * rows_at_once, rows_at_once), rows_at_once)
        t_ref[...] = jnp.dot(a_ref[rows, :], b_ref[...], preferred_element_type=F32)
        peak = functools.reduce(jnp.maximum, [t_ref[:, c : c + LANES] for c in range(0, nt, LANES)])
        peak = jnp.max(peak, 1, keepdims=True)
        hi, lo = halves(jnp.exp2(t_ref[...] - peak))
        sums = lax.dot_general(hi, v_ref[...], by_last, preferred_element_type=F32)
        sums += lax.dot_general(lo, v_ref[...], by_last, preferred_element_type=F32)
        mass = sums[:, 2 * K : 2 * K + 1]
        lane = lax.broadcasted_iota(jnp.int32, sums.shape, 1)
        o_ref[rows, :] = jnp.where(lane < 2 * K, sums / mass, peak + jnp.log2(mass))
        return 0

    lax.fori_loop(0, ns // rows_at_once, block, 0)
    sums = o_ref[...].T
    image = sums[0:K, :] + sums[K : 2 * K, :]
    tiles = ns // LANES
    for d in range(out_ref.shape[0]):
        for k in range(tiles):
            cut = slice(k * LANES, (k + 1) * LANES)
            out_ref[d, 0, k : k + 1, :] = sums[2 * K : 2 * K + 1, cut]
            for r in range(K // 8):
                out_ref[d, 1 + r * tiles + k] = image[8 * r : 8 * r + 8, cut]


def merge_rows(part_ref, out_ref):
    n, tiles = part_ref.shape[0], out_ref.shape[1] // LANES
    logs = [part_ref[d, 0] for d in range(n)]
    top = functools.reduce(jnp.maximum, logs)
    shares = [jnp.exp2(one - top) for one in logs]
    mass = functools.reduce(jnp.add, shares)
    shares = [one / mass for one in shares]
    for k in range(tiles):
        weights = [jnp.broadcast_to(one[k : k + 1, :], (8, LANES)) for one in shares]
        for r in range(K // 8):
            image = functools.reduce(jnp.add, [weights[d] * part_ref[d, 1 + r * tiles + k] for d in range(n)])
            out_ref[8 * r : 8 * r + 8, k * LANES : (k + 1) * LANES] = image


def call(kernel, ins, outs, scratch=()):
    return pl.pallas_call(
        kernel,
        out_shape=tuple(jax.ShapeDtypeStruct(shape, F32) for shape in outs),
        in_specs=[SM if spec == "s" else VM for spec in ins],
        out_specs=tuple(VM for _ in outs),
        scratch_shapes=[pltpu.VMEM(shape, dtype) for shape, dtype in scratch],
        compiler_params=pltpu.CompilerParams(vmem_limit_bytes=50 << 20),
    )


def solution(mesh):
    n_src, n_tgt = mesh.shape["src"], mesh.shape["tgt"]
    pairs = n_src // 2
    across = [[c + 2 * q for q in range(pairs)] for c in range(2)]
    swap = [(i, i ^ 1) for i in range(n_src)]

    def shards(x, y, g):
        ns, nt = x.shape[1], y.shape[1]
        tiles = ns // LANES
        core = (lax.axis_index("src") % 2).astype(jnp.int32).reshape(1)
        operands = [((ns, KD), BF), ((KD, nt), BF)]
        chunk = (pairs, K + 8, LANES)

        (part,) = call(
            row_sums,
            "vvv",
            [(n_tgt, tiles, LANES)],
            operands + [((256, nt), F32), ((ns, LANES), F32), ((ns, LANES), F32)],
        )(x, y, g.reshape(1, nt))
        part = lax.all_to_all(part, "tgt", 0, 0, tiled=True)

        source_potential, keep, send = call(
            functools.partial(column_sums, math.log2(ns * n_src)),
            "svvv",
            [(1, ns), chunk, chunk],
            operands + [((80, ns), BF), ((ns, 1024), F32)],
        )(core, x, y, part)
        (merged,) = call(merge_pair, "vv", [chunk])(keep, lax.ppermute(send, "src", swap))
        merged = lax.all_to_all(merged, "src", 0, 0, axis_index_groups=across, tiled=True)
        (whole,) = call(merge_chunk, "v", [chunk])(merged)
        mine = lax.all_to_all(whole, "src", 0, 0, axis_index_groups=across, tiled=True)
        other = lax.ppermute(mine, "src", swap)

        target_potential, target_image, part = call(
            functools.partial(row_images, math.log2(nt * n_tgt)),
            "svvvv",
            [(1, nt), (K, nt), (n_tgt, 1 + K // 8 * tiles, 8, LANES)],
            operands + [((LANES, nt), BF), ((256, nt), F32), ((ns, LANES), F32), ((8, nt), F32)],
        )(core, x, y, mine, other)
        part = lax.all_to_all(part, "tgt", 0, 0, tiled=True)
        (source_image,) = call(merge_rows, "v", [(K, ns)])(part)
        return source_potential.reshape(ns), target_potential.reshape(nt), source_image, target_image

    return jax.shard_map(
        shards,
        mesh=mesh,
        in_specs=(P(None, "src"), P(None, "tgt"), P("tgt")),
        out_specs=(P("src"), P("tgt"), P(None, "src"), P(None, "tgt")),
        check_vma=False,
    )
```

time: 762 us -> 110 us (0.14)
  blocking collectives: 436 us -> 60.2 us
  waiting for transfers between devices: 192 us -> 9.5 us
  matrix products: 90.5 us -> 0 us
  Pallas kernels: 0 us -> 29.8 us
  other arithmetic: 14 us -> 0 us
  between operations: 14.2 us -> 0.68 us
    psum x4 -> x0, blocking collectives: 291 us -> none  [the longest x1 128 us: shards(): tgt_numer, tgt_mass = lax.psum((tgt_numer, tgt_mass), 'src')]
    psum x2 -> x0, waiting for transfers between devices: 192 us -> none  [the longest x1 192 us: shards(): tgt_numer, tgt_mass = lax.psum((tgt_numer, tgt_mass), 'src')]
    pmax x2 -> x0, blocking collectives: 145 us -> none  [the longest x1 126 us: shards(): top = lax.pmax(col_peak, 'src')]
    dot_general x80 -> x0, matrix products: 90.5 us -> none  [the longest x48 63 us: cross_cost(): lax.dot_general(left, right, (((0,), (0,)), ((), ())), precision=lax.Prec...]
    all_to_all x0 -> x3, blocking collectives: none -> 60.2 us  [the longest x1 24 us: shards(): lax.all_to_all(merged, 'src', 0, 0, axis_index_groups=across, tiled=True)]
    pallas_call x0 -> x6, Pallas kernels: none -> 29.8 us  [the longest x1 14.7 us: shards(): call(functools.partial(row_images, math.log2(nt * n_tgt)), 'svvvv', [(1,...]
    reduce_sum x81 -> x0, other arithmetic: 10.2 us -> none  [the longest x16 5.11 us: column_step(): return (peak, jnp.sum(jnp.exp(scores - peak[None, :]), 0))]
  transfers between devices with their start and end apart: 2 -> 3, of which waited for: 1 -> 3; matrix products, arithmetic and copies ran while one was open for 0% -> 0% of each run, Pallas kernels for 0% -> 0%
where the time goes in v1:
time: 110 us; the launch traced here: 109 us
  blocking collectives  60.2 us (55%)
  Pallas kernels  29.8 us (27%)
  waiting for transfers between devices  9.5 us (9%)
  starting transfers between devices  5.41 us (5%)
  local copies, waits for them, and re-layouts  3.57 us (3%)
    all_to_all x1, blocking collectives, shards(): lax.all_to_all(merged, 'src', 0, 0, axis_index_groups=across, tiled=True)  24 us
    all_to_all x1, blocking collectives, shards(): part = lax.all_to_all(part, 'tgt', 0, 0, tiled=True)  19.2 us
    all_to_all x1, blocking collectives, shards(): lax.all_to_all(whole, 'src', 0, 0, axis_index_groups=across, tiled=True)  17.1 us
    pallas_call x1, Pallas kernels, shards(): call(functools.partial(row_images, math.log2(nt * n_tgt)), 'svvvv', [(1,...  14.7 us
    pallas_call x1, Pallas kernels, shards(): call(functools.partial(column_sums, math.log2(ns * n_src)), 'svvv', [(1,...  7.77 us
    pallas_call x1, Pallas kernels, shards(): call(row_sums, 'vvv', [(n_tgt, tiles, LANES)], operands + [((256, nt), F3...  6.47 us
    all_to_all x1, waiting for transfers between devices, shards(): part = lax.all_to_all(part, 'tgt', 0, 0, tiled=True)  6.26 us
    all_to_all x1, starting transfers between devices, shards(): part = lax.all_to_all(part, 'tgt', 0, 0, tiled=True)  5.31 us
  transfers between devices with their start and end apart: 3, of which 3 were waited for; matrix products, arithmetic and copies ran while one was open for 0% of the time, Pallas kernels for 0%

profile of v1, /device:TPU:32, one launch (start us, length us, event | category | flops | bytes accessed | tf_op | source)
XLA Modules:
  0.0 109.2 jit_solution(12046483187651302681)
XLA Ops:
  0.6 0.0 copy-start
  0.6 1.0 copy-done
  1.7 0.0 copy-start.2
  1.7 0.9 copy-done.2
  2.6 0.0 copy-start.5
  2.6 0.7 copy-done.5
  3.3 0.0 copy-start.1
  3.3 6.5 %shard_map.66 = f32[8,8,128]{2,1,0:T(8,128)} custom-call(f32[32,1024]{1,0:T(8,128)S(1)} %copy-done.2, f32[32,4096]{1,0:T(8,128)S(1)} %copy-done, f32[1,4096]{1,0:T(1,128)S(1)} %bitcast.4), custom_call_target="tpu_custom_call" | custom-call | tf_op jit(solution)/shard_map/pallas_call | solution.py:222
  9.8 5.3 %all-to-all-start = ((f32[8,8,128]{2,1,0:T(8,128)}), f32[8,8,128]{2,1,0:T(8,128)S(1)}, u32[]{:S(2)}, u32[]{:S(2)}) async-start(f32[8,8,128]{2,1,0:T(8,128)} %shard_map.66), calls=%async_computation | async-start | bytes 65536 | tf_op jit(solution)/shard_map/all_to_all | solution.py:228
  15.1 6.3 %all-to-all-done.part_ref = f32[8,8,128]{2,1,0:T(8,128)S(1)} async-done(((f32[8,8,128]{2,1,0:T(8,128)}), f32[8,8,128]{2,1,0:T(8,128)S(1)}, u32[]{:S(2)}, u32[]{:S(2)}) %all-to-all-start) | async-done | bytes 32800 | tf_op jit(solution)/shard_map/all_to_all | solution.py:228
  21.3 0.0 copy-done.1
  21.3 0.0 copy-start.3
  21.3 0.9 copy-done.3
  22.2 7.8 %shard_map.67 = (f32[1,1024]{1,0:T(1,128)}, f32[16,40,128]{2,1,0:T(8,128)S(1)}, f32[16,40,128]{2,1,0:T(8,128)S(1)}) custom-call(s32[1]{0:T(128)} %bitcast.core_ref, f32[32,1024]{1,0:T(8,128)S(1)} %copy-done.3, f32[32,4096]{1,0:T(8,128)S(1)} %copy-done.1, f32[8,8,128]{2,1,0:T(8,128)S(1)} %all-to-all-done.part_ref), custom_call_target="tpu_custom_call" | custom-call | tf_op jit(solution)/shard_map/pallas_call | solution.py:230
  30.0 0.1 collective-permute-start
  30.1 1.6 %collective-permute-done.two_ref = f32[16,40,128]{2,1,0:T(8,128)S(1)} collective-permute-done((f32[16,40,128]{2,1,0:T(8,128)S(1)}, f32[16,40,128]{2,1,0:T(8,128)S(1)}, u32[]{:S(2)}, u32[]{:S(2)}) %collective-permute-start) | collective-permute-done | bytes 327712 | tf_op jit(solution)/shard_map/ppermute | solution.py:236
  31.7 0.1 shard_map.68
  31.8 0.0 copy-start.4
  31.8 24.0 %all_to_all.20.part_ref = f32[16,40,128]{2,1,0:T(8,128)S(1)} all-to-all(f32[16,40,128]{2,1,0:T(8,128)S(1)} %shard_map.68), channel_id=1, replica_groups={{0,16,32,48,64,80,96,112,128,144,160,176,192,208,224,240},{8,24,40,56,7..., dimensions={0} | all-to-all | bytes 655360 | tf_op jit(solution)/shard_map/all_to_all | solution.py:237
  55.8 0.1 shard_map.69
  55.9 17.1 %all_to_all.21.mine_ref = f32[16,40,128]{2,1,0:T(8,128)S(1)} all-to-all(f32[16,40,128]{2,1,0:T(8,128)S(1)} %shard_map.69), channel_id=1, replica_groups={{0,16,32,48,64,80,96,112,128,144,160,176,192,208,224,240},{8,24,40,56,7..., dimensions={0} | all-to-all | bytes 655360 | tf_op jit(solution)/shard_map/all_to_all | solution.py:239
  72.9 0.0 collective-permute-start.1
  72.9 1.6 %collective-permute-done.1.other_ref = f32[16,40,128]{2,1,0:T(8,128)S(1)} collective-permute-done((f32[16,40,128]{2,1,0:T(8,128)S(1)}, f32[16,40,128]{2,1,0:T(8,128)S(1)}, u32[]{:S(2)}, u32[]{:S(2)}) %collective-permute-start.1) | collective-permute-done | bytes 327712 | tf_op jit(solution)/shard_map/ppermute | solution.py:240
  74.6 0.0 copy-done.4
  74.6 14.7 %shard_map.70 = (f32[1,4096]{1,0:T(1,128)}, f32[32,4096]{1,0:T(8,128)}, f32[8,33,8,128]{3,2,1,0:T(8,128)S(1)}) custom-call(s32[1]{0:T(128)} %bitcast.core_ref, f32[32,1024]{1,0:T(8,128)S(1)} %copy-done.4, f32[32,4096]{1,0:T(8,128)S(1)} %copy-done.1, f32[16,40,128]{2,1,0:T(8,128)S(1)} %all_to_all.21.mine_ref, f32[16,40,128]{2,1,0:T(8,128)S(1)} %collective-permute-done.1.other_ref), custom_call_target="tpu_custom_call" | custom-call | tf_op jit(solution)/shard_map/pallas_call | solution.py:242
  89.2 19.2 %all_to_all.22.part_ref = f32[8,33,8,128]{3,2,1,0:T(8,128)S(1)} all-to-all(f32[8,33,8,128]{3,2,1,0:T(8,128)S(1)} %get-tuple-element.14), channel_id=1, replica_groups=mesh['src'=32,'tgt'=8] {'tgt'}, dimensions={0} | all-to-all | bytes 2162688 | tf_op jit(solution)/shard_map/all_to_all | solution.py:248
  108.5 0.8 shard_map.71
Async XLA Ops:
  0.6 1.0 copy-start
  1.7 0.9 copy-start.2
  2.6 0.7 copy-start.5
  3.3 18.0 %copy-start.1 = (f32[32,4096]{1,0:T(8,128)S(1)}, f32[32,4096]{1,0:T(8,128)}, u32[]{:S(2)}) copy-start(f32[32,4096]{1,0:T(8,128)} %y_ref.5) | copy-start | bytes 1572868
  9.8 11.6 %all-to-all-start = ((f32[8,8,128]{2,1,0:T(8,128)}), f32[8,8,128]{2,1,0:T(8,128)S(1)}, u32[]{:S(2)}, u32[]{:S(2)}) async-start(f32[8,8,128]{2,1,0:T(8,128)} %shard_map.66), calls=%async_computation | async-start | bytes 65536 | tf_op jit(solution)/shard_map/all_to_all | solution.py:228
  21.3 0.9 copy-start.3
  30.0 1.7 %collective-permute-start = (f32[16,40,128]{2,1,0:T(8,128)S(1)}, f32[16,40,128]{2,1,0:T(8,128)S(1)}, u32[]{:S(2)}, u32[]{:S(2)}) collective-permute-start(f32[16,40,128]{2,1,0:T(8,128)S(1)} %get-tuple-element.12), channel_id=1, source_target_pairs={{0,8},{8,0},{16,24},{24,16},{32,40},{40,32},{48,56},{56,48},{64,72... | collective-permute-start | bytes 983048 | tf_op jit(solution)/shard_map/ppermute | solution.py:236
  31.8 42.7 %copy-start.4 = (f32[32,1024]{1,0:T(8,128)S(1)}, f32[32,1024]{1,0:T(8,128)}, u32[]{:S(2)}) copy-start(f32[32,1024]{1,0:T(8,128)} %x_ref.5) | copy-start | bytes 393220
  72.9 1.6 %collective-permute-start.1 = (f32[16,40,128]{2,1,0:T(8,128)S(1)}, f32[16,40,128]{2,1,0:T(8,128)S(1)}, u32[]{:S(2)}, u32[]{:S(2)}) collective-permute-start(f32[16,40,128]{2,1,0:T(8,128)S(1)} %all_to_all.21.mine_ref), channel_id=1, source_target_pairs={{0,8},{8,0},{16,24},{24,16},{32,40},{40,32},{48,56},{56,48},{64,72... | collective-permute-start | bytes 983048 | tf_op jit(solution)/shard_map/ppermute | solution.py:240

commit v2 on v0

v2 whole, which is shorter than its diff:
```python
import functools
import math

import jax
import jax.numpy as jnp
from jax import lax
from jax.experimental import pallas as pl
from jax.experimental.pallas import tpu as pltpu
from jax.sharding import PartitionSpec as P

EPS = 0.05
C2 = 1.4426950408889634 / EPS
LN = EPS * math.log(2.0)
LEAST = 2.0**-80
LIFT = 64.0
BF = jnp.bfloat16
F32 = jnp.float32
K = 32
KD = 8 * K
VM = pl.BlockSpec(memory_space=pltpu.VMEM)
SM = pl.BlockSpec(memory_space=pltpu.SMEM)
LANES = 128
TALL, WIDE = 1024, 512
BLOCK = ((TALL, WIDE), F32)


def thirds(v):
    hi = v.astype(BF)
    rest = v - hi.astype(F32)
    mid = rest.astype(BF)
    return hi, mid, (rest - mid.astype(F32)).astype(BF)


def halves(v):
    hi = v.astype(BF)
    return hi, (v - hi.astype(F32)).astype(BF)


def offsets(b, first):
    hi, mid, lo = (part.astype(F32) for part in thirds(b))
    row = lax.broadcasted_iota(jnp.int32, (2 * K, b.shape[1]), 0)
    row, one = (row, row - 3) if first else (row - 3, row)
    value = jnp.where(row == 0, hi, jnp.where(row == 1, mid, jnp.where(row == 2, lo, 0.0)))
    return jnp.where((one >= 0) & (one < 3), 1.0, value).astype(BF)


def first_side(v, b):
    hi, mid, lo = thirds(v)
    return jnp.concatenate([hi, hi, hi, mid, mid, lo, offsets(b, True)], 0)


def second_side(v, b):
    hi, mid, lo = thirds(v)
    return jnp.concatenate([hi, mid, lo, hi, mid, hi, offsets(b, False)], 0)


def coordinates(v):
    hi, lo = halves(v)
    return jnp.concatenate([hi, lo, jnp.ones((K // 2, v.shape[1]), BF)], 0)


def cut(tiles, k):
    return tiles[:, k * LANES : (k + 1) * LANES]


def blocks(a_ref, b_ref, t_refs, first, use):
    tall, wide = t_refs[0].shape
    places = [(r, c) for c in range(first, first + b_ref.shape[1], wide) for r in range(0, a_ref.shape[0], tall)]

    def fill(i):
        r, c = places[i]
        t_refs[i % 2][...] = jnp.dot(a_ref[r : r + tall, :], b_ref[:, c : c + wide], preferred_element_type=F32)

    fill(0)
    for i, (r, c) in enumerate(places):
        if i + 1 < len(places):
            fill(i + 1)
        use(t_refs[i % 2], slice(r, r + tall), slice(c, c + wide))


def log_sums(a_ref, b_ref, t_refs, l_ref):
    tall, wide = t_refs[0].shape

    def use(t_ref, rows, cols):
        part = jnp.sum(jnp.exp2(t_ref[...]), 0, keepdims=True)
        l_ref[:, cols] = part if rows.start == 0 else l_ref[:, cols] + part

    blocks(a_ref, b_ref, t_refs, 0, use)
    least = jnp.min(l_ref[...])
    l_ref[...] = jnp.log2(l_ref[...])

    @pl.when(least < LEAST)
    def _():
        t_ref = t_refs[0]

        def column(c, _):
            cols = pl.ds(pl.multiple_of(c * wide, wide), wide)

            def fill(r):
                rows = pl.ds(pl.multiple_of(r * tall, tall), tall)
                t_ref[...] = jnp.dot(a_ref[rows, :], b_ref[:, cols], preferred_element_type=F32)

            def highest(r, peak):
                fill(r)
                return jnp.maximum(peak, jnp.max(t_ref[...], 0, keepdims=True))

            count = a_ref.shape[0] // tall
            peak = lax.fori_loop(0, count, highest, jnp.full((1, wide), -1e30, F32))

            def add(r, total):
                fill(r)
                return total + jnp.sum(jnp.exp2(t_ref[...] - peak), 0, keepdims=True)

            l_ref[:, cols] = peak + jnp.log2(lax.fori_loop(0, count, add, jnp.zeros((1, wide), F32)))
            return 0

        lax.fori_loop(0, b_ref.shape[1] // wide, column, 0)


def weighted(a_ref, b_ref, v_ref, t_refs, o_ref):
    def use(t_ref, rows, cols):
        hi, lo = halves(jnp.exp2(t_ref[...]))
        part = jnp.dot(v_ref[:, rows], hi, preferred_element_type=F32)
        part += jnp.dot(v_ref[:, rows], lo, preferred_element_type=F32)
        o_ref[:, cols] = part if rows.start == 0 else o_ref[:, cols] + part

    blocks(a_ref, b_ref, t_refs, 0, use)


def row_logs(x_ref, y_ref, g_ref, out_ref, a_ref, b_ref, l_ref, *t_refs):
    x, y = x_ref[...], y_ref[...]
    y_sq = jnp.sum(y * y, 0, keepdims=True)
    lift = (g_ref[...] - y_sq) * C2
    longest = jnp.sqrt(jnp.sum(x * x, 0, keepdims=True)) * jnp.sqrt(jnp.max(y_sq, 1, keepdims=True))
    bound = jnp.max(lift, 1, keepdims=True) + 2 * C2 * longest
    a_ref[...] = first_side(y, lift).T
    b_ref[...] = second_side(x * (2 * C2), -bound)
    log_sums(a_ref, b_ref, t_refs, l_ref)
    total = l_ref[...] + bound
    for k in range(out_ref.shape[1]):
        for d in range(out_ref.shape[0]):
            out_ref[d, k : k + 1, :] = cut(total, k)


def column_logs(log_n, x_ref, y_ref, g_ref, part_ref, pot_ref, total_ref, log_ref, out_ref, a_ref, b_ref, l_ref, *t_refs):
    parts = part_ref[...]
    top = jnp.max(parts, 0)
    total = top + jnp.log2(jnp.sum(jnp.exp2(parts - top[None]), 0))
    total = jnp.concatenate([total[k : k + 1, :] for k in range(total.shape[0])], 1) + log_n
    total_ref[...] = total
    x, y = x_ref[...], y_ref[...]
    pot_ref[...] = jnp.sum(x * x, 0, keepdims=True) - LN * total
    bound = (jnp.sum(y * y, 0, keepdims=True) - g_ref[...]) * C2 - log_n
    a_ref[...] = first_side(x * (2 * C2), -total).T
    b_ref[...] = second_side(y, -bound)
    log_sums(a_ref, b_ref, t_refs, l_ref)
    logs = l_ref[...] + bound
    log_ref[...] = logs
    for k in range(out_ref.shape[1]):
        out_ref[0, k : k + 1, :] = cut(logs, k)
    for d in range(1, out_ref.shape[0]):
        out_ref[d] = out_ref[0]


def column_images(core_ref, x_ref, y_ref, total_ref, log_ref, keep_ref, send_ref, a_ref, b_ref, v_ref, o_ref, *t_refs):
    x = x_ref[...]
    a_ref[...] = first_side(x * (2 * C2), -total_ref[...]).T
    b_ref[...] = second_side(y_ref[...], -log_ref[...])
    v_ref[...] = coordinates(x)
    weighted(a_ref, b_ref, v_ref, t_refs, o_ref)
    half = o_ref.shape[1] // 2
    for out_ref, side in ((send_ref, 1 - core_ref[0]), (keep_ref, core_ref[0])):
        for q in range(out_ref.shape[0]):
            cols = pl.ds(pl.multiple_of(side * half + q * LANES, LANES), LANES)
            out_ref[q, 0:K, :] = (o_ref[0:K, cols] + o_ref[K : 2 * K, cols]) / o_ref[2 * K : 2 * K + 1, cols]
            out_ref[q, K : K + 8, :] = jnp.broadcast_to(log_ref[:, cols], (8, LANES))


def merge(logs, images):
    top = functools.reduce(jnp.maximum, logs)
    shares = [jnp.exp2(one - top) for one in logs]
    mass = functools.reduce(jnp.add, shares)
    image = functools.reduce(jnp.add, [w * i for w, i in zip(shares, images)])
    return top + jnp.log2(mass), image / mass


def merge_pair(one_ref, two_ref, out_ref):
    logs = [ref[:, K : K + 8, :][:, 0:1, :] for ref in (one_ref, two_ref)]
    log, image = merge(logs, [one_ref[:, 0:K, :], two_ref[:, 0:K, :]])
    out_ref[:, 0:K, :] = image
    out_ref[:, K : K + 8, :] = jnp.broadcast_to(log, (out_ref.shape[0], 8, LANES))


def merge_chunk(part_ref, out_ref):
    n = part_ref.shape[0]
    _, image = merge([part_ref[d, K : K + 1, :] for d in range(n)], [part_ref[d, 0:K, :] for d in range(n)])
    for d in range(n):
        out_ref[d] = image


def merge_logs(part_ref, out_ref):
    n = part_ref.shape[0]
    top = functools.reduce(jnp.maximum, [part_ref[d] for d in range(n)])
    out_ref[...] = top + jnp.log2(functools.reduce(jnp.add, [jnp.exp2(part_ref[d] - top) for d in range(n)]))


def row_images(log_n, side_ref, x_ref, y_ref, total_ref, mine_ref, other_ref, pot_ref, out_ref, a_ref, b_ref, v_ref, o_ref, *t_refs):
    mine, other = mine_ref[...], other_ref[...]
    top = jnp.maximum(mine, other)
    logs = top + jnp.log2(jnp.exp2(mine - top) + jnp.exp2(other - top))
    logs = jnp.concatenate([logs[k : k + 1, :] for k in range(logs.shape[0])], 1)
    y = y_ref[...]
    pot_ref[...] = jnp.sum(y * y, 0, keepdims=True) - LN * (logs + log_n)
    half = o_ref.shape[1]
    cols = pl.ds(pl.multiple_of(side_ref[0] * half, half), half)
    a_ref[...] = first_side(y, -logs).T
    b_ref[...] = second_side(x_ref[:, cols] * (2 * C2), LIFT - total_ref[:, cols])
    v_ref[...] = coordinates(y)
    weighted(a_ref, b_ref, v_ref, t_refs, o_ref)
    tiles = half // LANES
    for k in range(tiles):
        lanes = slice(k * LANES, (k + 1) * LANES)
        for r in range(0, K, 8):
            out_ref[r * tiles + 8 * k : r * tiles + 8 * k + 8, :] = o_ref[r : r + 8, lanes] + o_ref[K + r : K + r + 8, lanes]
        out_ref[K * tiles + k : K * tiles + k + 1, :] = o_ref[2 * K : 2 * K + 1, lanes]
    out_ref[K * tiles + tiles :, :] = jnp.ones((out_ref.shape[0] - (K + 1) * tiles, LANES), F32)


def add_divide(one_ref, two_ref, out_ref):
    rows = out_ref.shape[0]
    tiles = rows // K
    mass = one_ref[rows : rows + 8, :] + two_ref[rows : rows + 8, :]
    for k in range(tiles):
        under = jnp.broadcast_to(mass[k : k + 1, :], (8, LANES))
        for r in range(0, K, 8):
            at = slice(r * tiles + 8 * k, r * tiles + 8 * k + 8)
            out_ref[at, :] = (one_ref[at, :] + two_ref[at, :]) / under


def lay_rows(side_ref, mine_ref, other_ref, out_ref):
    half = out_ref.shape[1] // 2
    tiles = half // LANES
    for side, ref in ((side_ref[0], mine_ref), (1 - side_ref[0], other_ref)):
        for k in range(tiles):
            cols = pl.ds(pl.multiple_of(side * half + k * LANES, LANES), LANES)
            for r in range(0, K, 8):
                out_ref[r : r + 8, cols] = ref[r * tiles + 8 * k : r * tiles + 8 * k + 8, :]


def lay_columns(core_ref, mine_ref, other_ref, out_ref):
    half = out_ref.shape[1] // 2
    for side, ref in ((core_ref[0], mine_ref), (1 - core_ref[0], other_ref)):
        for q in range(ref.shape[0]):
            out_ref[:, pl.ds(pl.multiple_of(side * half + q * LANES, LANES), LANES)] = ref[q]


def call(kernel, ins, outs, scratch=()):
    return pl.pallas_call(
        kernel,
        out_shape=tuple(jax.ShapeDtypeStruct(shape, F32) for shape in outs),
        in_specs=[SM if spec == "s" else VM for spec in ins],
        out_specs=tuple(VM for _ in outs),
        scratch_shapes=[pltpu.VMEM(shape, dtype) for shape, dtype in scratch],
        compiler_params=pltpu.CompilerParams(vmem_limit_bytes=50 << 20),
    )


def solution(mesh):
    n_src, n_tgt = mesh.shape["src"], mesh.shape["tgt"]
    pairs, ring = n_src // 2, n_tgt // 2
    across = [[c + 2 * q for q in range(pairs)] for c in range(2)]
    swap = [(i, i ^ 1) for i in range(n_src)]
    over = [(i, (i + ring) % n_tgt) for i in range(n_tgt)]
    near = [(i, i ^ 1) for i in range(n_tgt)]
    far = [(i, i ^ 3) for i in range(n_tgt)]

    def shards(x, y, g):
        ns, nt = x.shape[1], y.shape[1]
        rows, cols = ns // LANES, nt // LANES
        core = (lax.axis_index("src") & 1).astype(jnp.int32).reshape(1)
        side = (lax.axis_index("tgt") // ring).astype(jnp.int32).reshape(1)
        g = g.reshape(1, nt)
        by_source = [((ns, KD), BF), ((KD, nt), BF)]
        chunk = (pairs, K + 8, LANES)

        (part,) = call(
            row_logs, "vvv", [(n_tgt, rows, LANES)], [((nt, KD), BF), ((KD, ns), BF), ((1, ns), F32), BLOCK, BLOCK]
        )(x, y, g)
        part = lax.all_to_all(part, "tgt", 0, 0, tiled=True)

        source_potential, total, logs, part = call(
            functools.partial(column_logs, math.log2(ns * n_src)),
            "vvvv",
            [(1, ns), (1, ns), (1, nt), (pairs, cols, LANES)],
            by_source + [((1, nt), F32), BLOCK, BLOCK],
        )(x, y, g, part)
        part = lax.all_to_all(part, "src", 0, 0, axis_index_groups=across, tiled=True)
        (mine,) = call(merge_logs, "v", [(cols, LANES)])(part)
        other = lax.ppermute(mine, "src", swap)

        keep, send = call(
            column_images, "svvvv", [chunk, chunk], by_source + [((80, ns), BF), ((80, nt), F32), BLOCK, BLOCK]
        )(core, x, y, total, logs)
        (image,) = call(merge_pair, "vv", [chunk])(keep, lax.ppermute(send, "src", swap))
        image = lax.all_to_all(image, "src", 0, 0, axis_index_groups=across, tiled=True)

        half = ns // 2
        tall = (K * half) // LANES
        images = call(
            functools.partial(row_images, math.log2(nt * n_tgt)),
            "svvvvv",
            [(1, nt), (tall + 8, LANES)],
            [((nt, KD), BF), ((KD, half), BF), ((80, nt), BF), ((80, half), F32), BLOCK, BLOCK],
        )
        target_potential, sent = images(1 - side, x, y, total, mine, other)
        sent = lax.ppermute(sent, "tgt", over)
        _, held = images(side, x, y, total, mine, other)
        held = held + sent
        held = held + lax.ppermute(held, "tgt", near)
        (held,) = call(add_divide, "vv", [(tall, LANES)])(held, lax.ppermute(held, "tgt", far))
        (source_image,) = call(lay_rows, "svv", [(K, ns)])(side, held, lax.ppermute(held, "tgt", over))

        (image,) = call(merge_chunk, "v", [(pairs, K, LANES)])(image)
        image = lax.all_to_all(image, "src", 0, 0, axis_index_groups=across, tiled=True)
        (target_image,) = call(lay_columns, "svv", [(K, nt)])(core, image, lax.ppermute(image, "src", swap))
        return source_potential.reshape(ns), target_potential.reshape(nt), source_image, target_image

    return jax.shard_map(
        shards,
        mesh=mesh,
        in_specs=(P(None, "src"), P(None, "tgt"), P("tgt")),
        out_specs=(P("src"), P("tgt"), P(None, "src"), P(None, "tgt")),
        check_vma=False,
    )
```

time: 762 us -> 114 us (0.15)
  blocking collectives: 436 us -> 23.8 us
  waiting for transfers between devices: 192 us -> 38.6 us
  matrix products: 90.5 us -> 0 us
  Pallas kernels: 0 us -> 30.2 us
  starting transfers between devices: 0.08 us -> 17.1 us
  other arithmetic: 14 us -> 0.02 us
  between operations: 14.2 us -> 0.72 us
    psum x4 -> x0, blocking collectives: 291 us -> none  [the longest x1 128 us: shards(): tgt_numer, tgt_mass = lax.psum((tgt_numer, tgt_mass), 'src')]
    psum x2 -> x0, waiting for transfers between devices: 192 us -> none  [the longest x1 192 us: shards(): tgt_numer, tgt_mass = lax.psum((tgt_numer, tgt_mass), 'src')]
    pmax x2 -> x0, blocking collectives: 145 us -> none  [the longest x1 126 us: shards(): top = lax.pmax(col_peak, 'src')]
    dot_general x80 -> x0, matrix products: 90.5 us -> none  [the longest x48 63 us: cross_cost(): lax.dot_general(left, right, (((0,), (0,)), ((), ())), precision=lax.Prec...]
    pallas_call x0 -> x11, Pallas kernels: none -> 30.2 us  [the longest x1 10.9 us: shards(): call(row_logs, 'vvv', [(n_tgt, rows, LANES)], [((nt, KD), BF), ((KD, ns),...]
    all_to_all x0 -> x1, blocking collectives: none -> 23.8 us  [shards(): lax.all_to_all(image, 'src', 0, 0, axis_index_groups=across, tiled=True)]
    all_to_all x0 -> x3, waiting for transfers between devices: none -> 23.4 us  [the longest x1 10.7 us: shards(): lax.all_to_all(part, 'src', 0, 0, axis_index_groups=across, tiled=True)]
    ppermute x0 -> x7, waiting for transfers between devices: none -> 15.3 us  [the longest x1 4.29 us: shards(): lax.ppermute(held, 'tgt', far)]
  transfers between devices with their start and end apart: 2 -> 10, of which waited for: 1 -> 8; matrix products, arithmetic and copies ran while one was open for 0% -> 0% of each run, Pallas kernels for 0% -> 8%
where the time goes in v2:
time: 114 us; the launch traced here: 113 us
  waiting for transfers between devices  38.6 us (34%)
  Pallas kernels  30.2 us (26%)
  blocking collectives  23.8 us (21%)
  starting transfers between devices  17.1 us (15%)
  local copies, waits for them, and re-layouts  2.67 us (2%)
    all_to_all x1, blocking collectives, shards(): lax.all_to_all(image, 'src', 0, 0, axis_index_groups=across, tiled=True)  23.8 us
    pallas_call x1, Pallas kernels, shards(): call(row_logs, 'vvv', [(n_tgt, rows, LANES)], [((nt, KD), BF), ((KD, ns),...  10.9 us
    all_to_all x1, waiting for transfers between devices, shards(): lax.all_to_all(part, 'src', 0, 0, axis_index_groups=across, tiled=True)  10.7 us
    all_to_all x1, waiting for transfers between devices, shards(): lax.all_to_all(image, 'src', 0, 0, axis_index_groups=across, tiled=True)  6.4 us
    all_to_all x1, waiting for transfers between devices, shards(): part = lax.all_to_all(part, 'tgt', 0, 0, tiled=True)  6.26 us
    pallas_call x1, Pallas kernels, shards(): call(column_images, 'svvvv', [chunk, chunk], by_source + [((80, ns), BF),...  5.8 us
    all_to_all x1, starting transfers between devices, shards(): part = lax.all_to_all(part, 'tgt', 0, 0, tiled=True)  5.45 us
    all_to_all x1, starting transfers between devices, shards(): lax.all_to_all(part, 'src', 0, 0, axis_index_groups=across, tiled=True)  4.73 us
  transfers between devices with their start and end apart: 10, of which 8 were waited for; matrix products, arithmetic and copies ran while one was open for 0% of the time, Pallas kernels for 8%

profile of v2, /device:TPU:32, one launch (start us, length us, event | category | flops | bytes accessed | tf_op | source)
XLA Modules:
  0.0 113.1 jit_solution(3176268938785101933)
XLA Ops:
  0.6 0.0 copy-start
  0.6 1.0 copy-done
  1.7 0.0 copy-start.2
  1.7 0.9 copy-done.2
  2.6 0.0 copy-start.4
  2.6 0.7 copy-done.4
  3.3 0.0 copy-start.1
  3.3 0.0 copy-start.3
  3.3 10.9 %shard_map.66 = f32[8,8,128]{2,1,0:T(8,128)} custom-call(f32[32,1024]{1,0:T(8,128)S(1)} %copy-done.2, f32[32,4096]{1,0:T(8,128)S(1)} %copy-done, f32[1,4096]{1,0:T(1,128)S(1)} %bitcast.5), custom_call_target="tpu_custom_call" | custom-call | tf_op jit(solution)/shard_map/pallas_call | solution.py:286
  14.2 0.0 copy-start.5
  14.2 5.4 %all-to-all-start = ((f32[8,8,128]{2,1,0:T(8,128)}), f32[8,8,128]{2,1,0:T(8,128)S(1)}, u32[]{:S(2)}, u32[]{:S(2)}) async-start(f32[8,8,128]{2,1,0:T(8,128)} %shard_map.66), calls=%async_computation | async-start | bytes 65536 | tf_op jit(solution)/shard_map/all_to_all | solution.py:289
  19.6 6.3 %all-to-all-done.part_ref = f32[8,8,128]{2,1,0:T(8,128)S(1)} async-done(((f32[8,8,128]{2,1,0:T(8,128)}), f32[8,8,128]{2,1,0:T(8,128)S(1)}, u32[]{:S(2)}, u32[]{:S(2)}) %all-to-all-start) | async-done | bytes 32800 | tf_op jit(solution)/shard_map/all_to_all | solution.py:289
  25.9 0.0 copy-done.1
  25.9 0.0 copy-done.3
  25.9 0.0 copy-done.5
  25.9 3.8 %shard_map.67 = (f32[1,1024]{1,0:T(1,128)}, f32[1,1024]{1,0:T(1,128)S(1)}, f32[1,4096]{1,0:T(1,128)S(1)}, f32[16,32,128]{2,1,0:T(8,128)}) custom-call(f32[32,1024]{1,0:T(8,128)S(1)} %copy-done.3, f32[32,4096]{1,0:T(8,128)S(1)} %copy-done.1, f32[1,4096]{1,0:T(1,128)S(1)} %bitcast.6, f32[8,8,128]{2,1,0:T(8,128)S(1)} %all-to-all-done.part_ref), custom_call_target="tpu_custom_call" | custom-call | tf_op jit(solution)/shard_map/pallas_call | solution.py:291
  29.8 5.8 %shard_map.73 = (f32[16,40,128]{2,1,0:T(8,128)S(1)}, f32[16,40,128]{2,1,0:T(8,128)S(1)}) custom-call(s32[1]{0:T(128)} %bitcast.4.core_ref, f32[32,1024]{1,0:T(8,128)S(1)} %copy-done.3, f32[32,4096]{1,0:T(8,128)S(1)} %copy-done.1, f32[1,1024]{1,0:T(1,128)S(1)} %get-tuple-element.14.total_ref, f32[1,4096]{1,0:T(1,128)S(1)} %get-tuple-element.19.log_ref), custom_call_target="tpu_custom_call" | custom-call | tf_op jit(solution)/shard_map/pallas_call | solution.py:301
  35.6 0.1 collective-permute-start.5
  35.7 1.6 %collective-permute-done.5.two_ref = f32[16,40,128]{2,1,0:T(8,128)S(1)} collective-permute-done((f32[16,40,128]{2,1,0:T(8,128)S(1)}, f32[16,40,128]{2,1,0:T(8,128)S(1)}, u32[]{:S(2)}, u32[]{:S(2)}) %collective-permute-start.5) | collective-permute-done | bytes 327712 | tf_op jit(solution)/shard_map/ppermute | solution.py:304
  37.3 0.1 shard_map.74
  37.4 23.8 %all_to_all.20.part_ref = f32[16,40,128]{2,1,0:T(8,128)S(1)} all-to-all(f32[16,40,128]{2,1,0:T(8,128)S(1)} %shard_map.74), channel_id=1, replica_groups={{0,16,32,48,64,80,96,112,128,144,160,176,192,208,224,240},{8,24,40,56,7..., dimensions={0} | all-to-all | bytes 655360 | tf_op jit(solution)/shard_map/all_to_all | solution.py:305
  61.2 4.7 %all-to-all-start.1 = ((f32[16,32,128]{2,1,0:T(8,128)}), f32[16,32,128]{2,1,0:T(8,128)S(1)}, u32[]{:S(2)}, u32[]{:S(2)}) async-start(f32[16,32,128]{2,1,0:T(8,128)} %get-tuple-element.15), calls=%async_computation.1 | async-start | bytes 524288 | tf_op jit(solution)/shard_map/all_to_all | solution.py:297
  65.9 0.8 shard_map.75
  66.7 10.7 %all-to-all-done.1.part_ref = f32[16,32,128]{2,1,0:T(8,128)S(1)} async-done(((f32[16,32,128]{2,1,0:T(8,128)}), f32[16,32,128]{2,1,0:T(8,128)S(1)}, u32[]{:S(2)}, u32[]{:S(2)}) %all-to-all-start.1) | async-done | bytes 262176 | tf_op jit(solution)/shard_map/all_to_all | solution.py:297
  77.4 4.5 %all-to-all-start.3 = ((f32[16,32,128]{2,1,0:T(8,128)}), f32[16,32,128]{2,1,0:T(8,128)S(1)}, u32[]{:S(2)}, u32[]{:S(2)}) async-start(f32[16,32,128]{2,1,0:T(8,128)} %shard_map.75), calls=%async_computation.3 | async-start | bytes 524288 | tf_op jit(solution)/shard_map/all_to_all | solution.py:324
  82.0 0.1 shard_map.68.mine_ref
  82.0 0.1 collective-permute-start
  82.1 1.2 %collective-permute-done.other_ref = f32[32,128]{1,0:T(8,128)S(1)} collective-permute-done((f32[32,128]{1,0:T(8,128)S(1)}, f32[32,128]{1,0:T(8,128)S(1)}, u32[]{:S(2)}, u32[]{:S(2)}) %collective-permute-start) | collective-permute-done | bytes 16416 | tf_op jit(solution)/shard_map/ppermute | solution.py:299
  83.3 3.6 %shard_map.69 = (f32[1,4096]{1,0:T(1,128)}, f32[136,128]{1,0:T(8,128)S(1)}) custom-call(s32[1]{0:T(128)S(6)} %sub.8.side_ref, f32[32,1024]{1,0:T(8,128)S(1)} %copy-done.3, f32[32,4096]{1,0:T(8,128)S(1)} %copy-done.1, f32[1,1024]{1,0:T(1,128)S(1)} %get-tuple-element.14.total_ref, f32[32,128]{1,0:T(8,128)S(1)} %shard_map.68.mine_ref, ...), custom_call_target="tpu_custom_call" | custom-call | tf_op jit(solution)/shard_map/pallas_call | solution.py:315
  86.9 0.0 collective-permute-start.1
  86.9 6.4 %all-to-all-done.3.mine_ref = f32[16,32,128]{2,1,0:T(8,128)S(1)} async-done(((f32[16,32,128]{2,1,0:T(8,128)}), f32[16,32,128]{2,1,0:T(8,128)S(1)}, u32[]{:S(2)}, u32[]{:S(2)}) %all-to-all-start.3) | async-done | bytes 262176 | tf_op jit(solution)/shard_map/all_to_all | solution.py:324
  93.3 0.0 collective-permute-start.6
  93.3 3.6 %shard_map.70 = (f32[1,4096]{1,0:T(1,128)}, f32[136,128]{1,0:T(8,128)S(1)}) custom-call(s32[1]{0:T(128)} %bitcast.2.side_ref, f32[32,1024]{1,0:T(8,128)S(1)} %copy-done.3, f32[32,4096]{1,0:T(8,128)S(1)} %copy-done.1, f32[1,1024]{1,0:T(1,128)S(1)} %get-tuple-element.14.total_ref, f32[32,128]{1,0:T(8,128)S(1)} %shard_map.68.mine_ref, ...), custom_call_target="tpu_custom_call" | custom-call | tf_op jit(solution)/shard_map/pallas_call | solution.py:317
  96.9 0.0 collective-permute-done.1
  96.9 0.8 collective-permute-start.2
  97.7 3.9 %collective-permute-done.2 = f32[136,128]{1,0:T(8,128)S(1)} collective-permute-done((f32[136,128]{1,0:T(8,128)S(1)}, f32[136,128]{1,0:T(8,128)S(1)}, u32[]{:S(2)}, u32[]{:S(2)}) %collective-permute-start.2) | collective-permute-done | bytes 69664 | tf_op jit(solution)/shard_map/ppermute | solution.py:319
  101.6 1.3 %collective-permute-start.3 = (f32[136,128]{1,0:T(8,128)S(1)}, f32[136,128]{1,0:T(8,128)S(1)}, u32[]{:S(2)}, u32[]{:S(2)}) collective-permute-start(f32[136,128]{1,0:T(8,128)S(1)} %add.8.one_ref), channel_id=1, source_target_pairs={{0,3},{1,2},{2,1},{3,0},{4,7},{5,6},{6,5},{7,4},{8,11},{9,10},{10,... | collective-permute-start | bytes 208904 | tf_op jit(solution)/shard_map/ppermute | solution.py:320
  102.9 4.3 %collective-permute-done.3.two_ref = f32[136,128]{1,0:T(8,128)S(1)} collective-permute-done((f32[136,128]{1,0:T(8,128)S(1)}, f32[136,128]{1,0:T(8,128)S(1)}, u32[]{:S(2)}, u32[]{:S(2)}) %collective-permute-start.3) | collective-permute-done | bytes 69664 | tf_op jit(solution)/shard_map/ppermute | solution.py:320
  107.2 0.1 collective-permute-start.4
  107.3 4.3 %collective-permute-done.4.other_ref = f32[128,128]{1,0:T(8,128)S(1)} collective-permute-done((f32[128,128]{1,0:T(8,128)S(1)}, f32[128,128]{1,0:T(8,128)S(1)}, u32[]{:S(2)}, u32[]{:S(2)}) %collective-permute-start.4) | collective-permute-done | bytes 65568 | tf_op jit(solution)/shard_map/ppermute | solution.py:321
  111.6 0.7 shard_map.72
  112.3 0.0 collective-permute-done.6.other_ref
  112.3 0.8 shard_map.76
  (3 shorter events, 0.0 us)
Async XLA Ops:
  0.6 1.0 copy-start
  1.7 0.9 copy-start.2
  2.6 0.7 copy-start.4
  3.3 22.6 %copy-start.1 = (f32[32,4096]{1,0:T(8,128)S(1)}, f32[32,4096]{1,0:T(8,128)}, u32[]{:S(2)}) copy-start(f32[32,4096]{1,0:T(8,128)} %y_ref.9) | copy-start | bytes 1572868
  3.3 22.6 %copy-start.3 = (f32[32,1024]{1,0:T(8,128)S(1)}, f32[32,1024]{1,0:T(8,128)}, u32[]{:S(2)}) copy-start(f32[32,1024]{1,0:T(8,128)} %x_ref.9) | copy-start | bytes 393220
  14.2 11.7 %copy-start.5 = (f32[4096]{0:T(1024)S(1)}, f32[4096]{0:T(1024)}, u32[]{:S(2)}) copy-start(f32[4096]{0:T(1024)} %param.5) | copy-start | bytes 49156
  14.2 11.7 %all-to-all-start = ((f32[8,8,128]{2,1,0:T(8,128)}), f32[8,8,128]{2,1,0:T(8,128)S(1)}, u32[]{:S(2)}, u32[]{:S(2)}) async-start(f32[8,8,128]{2,1,0:T(8,128)} %shard_map.66), calls=%async_computation | async-start | bytes 65536 | tf_op jit(solution)/shard_map/all_to_all | solution.py:289
  35.6 1.7 %collective-permute-start.5 = (f32[16,40,128]{2,1,0:T(8,128)S(1)}, f32[16,40,128]{2,1,0:T(8,128)S(1)}, u32[]{:S(2)}, u32[]{:S(2)}) collective-permute-start(f32[16,40,128]{2,1,0:T(8,128)S(1)} %get-tuple-element.21), channel_id=1, source_target_pairs={{0,8},{8,0},{16,24},{24,16},{32,40},{40,32},{48,56},{56,48},{64,72... | collective-permute-start | bytes 983048 | tf_op jit(solution)/shard_map/ppermute | solution.py:304
  61.2 16.2 %all-to-all-start.1 = ((f32[16,32,128]{2,1,0:T(8,128)}), f32[16,32,128]{2,1,0:T(8,128)S(1)}, u32[]{:S(2)}, u32[]{:S(2)}) async-start(f32[16,32,128]{2,1,0:T(8,128)} %get-tuple-element.15), calls=%async_computation.1 | async-start | bytes 524288 | tf_op jit(solution)/shard_map/all_to_all | solution.py:297
  77.4 15.9 %all-to-all-start.3 = ((f32[16,32,128]{2,1,0:T(8,128)}), f32[16,32,128]{2,1,0:T(8,128)S(1)}, u32[]{:S(2)}, u32[]{:S(2)}) async-start(f32[16,32,128]{2,1,0:T(8,128)} %shard_map.75), calls=%async_computation.3 | async-start | bytes 524288 | tf_op jit(solution)/shard_map/all_to_all | solution.py:324
  82.0 1.3 %collective-permute-start = (f32[32,128]{1,0:T(8,128)S(1)}, f32[32,128]{1,0:T(8,128)S(1)}, u32[]{:S(2)}, u32[]{:S(2)}) collective-permute-start(f32[32,128]{1,0:T(8,128)S(1)} %shard_map.68.mine_ref), channel_id=1, source_target_pairs={{0,8},{8,0},{16,24},{24,16},{32,40},{40,32},{48,56},{56,48},{64,72... | collective-permute-start | bytes 49160 | tf_op jit(solution)/shard_map/ppermute | solution.py:299
  86.9 10.0 %collective-permute-start.1 = (f32[136,128]{1,0:T(8,128)S(1)}, f32[136,128]{1,0:T(8,128)S(1)}, u32[]{:S(2)}, u32[]{:S(2)}) collective-permute-start(f32[136,128]{1,0:T(8,128)S(1)} %get-tuple-element.18), channel_id=1, source_target_pairs={{0,4},{1,5},{2,6},{3,7},{4,0},{5,1},{6,2},{7,3},{8,12},{9,13},{10,... | collective-permute-start | bytes 208904 | tf_op jit(solution)/shard_map/ppermute | solution.py:316
  93.3 19.0 %collective-permute-start.6 = (f32[16,32,128]{2,1,0:T(8,128)S(1)}, f32[16,32,128]{2,1,0:T(8,128)S(1)}, u32[]{:S(2)}, u32[]{:S(2)}) collective-permute-start(f32[16,32,128]{2,1,0:T(8,128)S(1)} %all-to-all-done.3.mine_ref), channel_id=1, source_target_pairs={{0,8},{8,0},{16,24},{24,16},{32,40},{40,32},{48,56},{56,48},{64,72... | collective-permute-start | bytes 786440 | tf_op jit(solution)/shard_map/ppermute | solution.py:325
  96.9 4.7 %collective-permute-start.2 = (f32[136,128]{1,0:T(8,128)S(1)}, f32[136,128]{1,0:T(8,128)S(1)}, u32[]{:S(2)}, u32[]{:S(2)}) collective-permute-start(f32[136,128]{1,0:T(8,128)S(1)} %add.7), channel_id=1, source_target_pairs={{0,1},{1,0},{2,3},{3,2},{4,5},{5,4},{6,7},{7,6},{8,9},{9,8},{10,11... | collective-permute-start | bytes 208904 | tf_op jit(solution)/shard_map/ppermute | solution.py:319
  101.6 5.6 %collective-permute-start.3 = (f32[136,128]{1,0:T(8,128)S(1)}, f32[136,128]{1,0:T(8,128)S(1)}, u32[]{:S(2)}, u32[]{:S(2)}) collective-permute-start(f32[136,128]{1,0:T(8,128)S(1)} %add.8.one_ref), channel_id=1, source_target_pairs={{0,3},{1,2},{2,1},{3,0},{4,7},{5,6},{6,5},{7,4},{8,11},{9,10},{10,... | collective-permute-start | bytes 208904 | tf_op jit(solution)/shard_map/ppermute | solution.py:320
  107.2 4.4 %collective-permute-start.4 = (f32[128,128]{1,0:T(8,128)S(1)}, f32[128,128]{1,0:T(8,128)S(1)}, u32[]{:S(2)}, u32[]{:S(2)}) collective-permute-start(f32[128,128]{1,0:T(8,128)S(1)} %shard_map.71.mine_ref), channel_id=1, source_target_pairs={{0,4},{1,5},{2,6},{3,7},{4,0},{5,1},{6,2},{7,3},{8,12},{9,13},{10,... | collective-permute-start | bytes 196616 | tf_op jit(solution)/shard_map/ppermute | solution.py:321

commit v3 on v2

--- a/solution.py
+++ b/solution.py
@@ -127,7 +127,14 @@
     blocks(a_ref, b_ref, t_refs, 0, use)
 
 
-def row_logs(x_ref, y_ref, g_ref, out_ref, a_ref, b_ref, l_ref, *t_refs):
+def row_logs(x_hbm, y_hbm, g_hbm, out_ref, x_ref, y_ref, g_ref, a_ref, b_ref, l_ref, t0_ref, t1_ref, sems):
+    t_refs = (t0_ref, t1_ref)
+    sides = ((y_hbm, y_ref), (x_hbm, x_ref), (g_hbm, g_ref))
+    copies = [pltpu.make_async_copy(*pair, sems.at[i]) for i, pair in enumerate(sides)]
+    for copy in copies:
+        copy.start()
+    for copy in copies:
+        copy.wait()
     x, y = x_ref[...], y_ref[...]
     y_sq = jnp.sum(y * y, 0, keepdims=True)
     lift = (g_ref[...] - y_sq) * C2
@@ -184,17 +191,17 @@
     return top + jnp.log2(mass), image / mass
 
 
-def merge_pair(one_ref, two_ref, out_ref):
-    logs = [ref[:, K : K + 8, :][:, 0:1, :] for ref in (one_ref, two_ref)]
-    log, image = merge(logs, [one_ref[:, 0:K, :], two_ref[:, 0:K, :]])
+def merge_pair(one_ref, two_ref, after_ref, out_ref):
+    pair = (one_ref, two_ref)
+    log, image = merge([ref[:, K : K + 8, :][:, 0:1, :] for ref in pair], [ref[:, 0:K, :] for ref in pair])
     out_ref[:, 0:K, :] = image
     out_ref[:, K : K + 8, :] = jnp.broadcast_to(log, (out_ref.shape[0], 8, LANES))
 
 
-def merge_chunk(part_ref, out_ref):
+def merge_chunk(part_ref, after_ref, out_ref):
     n = part_ref.shape[0]
     _, image = merge([part_ref[d, K : K + 1, :] for d in range(n)], [part_ref[d, 0:K, :] for d in range(n)])
-    for d in range(n):
+    for d in range(out_ref.shape[0]):
         out_ref[d] = image
 
 
@@ -204,7 +211,7 @@
     out_ref[...] = top + jnp.log2(functools.reduce(jnp.add, [jnp.exp2(part_ref[d] - top) for d in range(n)]))
 
 
-def row_images(log_n, side_ref, x_ref, y_ref, total_ref, mine_ref, other_ref, pot_ref, out_ref, a_ref, b_ref, v_ref, o_ref, *t_refs):
+def row_images(log_n, side_ref, x_ref, y_ref, total_ref, mine_ref, other_ref, after_ref, pot_ref, out_ref, a_ref, b_ref, v_ref, o_ref, *t_refs):
     mine, other = mine_ref[...], other_ref[...]
     top = jnp.maximum(mine, other)
     logs = top + jnp.log2(jnp.exp2(mine - top) + jnp.exp2(other - top))
@@ -247,6 +254,10 @@
                 out_ref[r : r + 8, cols] = ref[r * tiles + 8 * k : r * tiles + 8 * k + 8, :]
 
 
+def hold(image_ref, after_ref, out_ref):
+    pass
+
+
 def lay_columns(core_ref, mine_ref, other_ref, out_ref):
     half = out_ref.shape[1] // 2
     for side, ref in ((core_ref[0], mine_ref), (1 - core_ref[0], other_ref)):
@@ -254,15 +265,21 @@
             out_ref[:, pl.ds(pl.multiple_of(side * half + q * LANES, LANES), LANES)] = ref[q]
 
 
-def call(kernel, ins, outs, scratch=()):
+def call(kernel, ins, outs, scratch=(), copies=0, aliases={}, cost=None):
     return pl.pallas_call(
         kernel,
         out_shape=tuple(jax.ShapeDtypeStruct(shape, F32) for shape in outs),
-        in_specs=[SM if spec == "s" else VM for spec in ins],
+        in_specs=[{"s": SM, "h": pl.BlockSpec(memory_space=pltpu.HBM), "v": VM}[spec] for spec in ins],
         out_specs=tuple(VM for _ in outs),
-        scratch_shapes=[pltpu.VMEM(shape, dtype) for shape, dtype in scratch],
+        scratch_shapes=[pltpu.VMEM(*one) for one in scratch] + [pltpu.SemaphoreType.DMA((copies,))] * (copies > 0),
+        input_output_aliases=aliases,
+        cost_estimate=cost,
         compiler_params=pltpu.CompilerParams(vmem_limit_bytes=50 << 20),
     )
+
+
+def work(pairs, sums):
+    return pl.CostEstimate(flops=2 * pairs * (KD + 256 * sums), transcendentals=pairs, bytes_accessed=8 * pairs)
 
 
 def solution(mesh):
@@ -283,9 +300,14 @@
         by_source = [((ns, KD), BF), ((KD, nt), BF)]
         chunk = (pairs, K + 8, LANES)
 
-        (part,) = call(
-            row_logs, "vvv", [(n_tgt, rows, LANES)], [((nt, KD), BF), ((KD, ns), BF), ((1, ns), F32), BLOCK, BLOCK]
-        )(x, y, g)
+        part, x, y, g = call(
+            row_logs,
+            "hhh",
+            [(n_tgt, rows, LANES), x.shape, y.shape, g.shape],
+            [((nt, KD), BF), ((KD, ns), BF), ((1, ns), F32), BLOCK, BLOCK],
+            3,
+            cost=work(ns * nt, 0),
+        )(*(pltpu.with_memory_space_constraint(one, pltpu.HBM) for one in (x, y, g)))
         part = lax.all_to_all(part, "tgt", 0, 0, tiled=True)
 
         source_potential, total, logs, part = call(
@@ -293,35 +315,41 @@
             "vvvv",
             [(1, ns), (1, ns), (1, nt), (pairs, cols, LANES)],
             by_source + [((1, nt), F32), BLOCK, BLOCK],
+            cost=work(ns * nt, 0),
         )(x, y, g, part)
         part = lax.all_to_all(part, "src", 0, 0, axis_index_groups=across, tiled=True)
         (mine,) = call(merge_logs, "v", [(cols, LANES)])(part)
         other = lax.ppermute(mine, "src", swap)
 
         keep, send = call(
-            column_images, "svvvv", [chunk, chunk], by_source + [((80, ns), BF), ((80, nt), F32), BLOCK, BLOCK]
+            column_images,
+            "svvvv",
+            [chunk, chunk],
+            by_source + [((80, ns), BF), ((80, nt), F32), BLOCK, BLOCK],
+            cost=work(ns * nt, 2),
         )(core, x, y, total, logs)
-        (image,) = call(merge_pair, "vv", [chunk])(keep, lax.ppermute(send, "src", swap))
+        (image,) = call(merge_pair, "vvv", [chunk])(keep, lax.ppermute(send, "src", swap), mine)
         image = lax.all_to_all(image, "src", 0, 0, axis_index_groups=across, tiled=True)
 
         half = ns // 2
         tall = (K * half) // LANES
         images = call(
             functools.partial(row_images, math.log2(nt * n_tgt)),
-            "svvvvv",
+            "svvvvvv",
             [(1, nt), (tall + 8, LANES)],
             [((nt, KD), BF), ((KD, half), BF), ((80, nt), BF), ((80, half), F32), BLOCK, BLOCK],
+            cost=work(half * nt, 2),
         )
-        target_potential, sent = images(1 - side, x, y, total, mine, other)
+        target_potential, sent = images(1 - side, x, y, total, mine, other, mine)
+        _, held = images(side, x, y, total, mine, other, sent)
         sent = lax.ppermute(sent, "tgt", over)
-        _, held = images(side, x, y, total, mine, other)
         held = held + sent
+        (image,) = call(merge_chunk, "vv", [(pairs, K, LANES)], cost=work(half * nt, 2))(image, held)
+        image = lax.all_to_all(image, "src", 0, 0, axis_index_groups=across, tiled=True)
         held = held + lax.ppermute(held, "tgt", near)
         (held,) = call(add_divide, "vv", [(tall, LANES)])(held, lax.ppermute(held, "tgt", far))
         (source_image,) = call(lay_rows, "svv", [(K, ns)])(side, held, lax.ppermute(held, "tgt", over))
-
-        (image,) = call(merge_chunk, "v", [(pairs, K, LANES)])(image)
-        image = lax.all_to_all(image, "src", 0, 0, axis_index_groups=across, tiled=True)
+        (image,) = call(hold, "vv", [image.shape], aliases={0: 0})(image, source_image)
         (target_image,) = call(lay_columns, "svv", [(K, nt)])(core, image, lax.ppermute(image, "src", swap))
         return source_potential.reshape(ns), target_potential.reshape(nt), source_image, target_image
 

time: 114 us -> 95.4 us (0.84)
  blocking collectives: 23.8 us -> 0 us
  starting transfers between devices: 17.1 us -> 30.3 us
  waiting for transfers between devices: 38.6 us -> 30 us
  local copies, waits for them, and re-layouts: 2.67 us -> 0.9 us
  Pallas kernels: 30.2 us -> 31.8 us
    all_to_all x1 -> x0, blocking collectives: 23.8 us -> none  [shards(): lax.all_to_all(image, 'src', 0, 0, axis_index_groups=across, tiled=True)]
    all_to_all x1 -> x2, starting transfers between devices: 4.54 us -> 11.4 us  [shards(): lax.all_to_all(image, 'src', 0, 0, axis_index_groups=across, tiled=True)]
    all_to_all x1, waiting for transfers between devices: 10.7 us -> 4.49 us  [shards(): lax.all_to_all(part, 'src', 0, 0, axis_index_groups=across, tiled=True)]
    all_to_all x1, starting transfers between devices: 4.73 us -> 10.9 us  [shards(): lax.all_to_all(part, 'src', 0, 0, axis_index_groups=across, tiled=True)]
    pallas_call x5 -> x6, Pallas kernels: 18.9 us -> 20.8 us  [the longest x1 12 us: shards(): call(row_logs, 'hhh', [(n_tgt, rows, LANES), x.shape, y.shape, g.shape],...]
    unnamed x12 -> x2, local copies, waits for them, and re-layouts: 2.67 us -> 0.9 us
    ppermute x1, waiting for transfers between devices: 1.62 us -> 0.01 us  [shards(): lax.ppermute(send, 'src', swap)]
    ppermute x1, waiting for transfers between devices: 0.01 us -> 1.53 us  [shards(): lax.ppermute(image, 'src', swap)]
  transfers between devices with their start and end apart: 10 -> 11, of which waited for: 8 -> 8; matrix products, arithmetic and copies ran while one was open for 0% -> 0% of each run, Pallas kernels for 8% -> 16%
where the time goes in v3:
time: 95.4 us; the launch traced here: 93.7 us
  Pallas kernels  31.8 us (33%)
  starting transfers between devices  30.3 us (32%)
  waiting for transfers between devices  30 us (31%)
    pallas_call x1, Pallas kernels, shards(): call(row_logs, 'hhh', [(n_tgt, rows, LANES), x.shape, y.shape, g.shape],...  12 us
    all_to_all x2, starting transfers between devices, shards(): lax.all_to_all(image, 'src', 0, 0, axis_index_groups=across, tiled=True)  11.4 us
    all_to_all x1, starting transfers between devices, shards(): lax.all_to_all(part, 'src', 0, 0, axis_index_groups=across, tiled=True)  10.9 us
    all_to_all x1, waiting for transfers between devices, shards(): part = lax.all_to_all(part, 'tgt', 0, 0, tiled=True)  6.26 us
    pallas_call x1, Pallas kernels, shards(): call(column_images, 'svvvv', [chunk, chunk], by_source + [((80, ns), BF),...  5.8 us
    all_to_all x1, starting transfers between devices, shards(): part = lax.all_to_all(part, 'tgt', 0, 0, tiled=True)  5.31 us
    all_to_all x2, waiting for transfers between devices, shards(): lax.all_to_all(image, 'src', 0, 0, axis_index_groups=across, tiled=True)  5.14 us
    all_to_all x1, waiting for transfers between devices, shards(): lax.all_to_all(part, 'src', 0, 0, axis_index_groups=across, tiled=True)  4.49 us
  transfers between devices with their start and end apart: 11, of which 8 were waited for; matrix products, arithmetic and copies ran while one was open for 0% of the time, Pallas kernels for 16%

profile of v3, /device:TPU:32, one launch (start us, length us, event | category | flops | bytes accessed | tf_op | source)
XLA Modules:
  0.0 93.7 jit_solution(18354724981124107985)
XLA Ops:
  0.6 12.0 %shard_map.66 = (f32[8,8,128]{2,1,0:T(8,128)}, f32[32,1024]{1,0:T(8,128)S(1)}, f32[32,4096]{1,0:T(8,128)S(1)}, f32[1,4096]{1,0:T(1,128)S(1)}) custom-call(f32[32,1024]{1,0:T(8,128)} %x_hbm.1, f32[32,4096]{1,0:T(8,128)} %y_hbm.1, f32[1,4096]{1,0:T(1,128)} %bitcast.5), custom_call_target="tpu_custom_call" | custom-call | flops 2147483648 | bytes 33554432 | tf_op jit(solution)/shard_map/pallas_call | solution.py:303
  12.6 5.3 %all-to-all-start = ((f32[8,8,128]{2,1,0:T(8,128)}), f32[8,8,128]{2,1,0:T(8,128)S(1)}, u32[]{:S(2)}, u32[]{:S(2)}) async-start(f32[8,8,128]{2,1,0:T(8,128)} %get-tuple-element.20), calls=%async_computation | async-start | bytes 65536 | tf_op jit(solution)/shard_map/all_to_all | solution.py:311
  17.9 6.3 %all-to-all-done.part_ref = f32[8,8,128]{2,1,0:T(8,128)S(1)} async-done(((f32[8,8,128]{2,1,0:T(8,128)}), f32[8,8,128]{2,1,0:T(8,128)S(1)}, u32[]{:S(2)}, u32[]{:S(2)}) %all-to-all-start) | async-done | bytes 32800 | tf_op jit(solution)/shard_map/all_to_all | solution.py:311
  24.2 3.7 %shard_map.67 = (f32[1,1024]{1,0:T(1,128)}, f32[1,1024]{1,0:T(1,128)S(1)}, f32[1,4096]{1,0:T(1,128)S(1)}, f32[16,32,128]{2,1,0:T(8,128)}) custom-call(f32[32,1024]{1,0:T(8,128)S(1)} %get-tuple-element.17.x_ref, f32[32,4096]{1,0:T(8,128)S(1)} %get-tuple-element.18.y_ref, f32[1,4096]{1,0:T(1,128)S(1)} %get-tuple-element.19.g_ref, ...), custom_call_target="tpu_custom_call" | custom-call | flops 2147483648 | bytes 33554432 | tf_op jit(solution)/shard_map/pallas_call | solution.py:313
  27.9 10.9 %all-to-all-start.1 = ((f32[16,32,128]{2,1,0:T(8,128)}), f32[16,32,128]{2,1,0:T(8,128)S(1)}, u32[]{:S(2)}, u32[]{:S(2)}) async-start(f32[16,32,128]{2,1,0:T(8,128)} %get-tuple-element.23), calls=%async_computation.1 | async-start | bytes 524288 | tf_op jit(solution)/shard_map/all_to_all | solution.py:320
  38.8 5.8 %shard_map.73 = (f32[16,40,128]{2,1,0:T(8,128)S(1)}, f32[16,40,128]{2,1,0:T(8,128)S(1)}) custom-call(s32[1]{0:T(128)} %bitcast.4.core_ref, f32[32,1024]{1,0:T(8,128)S(1)} %get-tuple-element.17.x_ref, f32[32,4096]{1,0:T(8,128)S(1)} %get-tuple-element.18.y_ref, f32[1,1024]{1,0:T(1,128)S(1)} %get-tuple-element.22.total_ref, f32[1,4096]{1,0:T(1,128)S(1)} %get-tuple-element.27.log_ref), custom_call_target="tpu_custom_call" | custom-call | flops 6442450944 | bytes 33554432 | tf_op jit(solution)/shard_map/pallas_call | solution.py:324
  44.6 0.1 collective-permute-start.5
  44.7 4.5 %all-to-all-done.1.part_ref = f32[16,32,128]{2,1,0:T(8,128)S(1)} async-done(((f32[16,32,128]{2,1,0:T(8,128)}), f32[16,32,128]{2,1,0:T(8,128)S(1)}, u32[]{:S(2)}, u32[]{:S(2)}) %all-to-all-start.1) | async-done | bytes 262176 | tf_op jit(solution)/shard_map/all_to_all | solution.py:320
  49.2 0.1 shard_map.68.mine_ref.after_ref
  49.3 0.1 collective-permute-start
  49.4 0.0 collective-permute-done.5.two_ref
  49.4 0.8 shard_map.74
  50.2 6.6 %all-to-all-start.2 = ((f32[16,40,128]{2,1,0:T(8,128)}), f32[16,40,128]{2,1,0:T(8,128)S(1)}, u32[]{:S(2)}, u32[]{:S(2)}) async-start(f32[16,40,128]{2,1,0:T(8,128)} %shard_map.74), calls=%async_computation.2 | async-start | bytes 655360 | tf_op jit(solution)/shard_map/all_to_all | solution.py:332
  56.7 0.0 collective-permute-done.other_ref
  56.8 3.6 %shard_map.69 = (f32[1,4096]{1,0:T(1,128)}, f32[136,128]{1,0:T(8,128)S(1)}) custom-call(s32[1]{0:T(128)S(6)} %sub.8.side_ref, f32[32,1024]{1,0:T(8,128)S(1)} %get-tuple-element.17.x_ref, f32[32,4096]{1,0:T(8,128)S(1)} %get-tuple-element.18.y_ref, f32[1,1024]{1,0:T(1,128)S(1)} %get-tuple-element.22.total_ref, f32[32,128]{1,0:T(8,128)S(1)} %shard_map.68.mine_ref.after_ref, ...), custom_call_target="tpu_custom_call" | custom-call | flops 3221225472 | bytes 16777216 | tf_op jit(solution)/shard_map/pallas_call | solution.py:343
  60.4 0.0 collective-permute-start.1
  60.4 3.6 %shard_map.70 = (f32[1,4096]{1,0:T(1,128)}, f32[136,128]{1,0:T(8,128)S(1)}) custom-call(s32[1]{0:T(128)} %bitcast.2.side_ref, f32[32,1024]{1,0:T(8,128)S(1)} %get-tuple-element.17.x_ref, f32[32,4096]{1,0:T(8,128)S(1)} %get-tuple-element.18.y_ref, f32[1,1024]{1,0:T(1,128)S(1)} %get-tuple-element.22.total_ref, f32[32,128]{1,0:T(8,128)S(1)} %shard_map.68.mine_ref.after_ref, ...), custom_call_target="tpu_custom_call" | custom-call | flops 3221225472 | bytes 16777216 | tf_op jit(solution)/shard_map/pallas_call | solution.py:344
  64.0 0.7 collective-permute-done.1
  64.7 5.1 %all-to-all-done.2.part_ref = f32[16,40,128]{2,1,0:T(8,128)S(1)} async-done(((f32[16,40,128]{2,1,0:T(8,128)}), f32[16,40,128]{2,1,0:T(8,128)S(1)}, u32[]{:S(2)}, u32[]{:S(2)}) %all-to-all-start.2) | async-done | bytes 327712 | tf_op jit(solution)/shard_map/all_to_all | solution.py:332
  69.9 0.8 shard_map.75
  70.6 4.9 %all-to-all-start.3 = ((f32[16,32,128]{2,1,0:T(8,128)}), f32[16,32,128]{2,1,0:T(8,128)S(1)}, u32[]{:S(2)}, u32[]{:S(2)}) async-start(f32[16,32,128]{2,1,0:T(8,128)} %shard_map.75), calls=%async_computation.3 | async-start | bytes 524288 | tf_op jit(solution)/shard_map/all_to_all | solution.py:348
  75.5 0.6 collective-permute-start.2
  76.1 3.7 %collective-permute-done.2 = f32[136,128]{1,0:T(8,128)S(1)} collective-permute-done((f32[136,128]{1,0:T(8,128)S(1)}, f32[136,128]{1,0:T(8,128)S(1)}, u32[]{:S(2)}, u32[]{:S(2)}) %collective-permute-start.2) | collective-permute-done | bytes 69664 | tf_op jit(solution)/shard_map/ppermute | solution.py:349
  79.8 1.3 %collective-permute-start.3 = (f32[136,128]{1,0:T(8,128)S(1)}, f32[136,128]{1,0:T(8,128)S(1)}, u32[]{:S(2)}, u32[]{:S(2)}) collective-permute-start(f32[136,128]{1,0:T(8,128)S(1)} %add.8.one_ref), channel_id=1, source_target_pairs={{0,3},{1,2},{2,1},{3,0},{4,7},{5,6},{6,5},{7,4},{8,11},{9,10},{10,... | collective-permute-start | bytes 208904 | tf_op jit(solution)/shard_map/ppermute | solution.py:350
  81.1 4.3 %collective-permute-done.3.two_ref = f32[136,128]{1,0:T(8,128)S(1)} collective-permute-done((f32[136,128]{1,0:T(8,128)S(1)}, f32[136,128]{1,0:T(8,128)S(1)}, u32[]{:S(2)}, u32[]{:S(2)}) %collective-permute-start.3) | collective-permute-done | bytes 69664 | tf_op jit(solution)/shard_map/ppermute | solution.py:350
  85.4 0.5 collective-permute-start.4
  85.9 3.9 %collective-permute-done.4.other_ref = f32[128,128]{1,0:T(8,128)S(1)} collective-permute-done((f32[128,128]{1,0:T(8,128)S(1)}, f32[128,128]{1,0:T(8,128)S(1)}, u32[]{:S(2)}, u32[]{:S(2)}) %collective-permute-start.4) | collective-permute-done | bytes 65568 | tf_op jit(solution)/shard_map/ppermute | solution.py:351
  89.8 0.7 shard_map.72.after_ref
  90.5 0.0 all-to-all-done.3.image_ref
  90.5 0.0 copy-start
  90.5 0.9 copy-done
  91.4 0.0 collective-permute-start.6
  91.4 1.5 %collective-permute-done.6.other_ref = f32[16,32,128]{2,1,0:T(8,128)S(1)} collective-permute-done((f32[16,32,128]{2,1,0:T(8,128)S(1)}, f32[16,32,128]{2,1,0:T(8,128)S(1)}, u32[]{:S(2)}, u32[]{:S(2)}) %collective-permute-start.6) | collective-permute-done | bytes 262176 | tf_op jit(solution)/shard_map/ppermute | solution.py:353
  92.9 0.8 shard_map.77
  (4 shorter events, 0.0 us)
Async XLA Ops:
  12.6 11.6 %all-to-all-start = ((f32[8,8,128]{2,1,0:T(8,128)}), f32[8,8,128]{2,1,0:T(8,128)S(1)}, u32[]{:S(2)}, u32[]{:S(2)}) async-start(f32[8,8,128]{2,1,0:T(8,128)} %get-tuple-element.20), calls=%async_computation | async-start | bytes 65536 | tf_op jit(solution)/shard_map/all_to_all | solution.py:311
  27.9 21.3 %all-to-all-start.1 = ((f32[16,32,128]{2,1,0:T(8,128)}), f32[16,32,128]{2,1,0:T(8,128)S(1)}, u32[]{:S(2)}, u32[]{:S(2)}) async-start(f32[16,32,128]{2,1,0:T(8,128)} %get-tuple-element.23), calls=%async_computation.1 | async-start | bytes 524288 | tf_op jit(solution)/shard_map/all_to_all | solution.py:320
  44.6 4.8 %collective-permute-start.5 = (f32[16,40,128]{2,1,0:T(8,128)S(1)}, f32[16,40,128]{2,1,0:T(8,128)S(1)}, u32[]{:S(2)}, u32[]{:S(2)}) collective-permute-start(f32[16,40,128]{2,1,0:T(8,128)S(1)} %get-tuple-element.29), channel_id=1, source_target_pairs={{0,8},{8,0},{16,24},{24,16},{32,40},{40,32},{48,56},{56,48},{64,72... | collective-permute-start | bytes 983048 | tf_op jit(solution)/shard_map/ppermute | solution.py:331
  49.3 7.5 %collective-permute-start = (f32[32,128]{1,0:T(8,128)S(1)}, f32[32,128]{1,0:T(8,128)S(1)}, u32[]{:S(2)}, u32[]{:S(2)}) collective-permute-start(f32[32,128]{1,0:T(8,128)S(1)} %shard_map.68.mine_ref.after_ref), channel_id=1, source_target_pairs={{0,8},{8,0},{16,24},{24,16},{32,40},{40,32},{48,56},{56,48},{64,72... | collective-permute-start | bytes 49160 | tf_op jit(solution)/shard_map/ppermute | solution.py:322
  50.2 19.7 %all-to-all-start.2 = ((f32[16,40,128]{2,1,0:T(8,128)}), f32[16,40,128]{2,1,0:T(8,128)S(1)}, u32[]{:S(2)}, u32[]{:S(2)}) async-start(f32[16,40,128]{2,1,0:T(8,128)} %shard_map.74), calls=%async_computation.2 | async-start | bytes 655360 | tf_op jit(solution)/shard_map/all_to_all | solution.py:332
  60.4 4.4 %collective-permute-start.1 = (f32[136,128]{1,0:T(8,128)S(1)}, f32[136,128]{1,0:T(8,128)S(1)}, u32[]{:S(2)}, u32[]{:S(2)}) collective-permute-start(f32[136,128]{1,0:T(8,128)S(1)} %get-tuple-element.25.after_ref), channel_id=1, source_target_pairs={{0,4},{1,5},{2,6},{3,7},{4,0},{5,1},{6,2},{7,3},{8,12},{9,13},{10,... | collective-permute-start | bytes 208904 | tf_op jit(solution)/shard_map/ppermute | solution.py:345
  70.6 19.8 %all-to-all-start.3 = ((f32[16,32,128]{2,1,0:T(8,128)}), f32[16,32,128]{2,1,0:T(8,128)S(1)}, u32[]{:S(2)}, u32[]{:S(2)}) async-start(f32[16,32,128]{2,1,0:T(8,128)} %shard_map.75), calls=%async_computation.3 | async-start | bytes 524288 | tf_op jit(solution)/shard_map/all_to_all | solution.py:348
  75.5 4.3 %collective-permute-start.2 = (f32[136,128]{1,0:T(8,128)S(1)}, f32[136,128]{1,0:T(8,128)S(1)}, u32[]{:S(2)}, u32[]{:S(2)}) collective-permute-start(f32[136,128]{1,0:T(8,128)S(1)} %add.7.after_ref), channel_id=1, source_target_pairs={{0,1},{1,0},{2,3},{3,2},{4,5},{5,4},{6,7},{7,6},{8,9},{9,8},{10,11... | collective-permute-start | bytes 208904 | tf_op jit(solution)/shard_map/ppermute | solution.py:349
  79.8 5.6 %collective-permute-start.3 = (f32[136,128]{1,0:T(8,128)S(1)}, f32[136,128]{1,0:T(8,128)S(1)}, u32[]{:S(2)}, u32[]{:S(2)}) collective-permute-start(f32[136,128]{1,0:T(8,128)S(1)} %add.8.one_ref), channel_id=1, source_target_pairs={{0,3},{1,2},{2,1},{3,0},{4,7},{5,6},{6,5},{7,4},{8,11},{9,10},{10,... | collective-permute-start | bytes 208904 | tf_op jit(solution)/shard_map/ppermute | solution.py:350
  85.4 4.4 %collective-permute-start.4 = (f32[128,128]{1,0:T(8,128)S(1)}, f32[128,128]{1,0:T(8,128)S(1)}, u32[]{:S(2)}, u32[]{:S(2)}) collective-permute-start(f32[128,128]{1,0:T(8,128)S(1)} %shard_map.71.mine_ref), channel_id=1, source_target_pairs={{0,4},{1,5},{2,6},{3,7},{4,0},{5,1},{6,2},{7,3},{8,12},{9,13},{10,... | collective-permute-start | bytes 196616 | tf_op jit(solution)/shard_map/ppermute | solution.py:351
  90.5 0.9 copy-start
  91.4 1.5 %collective-permute-start.6 = (f32[16,32,128]{2,1,0:T(8,128)S(1)}, f32[16,32,128]{2,1,0:T(8,128)S(1)}, u32[]{:S(2)}, u32[]{:S(2)}) collective-permute-start(f32[16,32,128]{2,1,0:T(8,128)S(1)} %shard_map.76.mine_ref), channel_id=1, source_target_pairs={{0,8},{8,0},{16,24},{24,16},{32,40},{40,32},{48,56},{56,48},{64,72... | collective-permute-start | bytes 786440 | tf_op jit(solution)/shard_map/ppermute | solution.py:353

commit v4 on v3

--- a/solution.py
+++ b/solution.py
@@ -347,9 +347,10 @@
         (image,) = call(merge_chunk, "vv", [(pairs, K, LANES)], cost=work(half * nt, 2))(image, held)
         image = lax.all_to_all(image, "src", 0, 0, axis_index_groups=across, tiled=True)
         held = held + lax.ppermute(held, "tgt", near)
-        (held,) = call(add_divide, "vv", [(tall, LANES)])(held, lax.ppermute(held, "tgt", far))
-        (source_image,) = call(lay_rows, "svv", [(K, ns)])(side, held, lax.ppermute(held, "tgt", over))
-        (image,) = call(hold, "vv", [image.shape], aliases={0: 0})(image, source_image)
+        (held,) = call(add_divide, "vv", [(tall, LANES)], cost=work(half * nt, 2))(held, lax.ppermute(held, "tgt", far))
+        sent = lax.ppermute(held, "tgt", over)
+        (source_image,) = call(lay_rows, "svv", [(K, ns)], cost=work(half * nt, 2))(side, held, sent)
+        (image,) = call(hold, "vv", [image.shape], aliases={0: 0})(image, sent)
         (target_image,) = call(lay_columns, "svv", [(K, nt)])(core, image, lax.ppermute(image, "src", swap))
         return source_potential.reshape(ns), target_potential.reshape(nt), source_image, target_image
 

time: 95.4 us -> 91.3 us (0.957)
  waiting for transfers between devices: 30 us -> 26.5 us
    ppermute x1, waiting for transfers between devices: 3.66 us -> 0.01 us  [shards(): held = held + lax.ppermute(held, 'tgt', near)]
  transfers between devices with their start and end apart: 11 -> 11, of which waited for: 8 -> 8; matrix products, arithmetic and copies ran while one was open for 0% -> 0% of each run, Pallas kernels for 16% -> 17%
where the time goes in v4:
time: 91.3 us; the launch traced here: 90 us
  Pallas kernels  31.8 us (35%)
  starting transfers between devices  31 us (34%)
  waiting for transfers between devices  26.5 us (29%)
    all_to_all x2, starting transfers between devices, shards(): lax.all_to_all(image, 'src', 0, 0, axis_index_groups=across, tiled=True)  12.2 us
    pallas_call x1, Pallas kernels, shards(): call(row_logs, 'hhh', [(n_tgt, rows, LANES), x.shape, y.shape, g.shape],...  12 us
    all_to_all x1, starting transfers between devices, shards(): lax.all_to_all(part, 'src', 0, 0, axis_index_groups=across, tiled=True)  10.9 us
    all_to_all x1, waiting for transfers between devices, shards(): part = lax.all_to_all(part, 'tgt', 0, 0, tiled=True)  6.26 us
    all_to_all x2, waiting for transfers between devices, shards(): lax.all_to_all(image, 'src', 0, 0, axis_index_groups=across, tiled=True)  5.82 us
    pallas_call x1, Pallas kernels, shards(): call(column_images, 'svvvv', [chunk, chunk], by_source + [((80, ns), BF),...  5.8 us
    all_to_all x1, starting transfers between devices, shards(): part = lax.all_to_all(part, 'tgt', 0, 0, tiled=True)  5.31 us
    all_to_all x1, waiting for transfers between devices, shards(): lax.all_to_all(part, 'src', 0, 0, axis_index_groups=across, tiled=True)  4.49 us
  transfers between devices with their start and end apart: 11, of which 8 were waited for; matrix products, arithmetic and copies ran while one was open for 0% of the time, Pallas kernels for 17%

profile of v4, /device:TPU:32, one launch (start us, length us, event | category | flops | bytes accessed | tf_op | source)
XLA Modules:
  0.0 90.0 jit_solution(10735571488763979593)
XLA Ops:
  0.6 12.0 %shard_map.66 = (f32[8,8,128]{2,1,0:T(8,128)}, f32[32,1024]{1,0:T(8,128)S(1)}, f32[32,4096]{1,0:T(8,128)S(1)}, f32[1,4096]{1,0:T(1,128)S(1)}) custom-call(f32[32,1024]{1,0:T(8,128)} %x_hbm.1, f32[32,4096]{1,0:T(8,128)} %y_hbm.1, f32[1,4096]{1,0:T(1,128)} %bitcast.5), custom_call_target="tpu_custom_call" | custom-call | flops 2147483648 | bytes 33554432 | tf_op jit(solution)/shard_map/pallas_call | solution.py:303
  12.6 5.3 %all-to-all-start = ((f32[8,8,128]{2,1,0:T(8,128)}), f32[8,8,128]{2,1,0:T(8,128)S(1)}, u32[]{:S(2)}, u32[]{:S(2)}) async-start(f32[8,8,128]{2,1,0:T(8,128)} %get-tuple-element.20), calls=%async_computation | async-start | bytes 65536 | tf_op jit(solution)/shard_map/all_to_all | solution.py:311
  17.9 6.3 %all-to-all-done.part_ref = f32[8,8,128]{2,1,0:T(8,128)S(1)} async-done(((f32[8,8,128]{2,1,0:T(8,128)}), f32[8,8,128]{2,1,0:T(8,128)S(1)}, u32[]{:S(2)}, u32[]{:S(2)}) %all-to-all-start) | async-done | bytes 32800 | tf_op jit(solution)/shard_map/all_to_all | solution.py:311
  24.2 3.7 %shard_map.67 = (f32[1,1024]{1,0:T(1,128)}, f32[1,1024]{1,0:T(1,128)S(1)}, f32[1,4096]{1,0:T(1,128)S(1)}, f32[16,32,128]{2,1,0:T(8,128)}) custom-call(f32[32,1024]{1,0:T(8,128)S(1)} %get-tuple-element.17.x_ref, f32[32,4096]{1,0:T(8,128)S(1)} %get-tuple-element.18.y_ref, f32[1,4096]{1,0:T(1,128)S(1)} %get-tuple-element.19.g_ref, ...), custom_call_target="tpu_custom_call" | custom-call | flops 2147483648 | bytes 33554432 | tf_op jit(solution)/shard_map/pallas_call | solution.py:313
  27.9 10.9 %all-to-all-start.1 = ((f32[16,32,128]{2,1,0:T(8,128)}), f32[16,32,128]{2,1,0:T(8,128)S(1)}, u32[]{:S(2)}, u32[]{:S(2)}) async-start(f32[16,32,128]{2,1,0:T(8,128)} %get-tuple-element.23), calls=%async_computation.1 | async-start | bytes 524288 | tf_op jit(solution)/shard_map/all_to_all | solution.py:320
  38.8 5.8 %shard_map.73 = (f32[16,40,128]{2,1,0:T(8,128)S(1)}, f32[16,40,128]{2,1,0:T(8,128)S(1)}) custom-call(s32[1]{0:T(128)} %bitcast.4.core_ref, f32[32,1024]{1,0:T(8,128)S(1)} %get-tuple-element.17.x_ref, f32[32,4096]{1,0:T(8,128)S(1)} %get-tuple-element.18.y_ref, f32[1,1024]{1,0:T(1,128)S(1)} %get-tuple-element.22.total_ref, f32[1,4096]{1,0:T(1,128)S(1)} %get-tuple-element.27.log_ref), custom_call_target="tpu_custom_call" | custom-call | flops 6442450944 | bytes 33554432 | tf_op jit(solution)/shard_map/pallas_call | solution.py:324
  44.6 0.1 collective-permute-start.5
  44.7 4.5 %all-to-all-done.1.part_ref = f32[16,32,128]{2,1,0:T(8,128)S(1)} async-done(((f32[16,32,128]{2,1,0:T(8,128)}), f32[16,32,128]{2,1,0:T(8,128)S(1)}, u32[]{:S(2)}, u32[]{:S(2)}) %all-to-all-start.1) | async-done | bytes 262176 | tf_op jit(solution)/shard_map/all_to_all | solution.py:320
  49.2 0.1 shard_map.68.mine_ref.after_ref
  49.3 0.1 collective-permute-start
  49.4 0.0 collective-permute-done.5.two_ref
  49.4 0.8 shard_map.74
  50.2 6.6 %all-to-all-start.2 = ((f32[16,40,128]{2,1,0:T(8,128)}), f32[16,40,128]{2,1,0:T(8,128)S(1)}, u32[]{:S(2)}, u32[]{:S(2)}) async-start(f32[16,40,128]{2,1,0:T(8,128)} %shard_map.74), calls=%async_computation.2 | async-start | bytes 655360 | tf_op jit(solution)/shard_map/all_to_all | solution.py:332
  56.7 0.0 collective-permute-done.other_ref
  56.8 3.6 %shard_map.69 = (f32[1,4096]{1,0:T(1,128)}, f32[136,128]{1,0:T(8,128)S(1)}) custom-call(s32[1]{0:T(128)S(6)} %sub.8.side_ref, f32[32,1024]{1,0:T(8,128)S(1)} %get-tuple-element.17.x_ref, f32[32,4096]{1,0:T(8,128)S(1)} %get-tuple-element.18.y_ref, f32[1,1024]{1,0:T(1,128)S(1)} %get-tuple-element.22.total_ref, f32[32,128]{1,0:T(8,128)S(1)} %shard_map.68.mine_ref.after_ref, ...), custom_call_target="tpu_custom_call" | custom-call | flops 3221225472 | bytes 16777216 | tf_op jit(solution)/shard_map/pallas_call | solution.py:343
  60.4 0.0 collective-permute-start.1
  60.4 3.6 %shard_map.70 = (f32[1,4096]{1,0:T(1,128)}, f32[136,128]{1,0:T(8,128)S(1)}) custom-call(s32[1]{0:T(128)} %bitcast.2.side_ref, f32[32,1024]{1,0:T(8,128)S(1)} %get-tuple-element.17.x_ref, f32[32,4096]{1,0:T(8,128)S(1)} %get-tuple-element.18.y_ref, f32[1,1024]{1,0:T(1,128)S(1)} %get-tuple-element.22.total_ref, f32[32,128]{1,0:T(8,128)S(1)} %shard_map.68.mine_ref.after_ref, ...), custom_call_target="tpu_custom_call" | custom-call | flops 3221225472 | bytes 16777216 | tf_op jit(solution)/shard_map/pallas_call | solution.py:344
  64.0 0.7 collective-permute-done.1
  64.7 0.7 collective-permute-start.2
  65.5 4.4 %all-to-all-done.2.part_ref = f32[16,40,128]{2,1,0:T(8,128)S(1)} async-done(((f32[16,40,128]{2,1,0:T(8,128)}), f32[16,40,128]{2,1,0:T(8,128)S(1)}, u32[]{:S(2)}, u32[]{:S(2)}) %all-to-all-start.2) | async-done | bytes 327712 | tf_op jit(solution)/shard_map/all_to_all | solution.py:332
  69.9 0.8 shard_map.75
  70.6 5.6 %all-to-all-start.3 = ((f32[16,32,128]{2,1,0:T(8,128)}), f32[16,32,128]{2,1,0:T(8,128)S(1)}, u32[]{:S(2)}, u32[]{:S(2)}) async-start(f32[16,32,128]{2,1,0:T(8,128)} %shard_map.75), calls=%async_computation.3 | async-start | bytes 524288 | tf_op jit(solution)/shard_map/all_to_all | solution.py:348
  76.2 0.0 collective-permute-done.2
  76.2 1.2 %collective-permute-start.3 = (f32[136,128]{1,0:T(8,128)S(1)}, f32[136,128]{1,0:T(8,128)S(1)}, u32[]{:S(2)}, u32[]{:S(2)}) collective-permute-start(f32[136,128]{1,0:T(8,128)S(1)} %add.8.one_ref), channel_id=1, source_target_pairs={{0,3},{1,2},{2,1},{3,0},{4,7},{5,6},{6,5},{7,4},{8,11},{9,10},{10,... | collective-permute-start | bytes 208904 | tf_op jit(solution)/shard_map/ppermute | solution.py:350
  77.4 4.4 %collective-permute-done.3.two_ref = f32[136,128]{1,0:T(8,128)S(1)} collective-permute-done((f32[136,128]{1,0:T(8,128)S(1)}, f32[136,128]{1,0:T(8,128)S(1)}, u32[]{:S(2)}, u32[]{:S(2)}) %collective-permute-start.3) | collective-permute-done | bytes 69664 | tf_op jit(solution)/shard_map/ppermute | solution.py:350
  81.9 0.5 collective-permute-start.4
  82.3 3.9 %collective-permute-done.4.other_ref.after_ref = f32[128,128]{1,0:T(8,128)S(1)} collective-permute-done((f32[128,128]{1,0:T(8,128)S(1)}, f32[128,128]{1,0:T(8,128)S(1)}, u32[]{:S(2)}, u32[]{:S(2)}) %collective-permute-start.4) | collective-permute-done | bytes 65568 | tf_op jit(solution)/shard_map/ppermute | solution.py:351
  86.2 1.4 %all-to-all-done.3.image_ref = f32[16,32,128]{2,1,0:T(8,128)S(1)} async-done(((f32[16,32,128]{2,1,0:T(8,128)}), f32[16,32,128]{2,1,0:T(8,128)S(1)}, u32[]{:S(2)}, u32[]{:S(2)}) %all-to-all-start.3) | async-done | bytes 262176 | tf_op jit(solution)/shard_map/all_to_all | solution.py:348
  87.6 0.0 collective-permute-start.6
  87.6 0.7 shard_map.72
  88.3 0.9 collective-permute-done.6.other_ref
  89.2 0.8 shard_map.77
  (4 shorter events, 0.0 us)
Async XLA Ops:
  12.6 11.6 %all-to-all-start = ((f32[8,8,128]{2,1,0:T(8,128)}), f32[8,8,128]{2,1,0:T(8,128)S(1)}, u32[]{:S(2)}, u32[]{:S(2)}) async-start(f32[8,8,128]{2,1,0:T(8,128)} %get-tuple-element.20), calls=%async_computation | async-start | bytes 65536 | tf_op jit(solution)/shard_map/all_to_all | solution.py:311
  27.9 21.3 %all-to-all-start.1 = ((f32[16,32,128]{2,1,0:T(8,128)}), f32[16,32,128]{2,1,0:T(8,128)S(1)}, u32[]{:S(2)}, u32[]{:S(2)}) async-start(f32[16,32,128]{2,1,0:T(8,128)} %get-tuple-element.23), calls=%async_computation.1 | async-start | bytes 524288 | tf_op jit(solution)/shard_map/all_to_all | solution.py:320
  44.6 4.8 %collective-permute-start.5 = (f32[16,40,128]{2,1,0:T(8,128)S(1)}, f32[16,40,128]{2,1,0:T(8,128)S(1)}, u32[]{:S(2)}, u32[]{:S(2)}) collective-permute-start(f32[16,40,128]{2,1,0:T(8,128)S(1)} %get-tuple-element.29), channel_id=1, source_target_pairs={{0,8},{8,0},{16,24},{24,16},{32,40},{40,32},{48,56},{56,48},{64,72... | collective-permute-start | bytes 983048 | tf_op jit(solution)/shard_map/ppermute | solution.py:331
  49.3 7.5 %collective-permute-start = (f32[32,128]{1,0:T(8,128)S(1)}, f32[32,128]{1,0:T(8,128)S(1)}, u32[]{:S(2)}, u32[]{:S(2)}) collective-permute-start(f32[32,128]{1,0:T(8,128)S(1)} %shard_map.68.mine_ref.after_ref), channel_id=1, source_target_pairs={{0,8},{8,0},{16,24},{24,16},{32,40},{40,32},{48,56},{56,48},{64,72... | collective-permute-start | bytes 49160 | tf_op jit(solution)/shard_map/ppermute | solution.py:322
  50.2 19.7 %all-to-all-start.2 = ((f32[16,40,128]{2,1,0:T(8,128)}), f32[16,40,128]{2,1,0:T(8,128)S(1)}, u32[]{:S(2)}, u32[]{:S(2)}) async-start(f32[16,40,128]{2,1,0:T(8,128)} %shard_map.74), calls=%async_computation.2 | async-start | bytes 655360 | tf_op jit(solution)/shard_map/all_to_all | solution.py:332
  60.4 4.4 %collective-permute-start.1 = (f32[136,128]{1,0:T(8,128)S(1)}, f32[136,128]{1,0:T(8,128)S(1)}, u32[]{:S(2)}, u32[]{:S(2)}) collective-permute-start(f32[136,128]{1,0:T(8,128)S(1)} %get-tuple-element.25.after_ref), channel_id=1, source_target_pairs={{0,4},{1,5},{2,6},{3,7},{4,0},{5,1},{6,2},{7,3},{8,12},{9,13},{10,... | collective-permute-start | bytes 208904 | tf_op jit(solution)/shard_map/ppermute | solution.py:345
  64.7 11.5 %collective-permute-start.2 = (f32[136,128]{1,0:T(8,128)S(1)}, f32[136,128]{1,0:T(8,128)S(1)}, u32[]{:S(2)}, u32[]{:S(2)}) collective-permute-start(f32[136,128]{1,0:T(8,128)S(1)} %add.7.after_ref), channel_id=1, source_target_pairs={{0,1},{1,0},{2,3},{3,2},{4,5},{5,4},{6,7},{7,6},{8,9},{9,8},{10,11... | collective-permute-start | bytes 208904 | tf_op jit(solution)/shard_map/ppermute | solution.py:349
  70.6 17.0 %all-to-all-start.3 = ((f32[16,32,128]{2,1,0:T(8,128)}), f32[16,32,128]{2,1,0:T(8,128)S(1)}, u32[]{:S(2)}, u32[]{:S(2)}) async-start(f32[16,32,128]{2,1,0:T(8,128)} %shard_map.75), calls=%async_computation.3 | async-start | bytes 524288 | tf_op jit(solution)/shard_map/all_to_all | solution.py:348
  76.2 5.6 %collective-permute-start.3 = (f32[136,128]{1,0:T(8,128)S(1)}, f32[136,128]{1,0:T(8,128)S(1)}, u32[]{:S(2)}, u32[]{:S(2)}) collective-permute-start(f32[136,128]{1,0:T(8,128)S(1)} %add.8.one_ref), channel_id=1, source_target_pairs={{0,3},{1,2},{2,1},{3,0},{4,7},{5,6},{6,5},{7,4},{8,11},{9,10},{10,... | collective-permute-start | bytes 208904 | tf_op jit(solution)/shard_map/ppermute | solution.py:350
  81.9 4.4 %collective-permute-start.4 = (f32[128,128]{1,0:T(8,128)S(1)}, f32[128,128]{1,0:T(8,128)S(1)}, u32[]{:S(2)}, u32[]{:S(2)}) collective-permute-start(f32[128,128]{1,0:T(8,128)S(1)} %shard_map.71.mine_ref), channel_id=1, source_target_pairs={{0,4},{1,5},{2,6},{3,7},{4,0},{5,1},{6,2},{7,3},{8,12},{9,13},{10,... | collective-permute-start | bytes 196616 | tf_op jit(solution)/shard_map/ppermute | solution.py:351
  87.6 1.5 %collective-permute-start.6 = (f32[16,32,128]{2,1,0:T(8,128)S(1)}, f32[16,32,128]{2,1,0:T(8,128)S(1)}, u32[]{:S(2)}, u32[]{:S(2)}) collective-permute-start(f32[16,32,128]{2,1,0:T(8,128)S(1)} %shard_map.76.mine_ref), channel_id=1, source_target_pairs={{0,8},{8,0},{16,24},{24,16},{32,40},{40,32},{48,56},{56,48},{64,72... | collective-permute-start | bytes 786440 | tf_op jit(solution)/shard_map/ppermute | solution.py:354

commit v5 on v4

v5 whole, which is shorter than its diff:
```python
import functools
import math

import jax
import jax.numpy as jnp
from jax import lax
from jax.experimental import pallas as pl
from jax.experimental.pallas import tpu as pltpu
from jax.sharding import Mesh
from jax.sharding import PartitionSpec as P

EPS = 0.05
C2 = 1.4426950408889634 / EPS
LN = EPS * math.log(2.0)
LEAST = 2.0**-80
LIFT = 64.0
BF = jnp.bfloat16
F32 = jnp.float32
K = 32
KD = 8 * K
VM = pl.BlockSpec(memory_space=pltpu.VMEM)
SM = pl.BlockSpec(memory_space=pltpu.SMEM)
LANES = 128
TALL, WIDE = 1024, 512
BLOCK = ((TALL, WIDE), F32)


def thirds(v):
    hi = v.astype(BF)
    rest = v - hi.astype(F32)
    mid = rest.astype(BF)
    return hi, mid, (rest - mid.astype(F32)).astype(BF)


def halves(v):
    hi = v.astype(BF)
    return hi, (v - hi.astype(F32)).astype(BF)


def offsets(b, first):
    hi, mid, lo = (part.astype(F32) for part in thirds(b))
    row = lax.broadcasted_iota(jnp.int32, (2 * K, b.shape[1]), 0)
    row, one = (row, row - 3) if first else (row - 3, row)
    value = jnp.where(row == 0, hi, jnp.where(row == 1, mid, jnp.where(row == 2, lo, 0.0)))
    return jnp.where((one >= 0) & (one < 3), 1.0, value).astype(BF)


def first_side(v, b):
    hi, mid, lo = thirds(v)
    return jnp.concatenate([hi, hi, hi, mid, mid, lo, offsets(b, True)], 0)


def second_side(v, b):
    hi, mid, lo = thirds(v)
    return jnp.concatenate([hi, mid, lo, hi, mid, hi, offsets(b, False)], 0)


def coordinates(v):
    hi, lo = halves(v)
    return jnp.concatenate([hi, lo, jnp.ones((K // 2, v.shape[1]), BF)], 0)


def cut(tiles, k):
    return tiles[:, k * LANES : (k + 1) * LANES]


def blocks(a_ref, b_ref, t_refs, first, use):
    tall, wide = t_refs[0].shape
    places = [(r, c) for c in range(first, first + b_ref.shape[1], wide) for r in range(0, a_ref.shape[0], tall)]

    def fill(i):
        r, c = places[i]
        t_refs[i % 2][...] = jnp.dot(a_ref[r : r + tall, :], b_ref[:, c : c + wide], preferred_element_type=F32)

    fill(0)
    for i, (r, c) in enumerate(places):
        if i + 1 < len(places):
            fill(i + 1)
        use(t_refs[i % 2], slice(r, r + tall), slice(c, c + wide))


def exact_logs(a_ref, b_ref, t_ref, l_ref):
    tall, wide = t_ref.shape

    def column(c, _):
        cols = pl.ds(pl.multiple_of(c * wide, wide), wide)

        def fill(r):
            rows = pl.ds(pl.multiple_of(r * tall, tall), tall)
            t_ref[...] = jnp.dot(a_ref[rows, :], b_ref[:, cols], preferred_element_type=F32)

        def highest(r, peak):
            fill(r)
            return jnp.maximum(peak, jnp.max(t_ref[...], 0, keepdims=True))

        count = a_ref.shape[0] // tall
        peak = lax.fori_loop(0, count, highest, jnp.full((1, wide), -1e30, F32))

        def add(r, total):
            fill(r)
            return total + jnp.sum(jnp.exp2(t_ref[...] - peak), 0, keepdims=True)

        l_ref[:, cols] = peak + jnp.log2(lax.fori_loop(0, count, add, jnp.zeros((1, wide), F32)))
        return 0

    lax.fori_loop(0, b_ref.shape[1] // wide, column, 0)


def log_sums(a_ref, b_ref, t_refs, l_ref):
    def use(t_ref, rows, cols):
        part = jnp.sum(jnp.exp2(t_ref[...]), 0, keepdims=True)
        l_ref[:, cols] = part if rows.start == 0 else l_ref[:, cols] + part

    blocks(a_ref, b_ref, t_refs, 0, use)
    least = jnp.min(l_ref[...])
    l_ref[...] = jnp.log2(l_ref[...])

    @pl.when(least < LEAST)
    def _():
        exact_logs(a_ref, b_ref, t_refs[0], l_ref)


def by_coordinates(v, p):
    hi, lo = halves(p)
    return jnp.dot(v, hi, preferred_element_type=F32) + jnp.dot(v, lo, preferred_element_type=F32)


def weighted(a_ref, b_ref, v_ref, t_refs, o_ref):
    def use(t_ref, rows, cols):
        part = by_coordinates(v_ref[:, rows], jnp.exp2(t_ref[...]))
        o_ref[:, cols] = part if rows.start == 0 else o_ref[:, cols] + part

    blocks(a_ref, b_ref, t_refs, 0, use)


def row_logs(x_hbm, y_hbm, g_hbm, out_ref, x_ref, y_ref, g_ref, a_ref, b_ref, l_ref, t0_ref, t1_ref, sems):
    t_refs = (t0_ref, t1_ref)
    sides = ((y_hbm, y_ref), (x_hbm, x_ref), (g_hbm, g_ref))
    copies = [pltpu.make_async_copy(*pair, sems.at[i]) for i, pair in enumerate(sides)]
    for copy in copies:
        copy.start()
    for copy in copies:
        copy.wait()
    x, y = x_ref[...], y_ref[...]
    y_sq = jnp.sum(y * y, 0, keepdims=True)
    lift = (g_ref[...] - y_sq) * C2
    longest = jnp.sqrt(jnp.sum(x * x, 0, keepdims=True)) * jnp.sqrt(jnp.max(y_sq, 1, keepdims=True))
    bound = jnp.max(lift, 1, keepdims=True) + 2 * C2 * longest
    a_ref[...] = first_side(y, lift).T
    b_ref[...] = second_side(x * (2 * C2), -bound)
    log_sums(a_ref, b_ref, t_refs, l_ref)
    total = l_ref[...] + bound
    for k in range(out_ref.shape[1]):
        for d in range(out_ref.shape[0]):
            out_ref[d, k : k + 1, :] = cut(total, k)


def core_of(me_ref):
    return me_ref[0] >> 3 & 1


def side_of(me_ref):
    return me_ref[0] >> 2 & 1


def column_sums(log_n, first, me_ref, x_ref, y_ref, g_ref, from_ref, *refs):
    if first:
        pot_ref, total_ref, out_ref, a_ref, b_ref, v_ref, o_ref, l_ref, *t_refs = refs
        parts = from_ref[...]
        top = jnp.max(parts, 0)
        total = top + jnp.log2(jnp.sum(jnp.exp2(parts - top[None]), 0))
        total = jnp.concatenate([total[k : k + 1, :] for k in range(total.shape[0])], 1) + log_n
        total_ref[...] = total
        pot_ref[...] = jnp.sum(x_ref[...] * x_ref[...], 0, keepdims=True) - LN * total
    else:
        out_ref, a_ref, b_ref, v_ref, o_ref, l_ref, *t_refs = refs
        total = from_ref[...]
    half = o_ref.shape[1]
    side = 1 - core_of(me_ref) if first else core_of(me_ref)
    cols = pl.ds(pl.multiple_of(side * half, half), half)
    x, y = x_ref[...], y_ref[:, cols]
    bound = (jnp.sum(y * y, 0, keepdims=True) - g_ref[:, cols]) * C2 - log_n
    a_ref[...] = first_side(x * (2 * C2), -total).T
    b_ref[...] = second_side(y, -bound)
    v_ref[...] = coordinates(x)
    weighted(a_ref, b_ref, v_ref, t_refs, o_ref)
    mass = o_ref[2 * K : 2 * K + 1, :]
    l_ref[...] = jnp.log2(mass) + bound

    @pl.when(jnp.min(mass) < LEAST)
    def _():
        t_ref = t_refs[0]
        wide = t_ref.shape[1]
        exact_logs(a_ref, b_ref, t_ref, l_ref)
        l_ref[...] += bound
        b_ref[6 * K : KD, :] = offsets(-l_ref[...], False)

        def column(c, _):
            at = pl.ds(pl.multiple_of(c * wide, wide), wide)
            t_ref[...] = jnp.dot(a_ref[...], b_ref[:, at], preferred_element_type=F32)
            o_ref[:, at] = by_coordinates(v_ref[...], jnp.exp2(t_ref[...]))
            return 0

        lax.fori_loop(0, half // wide, column, 0)

    for q in range(out_ref.shape[0]):
        at = slice(q * LANES, (q + 1) * LANES)
        out_ref[q, 0:K, :] = (o_ref[0:K, at] + o_ref[K : 2 * K, at]) / o_ref[2 * K : 2 * K + 1, at]
        out_ref[q, K : K + 8, :] = jnp.broadcast_to(l_ref[:, at], (8, LANES))


def merge(logs, images):
    top = functools.reduce(jnp.maximum, logs)
    shares = [jnp.exp2(one - top) for one in logs]
    mass = functools.reduce(jnp.add, shares)
    image = functools.reduce(jnp.add, [w * i for w, i in zip(shares, images)])
    return top + jnp.log2(mass), image / mass


def merge_pair(one_ref, two_ref, out_ref):
    pair, n = (one_ref, two_ref), out_ref.shape[0]
    log, image = merge([ref[:, K : K + 8, :][:, 0:1, :] for ref in pair], [ref[:, 0:K, :] for ref in pair])
    out_ref[:, 0:K, :] = image
    for q in range(n):
        out_ref[0, K + q : K + q + 1, :] = log[q]
    for d in range(1, n):
        out_ref[d, K:, :] = out_ref[0, K:, :]


def merge_logs(part_ref, out_ref):
    parts = [part_ref[d, K:, :] for d in range(part_ref.shape[0])]
    top = functools.reduce(jnp.maximum, parts)
    out_ref[...] = top + jnp.log2(functools.reduce(jnp.add, [jnp.exp2(part - top) for part in parts]))


def merge_chunk(me_ref, part_ref, after_ref, out_ref):
    n = part_ref.shape[0]
    logs = [part_ref[d, pl.ds(K + (me_ref[0] >> 4), 1), :] for d in range(n)]
    _, image = merge(logs, [part_ref[d, 0:K, :] for d in range(n)])
    for d in range(n):
        out_ref[d] = image


def row_images(log_n, own, me_ref, x_ref, y_ref, total_ref, mine_ref, other_ref, after_ref, pot_ref, out_ref, a_ref, b_ref, v_ref, o_ref, l_ref, *t_refs):
    for part, ref in ((core_of(me_ref), mine_ref), (1 - core_of(me_ref), other_ref)):
        for q in range(ref.shape[0]):
            at = pl.ds(pl.multiple_of((part * ref.shape[0] + q) * LANES, LANES), LANES)
            l_ref[:, at] = ref[q : q + 1, :]
    logs = l_ref[...]
    y = y_ref[...]
    pot_ref[...] = jnp.sum(y * y, 0, keepdims=True) - LN * (logs + log_n)
    half = o_ref.shape[1]
    side = side_of(me_ref) if own else 1 - side_of(me_ref)
    cols = pl.ds(pl.multiple_of(side * half, half), half)
    a_ref[...] = first_side(y, -logs).T
    b_ref[...] = second_side(x_ref[:, cols] * (2 * C2), LIFT - total_ref[:, cols])
    v_ref[...] = coordinates(y)
    weighted(a_ref, b_ref, v_ref, t_refs, o_ref)
    tiles = half // LANES
    for k in range(tiles):
        lanes = slice(k * LANES, (k + 1) * LANES)
        for r in range(0, K, 8):
            out_ref[r * tiles + 8 * k : r * tiles + 8 * k + 8, :] = o_ref[r : r + 8, lanes] + o_ref[K + r : K + r + 8, lanes]
        out_ref[K * tiles + k : K * tiles + k + 1, :] = o_ref[2 * K : 2 * K + 1, lanes]
    out_ref[K * tiles + tiles :, :] = jnp.ones((out_ref.shape[0] - (K + 1) * tiles, LANES), F32)


def add_divide(one_ref, two_ref, out_ref):
    rows = out_ref.shape[0]
    tiles = rows // K
    mass = one_ref[rows : rows + 8, :] + two_ref[rows : rows + 8, :]
    for k in range(tiles):
        under = jnp.broadcast_to(mass[k : k + 1, :], (8, LANES))
        for r in range(0, K, 8):
            at = slice(r * tiles + 8 * k, r * tiles + 8 * k + 8)
            out_ref[at, :] = (one_ref[at, :] + two_ref[at, :]) / under


def lay_rows(me_ref, mine_ref, other_ref, out_ref):
    half = out_ref.shape[1] // 2
    tiles = half // LANES
    for side, ref in ((side_of(me_ref), mine_ref), (1 - side_of(me_ref), other_ref)):
        for k in range(tiles):
            cols = pl.ds(pl.multiple_of(side * half + k * LANES, LANES), LANES)
            for r in range(0, K, 8):
                out_ref[r : r + 8, cols] = ref[r * tiles + 8 * k : r * tiles + 8 * k + 8, :]


def hold(image_ref, after_ref, out_ref):
    pass


def lay_columns(me_ref, mine_ref, other_ref, out_ref):
    half = out_ref.shape[1] // 2
    for side, ref in ((core_of(me_ref), mine_ref), (1 - core_of(me_ref), other_ref)):
        for q in range(ref.shape[0]):
            out_ref[:, pl.ds(pl.multiple_of(side * half + q * LANES, LANES), LANES)] = ref[q]


def call(kernel, ins, outs, scratch=(), copies=0, aliases={}, cost=None):
    return pl.pallas_call(
        kernel,
        out_shape=tuple(jax.ShapeDtypeStruct(shape, F32) for shape in outs),
        in_specs=[{"s": SM, "h": pl.BlockSpec(memory_space=pltpu.HBM), "v": VM}[spec] for spec in ins],
        out_specs=tuple(VM for _ in outs),
        scratch_shapes=[pltpu.VMEM(*one) for one in scratch] + [pltpu.SemaphoreType.DMA((copies,))] * (copies > 0),
        input_output_aliases=aliases,
        cost_estimate=cost,
        compiler_params=pltpu.CompilerParams(vmem_limit_bytes=50 << 20),
    )


def work(pairs, sums):
    return pl.CostEstimate(flops=2 * pairs * (KD + 256 * sums), transcendentals=pairs, bytes_accessed=8 * pairs)


def solution(mesh):
    n_src, n_tgt = mesh.shape["src"], mesh.shape["tgt"]
    pairs, ring = n_src // 2, n_tgt // 2
    grid = Mesh(mesh.devices.reshape(2, pairs // 2, 2, 2, ring), ("high", "line", "core", "low", "ring"))
    chips, tgt = ("high", "line"), ("low", "ring")
    src = (*chips, "core")
    swap = [(0, 1), (1, 0)]
    over = [(i, (i + ring) % n_tgt) for i in range(n_tgt)]
    near = [(i, i ^ 1) for i in range(n_tgt)]
    far = [(i, i ^ 3) for i in range(n_tgt)]

    def shards(x, y, g):
        ns, nt = x.shape[1], y.shape[1]
        rows = ns // LANES
        me = lax.axis_index(src + tgt).astype(jnp.int32).reshape(1)
        g = g.reshape(1, nt)
        chunk = (pairs, K + 8, LANES)

        part, x, y, g = call(
            row_logs,
            "hhh",
            [(n_tgt, rows, LANES), x.shape, y.shape, g.shape],
            [((nt, KD), BF), ((KD, ns), BF), ((1, ns), F32), BLOCK, BLOCK],
            3,
            cost=work(ns * nt, 0),
        )(*(pltpu.with_memory_space_constraint(one, pltpu.HBM) for one in (x, y, g)))
        part = lax.all_to_all(part, tgt, 0, 0, tiled=True)

        sums = [((ns, KD), BF), ((KD, nt // 2), BF), ((80, ns), BF), ((80, nt // 2), F32), ((1, nt // 2), F32), BLOCK, BLOCK]
        log_n = math.log2(ns * n_src)
        source_potential, total, send = call(
            functools.partial(column_sums, log_n, True), "svvvv", [(1, ns), (1, ns), chunk], sums, cost=work(ns * nt // 2, 2)
        )(me, x, y, g, part)
        sent = lax.ppermute(send, "core", swap)
        (keep,) = call(
            functools.partial(column_sums, log_n, False), "svvvv", [chunk], sums, cost=work(ns * nt // 2, 2)
        )(me, x, y, g, total)
        (part,) = call(merge_pair, "vv", [(pairs, K + pairs, LANES)])(keep, sent)
        image = lax.all_to_all(part, chips, 0, 0, tiled=True)
        (mine,) = call(merge_logs, "v", [(pairs, LANES)])(image)
        other = lax.ppermute(mine, "core", swap)

        half = ns // 2
        tall = (K * half) // LANES
        images = lambda own: call(
            functools.partial(row_images, math.log2(nt * n_tgt), own),
            "svvvvvv",
            [(1, nt), (tall + 8, LANES)],
            [((nt, KD), BF), ((KD, half), BF), ((80, nt), BF), ((80, half), F32), ((1, nt), F32), BLOCK, BLOCK],
            cost=work(half * nt, 2),
        )
        target_potential, sent = images(False)(me, x, y, total, mine, other, mine)
        _, held = images(True)(me, x, y, total, mine, other, sent)
        sent = lax.ppermute(sent, tgt, over)
        held = held + sent
        (image,) = call(merge_chunk, "svv", [(pairs, K, LANES)], cost=work(half * nt, 2))(me, image, held)
        image = lax.all_to_all(image, chips, 0, 0, tiled=True)
        held = held + lax.ppermute(held, tgt, near)
        (held,) = call(add_divide, "vv", [(tall, LANES)], cost=work(half * nt, 2))(held, lax.ppermute(held, tgt, far))
        sent = lax.ppermute(held, tgt, over)
        (source_image,) = call(lay_rows, "svv", [(K, ns)], cost=work(half * nt, 2))(me, held, sent)
        (image,) = call(hold, "vv", [image.shape], aliases={0: 0})(image, sent)
        (target_image,) = call(lay_columns, "svv", [(K, nt)])(me, image, lax.ppermute(image, "core", swap))
        return source_potential.reshape(ns), target_potential.reshape(nt), source_image, target_image

    return jax.shard_map(
        shards,
        mesh=grid,
        in_specs=(P(None, src), P(None, tgt), P(tgt)),
        out_specs=(P(src), P(tgt), P(None, src), P(None, tgt)),
        check_vma=False,
    )
```

time: 91.3 us -> 87.8 us (0.962)
  blocking collectives: 0 us -> 24.9 us
  starting transfers between devices: 31 us -> 13.7 us
  waiting for transfers between devices: 26.5 us -> 18.3 us
  Pallas kernels: 31.8 us -> 28.9 us
    all_to_all x0 -> x1, blocking collectives: none -> 24.9 us  [shards(): image = lax.all_to_all(part, chips, 0, 0, tiled=True)]
    all_to_all x4 -> x2, starting transfers between devices: 28.4 us -> 10.8 us  [the longest x1 5.44 us: shards(): image = lax.all_to_all(image, chips, 0, 0, tiled=True)]
    all_to_all x4 -> x2, waiting for transfers between devices: 16.6 us -> 7.7 us  [the longest x1 6.26 us: shards(): part = lax.all_to_all(part, tgt, 0, 0, tiled=True)]
    pallas_call x8, Pallas kernels: 19 us -> 16.1 us  [the longest x1 3.87 us: shards(): call(functools.partial(column_sums, log_n, True), 'svvvv', [(1, ns), (1,...]
  transfers between devices with their start and end apart: 11 -> 9, of which waited for: 8 -> 7; matrix products, arithmetic and copies ran while one was open for 0% -> 0% of each run, Pallas kernels for 17% -> 10%
where the time goes in v5:
time: 87.8 us; the launch traced here: 86.5 us
  Pallas kernels  28.9 us (33%)
  blocking collectives  24.9 us (28%)
  waiting for transfers between devices  18.3 us (21%)
  starting transfers between devices  13.7 us (16%)
    all_to_all x1, blocking collectives, shards(): image = lax.all_to_all(part, chips, 0, 0, tiled=True)  24.9 us
    pallas_call x1, Pallas kernels, shards(): call(row_logs, 'hhh', [(n_tgt, rows, LANES), x.shape, y.shape, g.shape],...  12 us
    all_to_all x1, waiting for transfers between devices, shards(): part = lax.all_to_all(part, tgt, 0, 0, tiled=True)  6.26 us
    all_to_all x1, starting transfers between devices, shards(): image = lax.all_to_all(image, chips, 0, 0, tiled=True)  5.44 us
    all_to_all x1, starting transfers between devices, shards(): part = lax.all_to_all(part, tgt, 0, 0, tiled=True)  5.31 us
    ppermute x1, waiting for transfers between devices, shards(): lax.ppermute(held, tgt, far)  4.44 us
    pallas_call x1, Pallas kernels, shards(): call(functools.partial(column_sums, log_n, True), 'svvvv', [(1, ns), (1,...  3.87 us
    pallas_call x1, Pallas kernels, shards(): target_potential, sent = images(False)(me, x, y, total, mine, other, mine)  3.62 us
  transfers between devices with their start and end apart: 9, of which 7 were waited for; matrix products, arithmetic and copies ran while one was open for 0% of the time, Pallas kernels for 10%

profile of v5, /device:TPU:32, one launch (start us, length us, event | category | flops | bytes accessed | tf_op | source)
XLA Modules:
  0.0 86.5 jit_solution(6383138987747475878)
XLA Ops:
  0.6 12.0 %shard_map.66 = (f32[8,8,128]{2,1,0:T(8,128)}, f32[32,1024]{1,0:T(8,128)S(1)}, f32[32,4096]{1,0:T(8,128)S(1)}, f32[1,4096]{1,0:T(1,128)S(1)}) custom-call(f32[32,1024]{1,0:T(8,128)} %x_hbm.1, f32[32,4096]{1,0:T(8,128)} %y_hbm.1, f32[1,4096]{1,0:T(1,128)} %bitcast.4), custom_call_target="tpu_custom_call" | custom-call | flops 2147483648 | bytes 33554432 | tf_op jit(solution)/shard_map/pallas_call | solution.py:335
  12.6 5.3 %all-to-all-start = ((f32[8,8,128]{2,1,0:T(8,128)}), f32[8,8,128]{2,1,0:T(8,128)S(1)}, u32[]{:S(2)}, u32[]{:S(2)}) async-start(f32[8,8,128]{2,1,0:T(8,128)} %get-tuple-element.17), calls=%async_computation | async-start | bytes 65536 | tf_op jit(solution)/shard_map/all_to_all | solution.py:343
  17.9 6.3 %all-to-all-done.from_ref = f32[8,8,128]{2,1,0:T(8,128)S(1)} async-done(((f32[8,8,128]{2,1,0:T(8,128)}), f32[8,8,128]{2,1,0:T(8,128)S(1)}, u32[]{:S(2)}, u32[]{:S(2)}) %all-to-all-start) | async-done | bytes 32800 | tf_op jit(solution)/shard_map/all_to_all | solution.py:343
  24.2 3.9 %shard_map.67 = (f32[1,1024]{1,0:T(1,128)}, f32[1,1024]{1,0:T(1,128)S(1)}, f32[16,40,128]{2,1,0:T(8,128)S(1)}) custom-call(s32[1]{0:T(128)} %bitcast.me_ref, f32[32,1024]{1,0:T(8,128)S(1)} %get-tuple-element.14.x_ref, f32[32,4096]{1,0:T(8,128)S(1)} %get-tuple-element.15.y_ref, f32[1,4096]{1,0:T(1,128)S(1)} %get-tuple-element.16.g_ref, ...), custom_call_target="tpu_custom_call" | custom-call | flops 3221225472 | bytes 16777216 | tf_op jit(solution)/shard_map/pallas_call | solution.py:347
  28.1 0.0 collective-permute-start
  28.1 3.4 %shard_map.68.one_ref = f32[16,40,128]{2,1,0:T(8,128)S(1)} custom-call(s32[1]{0:T(128)} %bitcast.me_ref, f32[32,1024]{1,0:T(8,128)S(1)} %get-tuple-element.14.x_ref, f32[32,4096]{1,0:T(8,128)S(1)} %get-tuple-element.15.y_ref, f32[1,4096]{1,0:T(1,128)S(1)} %get-tuple-element.16.g_ref, f32[1,1024]{1,0:T(1,128)S(1)} %get-tuple-element.19.from_ref.total_ref), custom_call_target="tpu_custom_call" | custom-call | flops 3221225472 | bytes 16777216 | tf_op jit(solution)/shard_map/pallas_call | solution.py:351
  31.5 0.0 collective-permute-done.two_ref
  31.5 0.1 shard_map.69
  31.6 24.9 %all_to_all.15.part_ref = f32[16,48,128]{2,1,0:T(8,128)S(1)} all-to-all(f32[16,48,128]{2,1,0:T(8,128)S(1)} %shard_map.69), channel_id=1, replica_groups=mesh['high'=2,'line'=8,'core'=2,'low'=2,'ring'=4] {'high','line'}, dimensions={0} | all-to-all | bytes 786432 | tf_op jit(solution)/shard_map/all_to_all | solution.py:355
  56.6 0.1 collective-permute-start.1
  56.7 1.2 %collective-permute-done.1.other_ref = f32[16,128]{1,0:T(8,128)S(1)} collective-permute-done((f32[16,128]{1,0:T(8,128)S(1)}, f32[16,128]{1,0:T(8,128)S(1)}, u32[]{:S(2)}, u32[]{:S(2)}) %collective-permute-start.1) | collective-permute-done | bytes 8224 | tf_op jit(solution)/shard_map/ppermute | solution.py:357
  57.8 3.6 %shard_map.71 = (f32[1,4096]{1,0:T(1,128)}, f32[136,128]{1,0:T(8,128)S(1)}) custom-call(s32[1]{0:T(128)} %bitcast.me_ref, f32[32,1024]{1,0:T(8,128)S(1)} %get-tuple-element.14.x_ref, f32[32,4096]{1,0:T(8,128)S(1)} %get-tuple-element.15.y_ref, f32[1,1024]{1,0:T(1,128)S(1)} %get-tuple-element.19.from_ref.total_ref, ...), custom_call_target="tpu_custom_call" | custom-call | flops 3221225472 | bytes 16777216 | tf_op jit(solution)/shard_map/pallas_call | solution.py:368
  61.5 0.0 collective-permute-start.2
  61.5 3.6 %shard_map.72 = (f32[1,4096]{1,0:T(1,128)}, f32[136,128]{1,0:T(8,128)S(1)}) custom-call(s32[1]{0:T(128)} %bitcast.me_ref, f32[32,1024]{1,0:T(8,128)S(1)} %get-tuple-element.14.x_ref, f32[32,4096]{1,0:T(8,128)S(1)} %get-tuple-element.15.y_ref, f32[1,1024]{1,0:T(1,128)S(1)} %get-tuple-element.19.from_ref.total_ref, ...), custom_call_target="tpu_custom_call" | custom-call | flops 3221225472 | bytes 16777216 | tf_op jit(solution)/shard_map/pallas_call | solution.py:369
  65.1 0.7 collective-permute-done.2
  65.8 0.7 collective-permute-start.3
  66.5 0.8 shard_map.75
  67.3 5.4 %all-to-all-start.2 = ((f32[16,32,128]{2,1,0:T(8,128)}), f32[16,32,128]{2,1,0:T(8,128)S(1)}, u32[]{:S(2)}, u32[]{:S(2)}) async-start(f32[16,32,128]{2,1,0:T(8,128)} %shard_map.75), calls=%async_computation.2 | async-start | bytes 524288 | tf_op jit(solution)/shard_map/all_to_all | solution.py:373
  72.7 0.0 collective-permute-done.3
  72.8 1.2 %collective-permute-start.4 = (f32[136,128]{1,0:T(8,128)S(1)}, f32[136,128]{1,0:T(8,128)S(1)}, u32[]{:S(2)}, u32[]{:S(2)}) collective-permute-start(f32[136,128]{1,0:T(8,128)S(1)} %add.23.one_ref), channel_id=1, source_target_pairs={{0,3},{1,2},{2,1},{3,0},{4,7},{5,6},{6,5},{7,4},{8,11},{9,10},{10,... | collective-permute-start | bytes 208904 | tf_op jit(solution)/shard_map/ppermute | solution.py:375
  73.9 4.4 %collective-permute-done.4.two_ref = f32[136,128]{1,0:T(8,128)S(1)} collective-permute-done((f32[136,128]{1,0:T(8,128)S(1)}, f32[136,128]{1,0:T(8,128)S(1)}, u32[]{:S(2)}, u32[]{:S(2)}) %collective-permute-start.4) | collective-permute-done | bytes 69664 | tf_op jit(solution)/shard_map/ppermute | solution.py:375
  78.4 0.9 %collective-permute-start.5 = (f32[128,128]{1,0:T(8,128)S(1)}, f32[128,128]{1,0:T(8,128)S(1)}, u32[]{:S(2)}, u32[]{:S(2)}) collective-permute-start(f32[128,128]{1,0:T(8,128)S(1)} %shard_map.73.mine_ref), channel_id=1, source_target_pairs={{0,4},{1,5},{2,6},{3,7},{4,0},{5,1},{6,2},{7,3},{8,12},{9,13},{10,... | collective-permute-start | bytes 196616 | tf_op jit(solution)/shard_map/ppermute | solution.py:376
  79.3 3.4 %collective-permute-done.5.other_ref.after_ref = f32[128,128]{1,0:T(8,128)S(1)} collective-permute-done((f32[128,128]{1,0:T(8,128)S(1)}, f32[128,128]{1,0:T(8,128)S(1)}, u32[]{:S(2)}, u32[]{:S(2)}) %collective-permute-start.5) | collective-permute-done | bytes 65568 | tf_op jit(solution)/shard_map/ppermute | solution.py:376
  82.7 1.4 %all-to-all-done.2.image_ref = f32[16,32,128]{2,1,0:T(8,128)S(1)} async-done(((f32[16,32,128]{2,1,0:T(8,128)}), f32[16,32,128]{2,1,0:T(8,128)S(1)}, u32[]{:S(2)}, u32[]{:S(2)}) %all-to-all-start.2) | async-done | bytes 262176 | tf_op jit(solution)/shard_map/all_to_all | solution.py:373
  84.2 0.0 collective-permute-start.6
  84.2 0.7 shard_map.74
  84.8 0.9 collective-permute-done.6.other_ref
  85.7 0.8 shard_map.77
  (5 shorter events, 0.1 us)
Async XLA Ops:
  12.6 11.6 %all-to-all-start = ((f32[8,8,128]{2,1,0:T(8,128)}), f32[8,8,128]{2,1,0:T(8,128)S(1)}, u32[]{:S(2)}, u32[]{:S(2)}) async-start(f32[8,8,128]{2,1,0:T(8,128)} %get-tuple-element.17), calls=%async_computation | async-start | bytes 65536 | tf_op jit(solution)/shard_map/all_to_all | solution.py:343
  28.1 3.5 %collective-permute-start = (f32[16,40,128]{2,1,0:T(8,128)S(1)}, f32[16,40,128]{2,1,0:T(8,128)S(1)}, u32[]{:S(2)}, u32[]{:S(2)}) collective-permute-start(f32[16,40,128]{2,1,0:T(8,128)S(1)} %get-tuple-element.20), channel_id=1, source_target_pairs={{0,8},{8,0},{1,9},{9,1},{2,10},{10,2},{3,11},{11,3},{4,12},{12,4},... | collective-permute-start | bytes 983048 | tf_op jit(solution)/shard_map/ppermute | solution.py:350
  56.6 1.3 %collective-permute-start.1 = (f32[16,128]{1,0:T(8,128)S(1)}, f32[16,128]{1,0:T(8,128)S(1)}, u32[]{:S(2)}, u32[]{:S(2)}) collective-permute-start(f32[16,128]{1,0:T(8,128)S(1)} %shard_map.70.mine_ref.after_ref), channel_id=1, source_target_pairs={{0,8},{8,0},{1,9},{9,1},{2,10},{10,2},{3,11},{11,3},{4,12},{12,4},... | collective-permute-start | bytes 24584 | tf_op jit(solution)/shard_map/ppermute | solution.py:357
  61.5 4.3 %collective-permute-start.2 = (f32[136,128]{1,0:T(8,128)S(1)}, f32[136,128]{1,0:T(8,128)S(1)}, u32[]{:S(2)}, u32[]{:S(2)}) collective-permute-start(f32[136,128]{1,0:T(8,128)S(1)} %get-tuple-element.22.after_ref), channel_id=1, source_target_pairs={{0,4},{1,5},{2,6},{3,7},{4,0},{5,1},{6,2},{7,3},{8,12},{9,13},{10,... | collective-permute-start | bytes 208904 | tf_op jit(solution)/shard_map/ppermute | solution.py:370
  65.8 7.0 %collective-permute-start.3 = (f32[136,128]{1,0:T(8,128)S(1)}, f32[136,128]{1,0:T(8,128)S(1)}, u32[]{:S(2)}, u32[]{:S(2)}) collective-permute-start(f32[136,128]{1,0:T(8,128)S(1)} %add.22.after_ref), channel_id=1, source_target_pairs={{0,1},{1,0},{2,3},{3,2},{4,5},{5,4},{6,7},{7,6},{8,9},{9,8},{10,11... | collective-permute-start | bytes 208904 | tf_op jit(solution)/shard_map/ppermute | solution.py:374
  67.3 16.9 %all-to-all-start.2 = ((f32[16,32,128]{2,1,0:T(8,128)}), f32[16,32,128]{2,1,0:T(8,128)S(1)}, u32[]{:S(2)}, u32[]{:S(2)}) async-start(f32[16,32,128]{2,1,0:T(8,128)} %shard_map.75), calls=%async_computation.2 | async-start | bytes 524288 | tf_op jit(solution)/shard_map/all_to_all | solution.py:373
  72.8 5.6 %collective-permute-start.4 = (f32[136,128]{1,0:T(8,128)S(1)}, f32[136,128]{1,0:T(8,128)S(1)}, u32[]{:S(2)}, u32[]{:S(2)}) collective-permute-start(f32[136,128]{1,0:T(8,128)S(1)} %add.23.one_ref), channel_id=1, source_target_pairs={{0,3},{1,2},{2,1},{3,0},{4,7},{5,6},{6,5},{7,4},{8,11},{9,10},{10,... | collective-permute-start | bytes 208904 | tf_op jit(solution)/shard_map/ppermute | solution.py:375
  78.4 4.4 %collective-permute-start.5 = (f32[128,128]{1,0:T(8,128)S(1)}, f32[128,128]{1,0:T(8,128)S(1)}, u32[]{:S(2)}, u32[]{:S(2)}) collective-permute-start(f32[128,128]{1,0:T(8,128)S(1)} %shard_map.73.mine_ref), channel_id=1, source_target_pairs={{0,4},{1,5},{2,6},{3,7},{4,0},{5,1},{6,2},{7,3},{8,12},{9,13},{10,... | collective-permute-start | bytes 196616 | tf_op jit(solution)/shard_map/ppermute | solution.py:376
  84.2 1.5 %collective-permute-start.6 = (f32[16,32,128]{2,1,0:T(8,128)S(1)}, f32[16,32,128]{2,1,0:T(8,128)S(1)}, u32[]{:S(2)}, u32[]{:S(2)}) collective-permute-start(f32[16,32,128]{2,1,0:T(8,128)S(1)} %shard_map.76.mine_ref), channel_id=1, source_target_pairs={{0,8},{8,0},{1,9},{9,1},{2,10},{10,2},{3,11},{11,3},{4,12},{12,4},... | collective-permute-start | bytes 786440 | tf_op jit(solution)/shard_map/ppermute | solution.py:379

commit v6 on v5

--- a/solution.py
+++ b/solution.py
@@ -133,7 +133,7 @@
     blocks(a_ref, b_ref, t_refs, 0, use)
 
 
-def row_logs(x_hbm, y_hbm, g_hbm, out_ref, x_ref, y_ref, g_ref, a_ref, b_ref, l_ref, t0_ref, t1_ref, sems):
+def row_logs(me_ref, x_hbm, y_hbm, g_hbm, out_ref, x_ref, y_ref, g_ref, a_ref, b_ref, l_ref, t0_ref, t1_ref, sems):
     t_refs = (t0_ref, t1_ref)
     sides = ((y_hbm, y_ref), (x_hbm, x_ref), (g_hbm, g_ref))
     copies = [pltpu.make_async_copy(*pair, sems.at[i]) for i, pair in enumerate(sides)]
@@ -165,24 +165,24 @@
 
 def column_sums(log_n, first, me_ref, x_ref, y_ref, g_ref, from_ref, *refs):
     if first:
-        pot_ref, total_ref, out_ref, a_ref, b_ref, v_ref, o_ref, l_ref, *t_refs = refs
+        pot_ref, total_ref, out_ref, a_ref, v_ref, b_ref, o_ref, l_ref, *t_refs = refs
         parts = from_ref[...]
         top = jnp.max(parts, 0)
         total = top + jnp.log2(jnp.sum(jnp.exp2(parts - top[None]), 0))
         total = jnp.concatenate([total[k : k + 1, :] for k in range(total.shape[0])], 1) + log_n
         total_ref[...] = total
-        pot_ref[...] = jnp.sum(x_ref[...] * x_ref[...], 0, keepdims=True) - LN * total
+        x = x_ref[...]
+        pot_ref[...] = jnp.sum(x * x, 0, keepdims=True) - LN * total
+        a_ref[...] = first_side(x * (2 * C2), -total).T
+        v_ref[...] = coordinates(x)
     else:
-        out_ref, a_ref, b_ref, v_ref, o_ref, l_ref, *t_refs = refs
-        total = from_ref[...]
+        a_ref, v_ref, out_ref, b_ref, o_ref, l_ref, *t_refs = refs
     half = o_ref.shape[1]
     side = 1 - core_of(me_ref) if first else core_of(me_ref)
     cols = pl.ds(pl.multiple_of(side * half, half), half)
-    x, y = x_ref[...], y_ref[:, cols]
+    y = y_ref[:, cols]
     bound = (jnp.sum(y * y, 0, keepdims=True) - g_ref[:, cols]) * C2 - log_n
-    a_ref[...] = first_side(x * (2 * C2), -total).T
     b_ref[...] = second_side(y, -bound)
-    v_ref[...] = coordinates(x)
     weighted(a_ref, b_ref, v_ref, t_refs, o_ref)
     mass = o_ref[2 * K : 2 * K + 1, :]
     l_ref[...] = jnp.log2(mass) + bound
@@ -241,7 +241,7 @@
         out_ref[d] = image
 
 
-def row_images(log_n, own, me_ref, x_ref, y_ref, total_ref, mine_ref, other_ref, after_ref, pot_ref, out_ref, a_ref, b_ref, v_ref, o_ref, l_ref, *t_refs):
+def row_sides(log_n, me_ref, y_ref, mine_ref, other_ref, pot_ref, a_ref, v_ref, l_ref):
     for part, ref in ((core_of(me_ref), mine_ref), (1 - core_of(me_ref), other_ref)):
         for q in range(ref.shape[0]):
             at = pl.ds(pl.multiple_of((part * ref.shape[0] + q) * LANES, LANES), LANES)
@@ -249,12 +249,20 @@
     logs = l_ref[...]
     y = y_ref[...]
     pot_ref[...] = jnp.sum(y * y, 0, keepdims=True) - LN * (logs + log_n)
+    a_ref[...] = first_side(y, -logs).T
+    v_ref[...] = coordinates(y)
+
+
+def row_images(log_n, own, me_ref, x_ref, total_ref, after_ref, *refs):
+    if own:
+        a_ref, v_ref, out_ref, b_ref, o_ref, *t_refs = refs
+    else:
+        y_ref, mine_ref, other_ref, pot_ref, out_ref, a_ref, v_ref, b_ref, o_ref, l_ref, *t_refs = refs
+        row_sides(log_n, me_ref, y_ref, mine_ref, other_ref, pot_ref, a_ref, v_ref, l_ref)
     half = o_ref.shape[1]
     side = side_of(me_ref) if own else 1 - side_of(me_ref)
     cols = pl.ds(pl.multiple_of(side * half, half), half)
-    a_ref[...] = first_side(y, -logs).T
     b_ref[...] = second_side(x_ref[:, cols] * (2 * C2), LIFT - total_ref[:, cols])
-    v_ref[...] = coordinates(y)
     weighted(a_ref, b_ref, v_ref, t_refs, o_ref)
     tiles = half // LANES
     for k in range(tiles):
@@ -276,7 +284,8 @@
             out_ref[at, :] = (one_ref[at, :] + two_ref[at, :]) / under
 
 
-def lay_rows(me_ref, mine_ref, other_ref, out_ref):
+def lay_rows(me_ref, mine_ref, other_ref, out_ref, token_ref):
+    token_ref[...] = mine_ref[0:8, :]
     half = out_ref.shape[1] // 2
     tiles = half // LANES
     for side, ref in ((side_of(me_ref), mine_ref), (1 - side_of(me_ref), other_ref)):
@@ -297,12 +306,13 @@
             out_ref[:, pl.ds(pl.multiple_of(side * half + q * LANES, LANES), LANES)] = ref[q]
 
 
-def call(kernel, ins, outs, scratch=(), copies=0, aliases={}, cost=None):
+def call(kernel, ins, outs, scratch=(), copies=0, aliases={}, cost=None, out="v"):
+    spaces = {"s": SM, "h": pl.BlockSpec(memory_space=pltpu.HBM), "v": VM}
     return pl.pallas_call(
         kernel,
-        out_shape=tuple(jax.ShapeDtypeStruct(shape, F32) for shape in outs),
-        in_specs=[{"s": SM, "h": pl.BlockSpec(memory_space=pltpu.HBM), "v": VM}[spec] for spec in ins],
-        out_specs=tuple(VM for _ in outs),
+        out_shape=tuple(jax.ShapeDtypeStruct(*(one if isinstance(one[0], tuple) else (one, F32))) for one in outs),
+        in_specs=[spaces[spec] for spec in ins],
+        out_specs=tuple(spaces[out] for _ in outs),
         scratch_shapes=[pltpu.VMEM(*one) for one in scratch] + [pltpu.SemaphoreType.DMA((copies,))] * (copies > 0),
         input_output_aliases=aliases,
         cost_estimate=cost,
@@ -334,48 +344,61 @@
 
         part, x, y, g = call(
             row_logs,
-            "hhh",
+            "shhh",
             [(n_tgt, rows, LANES), x.shape, y.shape, g.shape],
             [((nt, KD), BF), ((KD, ns), BF), ((1, ns), F32), BLOCK, BLOCK],
             3,
             cost=work(ns * nt, 0),
-        )(*(pltpu.with_memory_space_constraint(one, pltpu.HBM) for one in (x, y, g)))
+        )(me, *(pltpu.with_memory_space_constraint(one, pltpu.HBM) for one in (x, y, g)))
         part = lax.all_to_all(part, tgt, 0, 0, tiled=True)
 
-        sums = [((ns, KD), BF), ((KD, nt // 2), BF), ((80, ns), BF), ((80, nt // 2), F32), ((1, nt // 2), F32), BLOCK, BLOCK]
+        sums = [((KD, nt // 2), BF), ((80, nt // 2), F32), ((1, nt // 2), F32), BLOCK, BLOCK]
         log_n = math.log2(ns * n_src)
-        source_potential, total, send = call(
-            functools.partial(column_sums, log_n, True), "svvvv", [(1, ns), (1, ns), chunk], sums, cost=work(ns * nt // 2, 2)
+        source_potential, total, send, side, weights = call(
+            functools.partial(column_sums, log_n, True),
+            "svvvv",
+            [(1, ns), (1, ns), chunk, ((ns, KD), BF), ((80, ns), BF)],
+            sums,
+            cost=work(ns * nt // 2, 2),
         )(me, x, y, g, part)
         sent = lax.ppermute(send, "core", swap)
         (keep,) = call(
-            functools.partial(column_sums, log_n, False), "svvvv", [chunk], sums, cost=work(ns * nt // 2, 2)
-        )(me, x, y, g, total)
+            functools.partial(column_sums, log_n, False), "svvvvvv", [chunk], sums, cost=work(ns * nt // 2, 2)
+        )(me, x, y, g, total, side, weights)
         (part,) = call(merge_pair, "vv", [(pairs, K + pairs, LANES)])(keep, sent)
         image = lax.all_to_all(part, chips, 0, 0, tiled=True)
         (mine,) = call(merge_logs, "v", [(pairs, LANES)])(image)
         other = lax.ppermute(mine, "core", swap)
 
+        (image,) = call(merge_chunk, "svv", [(pairs, K, LANES)], cost=work(ns * nt // 2, 2))(me, image, mine)
+
         half = ns // 2
         tall = (K * half) // LANES
-        images = lambda own: call(
-            functools.partial(row_images, math.log2(nt * n_tgt), own),
-            "svvvvvv",
-            [(1, nt), (tall + 8, LANES)],
-            [((nt, KD), BF), ((KD, half), BF), ((80, nt), BF), ((80, half), F32), ((1, nt), F32), BLOCK, BLOCK],
+        sums = [((KD, half), BF), ((80, half), F32)]
+        log_n = math.log2(nt * n_tgt)
+        target_potential, sent, side, weights = call(
+            functools.partial(row_images, log_n, False),
+            "svvhvvv",
+            [(1, nt), (tall + 8, LANES), ((nt, KD), BF), ((80, nt), BF)],
+            [*sums, ((1, nt), F32), BLOCK, BLOCK],
             cost=work(half * nt, 2),
-        )
-        target_potential, sent = images(False)(me, x, y, total, mine, other, mine)
-        _, held = images(True)(me, x, y, total, mine, other, sent)
-        sent = lax.ppermute(sent, tgt, over)
-        held = held + sent
-        (image,) = call(merge_chunk, "svv", [(pairs, K, LANES)], cost=work(half * nt, 2))(me, image, held)
+        )(me, x, total, image, y, mine, other)
+        (held,) = call(
+            functools.partial(row_images, log_n, True),
+            "svvvvv",
+            [(tall + 8, LANES)],
+            [*sums, BLOCK, BLOCK],
+            cost=work(half * nt, 2),
+        )(me, x, total, sent, side, weights)
+        held = held + lax.ppermute(sent, tgt, over)
+        (image,) = call(hold, "hv", [image.shape], aliases={0: 0}, out="h")(image, held)
         image = lax.all_to_all(image, chips, 0, 0, tiled=True)
         held = held + lax.ppermute(held, tgt, near)
         (held,) = call(add_divide, "vv", [(tall, LANES)], cost=work(half * nt, 2))(held, lax.ppermute(held, tgt, far))
-        sent = lax.ppermute(held, tgt, over)
-        (source_image,) = call(lay_rows, "svv", [(K, ns)], cost=work(half * nt, 2))(me, held, sent)
-        (image,) = call(hold, "vv", [image.shape], aliases={0: 0})(image, sent)
+        source_image, token = call(lay_rows, "svv", [(K, ns), (8, LANES)])(
+            me, held, lax.ppermute(held, tgt, over)
+        )
+        (image,) = call(hold, "vv", [image.shape], aliases={0: 0})(image, token)
         (target_image,) = call(lay_columns, "svv", [(K, nt)])(me, image, lax.ppermute(image, "core", swap))
         return source_potential.reshape(ns), target_potential.reshape(nt), source_image, target_image
 

time: 87.8 us -> 85.8 us (0.977)
  blocking collectives: 24.9 us -> 36.2 us
  waiting for transfers between devices: 18.3 us -> 12.1 us
  starting transfers between devices: 13.7 us -> 7.6 us
  Pallas kernels: 28.9 us -> 27.6 us
    all_to_all x0 -> x1, blocking collectives: none -> 11.3 us  [shards(): part = lax.all_to_all(part, tgt, 0, 0, tiled=True)]
    all_to_all x1 -> x0, waiting for transfers between devices: 6.26 us -> none  [shards(): part = lax.all_to_all(part, tgt, 0, 0, tiled=True)]
    all_to_all x1 -> x0, starting transfers between devices: 5.31 us -> none  [shards(): part = lax.all_to_all(part, tgt, 0, 0, tiled=True)]
    ppermute x2, waiting for transfers between devices: 4.1 us -> 5.68 us  [the longest x1 4.19 us: shards(): lax.ppermute(held, tgt, over)]
    all_to_all x1, waiting for transfers between devices: 1.44 us -> 0.04 us  [shards(): image = lax.all_to_all(image, chips, 0, 0, tiled=True)]
    pallas_call x7 -> x8, Pallas kernels: 24.1 us -> 22.8 us  [the longest x1 11.4 us: shards(): call(row_logs, 'shhh', [(n_tgt, rows, LANES), x.shape, y.shape, g.shape],...]
  transfers between devices with their start and end apart: 9 -> 8, of which waited for: 7 -> 5; matrix products, arithmetic and copies ran while one was open for 0% -> 0% of each run, Pallas kernels for 10% -> 9%
where the time goes in v6:
time: 85.8 us; the launch traced here: 84.3 us
  blocking collectives  36.2 us (42%)
  Pallas kernels  27.6 us (32%)
  waiting for transfers between devices  12.1 us (14%)
  starting transfers between devices  7.6 us (9%)
    all_to_all x1, blocking collectives, shards(): image = lax.all_to_all(part, chips, 0, 0, tiled=True)  24.9 us
    pallas_call x1, Pallas kernels, shards(): call(row_logs, 'shhh', [(n_tgt, rows, LANES), x.shape, y.shape, g.shape],...  11.4 us
    all_to_all x1, blocking collectives, shards(): part = lax.all_to_all(part, tgt, 0, 0, tiled=True)  11.3 us
    all_to_all x1, starting transfers between devices, shards(): image = lax.all_to_all(image, chips, 0, 0, tiled=True)  5.43 us
    ppermute x1, waiting for transfers between devices, shards(): lax.ppermute(held, tgt, far)  4.43 us
    ppermute x1, waiting for transfers between devices, shards(): lax.ppermute(held, tgt, over)  4.19 us
    pallas_call x1, Pallas kernels, shards(): call(functools.partial(column_sums, log_n, True), 'svvvv', [(1, ns), (1,...  3.87 us
    pallas_call x1, Pallas kernels, shards(): call(functools.partial(row_images, log_n, False), 'svvhvvv', [(1, nt), (t...  3.66 us
  transfers between devices with their start and end apart: 8, of which 5 were waited for; matrix products, arithmetic and copies ran while one was open for 0% of the time, Pallas kernels for 9%

profile of v6, /device:TPU:32, one launch (start us, length us, event | category | flops | bytes accessed | tf_op | source)
XLA Modules:
  0.0 84.3 jit_solution(4812770673595716340)
XLA Ops:
  0.6 11.4 %shard_map.66 = (f32[8,8,128]{2,1,0:T(8,128)S(1)}, f32[32,1024]{1,0:T(8,128)S(1)}, f32[32,4096]{1,0:T(8,128)S(1)}, f32[1,4096]{1,0:T(1,128)S(1)}) custom-call(s32[1]{0:T(128)} %bitcast.me_ref, f32[32,1024]{1,0:T(8,128)} %x_hbm.1, f32[32,4096]{1,0:T(8,128)} %y_hbm.1, f32[1,4096]{1,0:T(1,128)} %bitcast.4), custom_call_target="tpu_custom_call" | custom-call | flops 2147483648 | bytes 33554432 | tf_op jit(solution)/shard_map/pallas_call | solution.py:345
  12.0 11.3 %all_to_all.15.from_ref = f32[8,8,128]{2,1,0:T(8,128)S(1)} all-to-all(f32[8,8,128]{2,1,0:T(8,128)S(1)} %get-tuple-element.22), channel_id=1, replica_groups=mesh['high'=2,'line'=8,'core'=2,'low'=2,'ring'=4] {'low','ring'}, dimensions={0} | all-to-all | bytes 65536 | tf_op jit(solution)/shard_map/all_to_all | solution.py:353
  23.4 3.9 %shard_map.67 = (f32[1,1024]{1,0:T(1,128)}, f32[1,1024]{1,0:T(1,128)S(1)}, f32[16,40,128]{2,1,0:T(8,128)S(1)}, bf16[1024,256]{1,0:T(8,128)(2,1)S(1)}, bf16[80,1024]{1,0:T(8,128)(2,1)S(1)}) custom-call(s32[1]{0:T(128)} %bitcast.me_ref, f32[32,1024]{1,0:T(8,128)S(1)} %get-tuple-element.19.x_ref, f32[32,4096]{1,0:T(8,128)S(1)} %get-tuple-element.20.y_ref.refs_0_, ...), custom_call_target="tpu_custom_call" | custom-call | flops 3221225472 | bytes 16777216 | tf_op jit(solution)/shard_map/pallas_call | solution.py:357
  27.3 0.0 collective-permute-start
  27.3 3.5 %shard_map.68.one_ref = f32[16,40,128]{2,1,0:T(8,128)S(1)} custom-call(s32[1]{0:T(128)} %bitcast.me_ref, f32[32,1024]{1,0:T(8,128)S(1)} %get-tuple-element.19.x_ref, f32[32,4096]{1,0:T(8,128)S(1)} %get-tuple-element.20.y_ref.refs_0_, f32[1,4096]{1,0:T(1,128)S(1)} %get-tuple-element.21.g_ref, f32[1,1024]{1,0:T(1,128)S(1)} %get-tuple-element.24.from_ref.total_ref, ...), custom_call_target="tpu_custom_call" | custom-call | flops 3221225472 | bytes 16777216 | tf_op jit(solution)/shard_map/pallas_call | solution.py:365
  30.7 0.0 collective-permute-done.two_ref
  30.8 0.1 shard_map.69
  30.8 24.9 %all_to_all.16.part_ref = f32[16,48,128]{2,1,0:T(8,128)S(1)} all-to-all(f32[16,48,128]{2,1,0:T(8,128)S(1)} %shard_map.69), channel_id=1, replica_groups=mesh['high'=2,'line'=8,'core'=2,'low'=2,'ring'=4] {'high','line'}, dimensions={0} | all-to-all | bytes 786432 | tf_op jit(solution)/shard_map/all_to_all | solution.py:369
  55.8 0.1 collective-permute-start.1
  55.9 0.8 shard_map.71.after_ref.image_ref
  56.7 0.4 collective-permute-done.1.refs_2_
  57.1 3.7 %shard_map.72 = (f32[1,4096]{1,0:T(1,128)}, f32[136,128]{1,0:T(8,128)S(1)}, bf16[4096,256]{1,0:T(8,128)(2,1)S(1)}, bf16[80,4096]{1,0:T(8,128)(2,1)S(1)}) custom-call(s32[1]{0:T(128)} %bitcast.me_ref, f32[32,1024]{1,0:T(8,128)S(1)} %get-tuple-element.19.x_ref, f32[1,1024]{1,0:T(1,128)S(1)} %get-tuple-element.24.from_ref.total_ref, ...), custom_call_target="tpu_custom_call" | custom-call | flops 3221225472 | bytes 16777216 | tf_op jit(solution)/shard_map/pallas_call | solution.py:379
  60.7 0.0 collective-permute-start.2
  60.7 2.8 %shard_map.73 = f32[136,128]{1,0:T(8,128)S(1)} custom-call(s32[1]{0:T(128)} %bitcast.me_ref, f32[32,1024]{1,0:T(8,128)S(1)} %get-tuple-element.19.x_ref, f32[1,1024]{1,0:T(1,128)S(1)} %get-tuple-element.24.from_ref.total_ref, f32[136,128]{1,0:T(8,128)S(1)} %get-tuple-element.29.after_ref, bf16[4096,256]{1,0:T(8,128)(2,1)S(1)} %get-tuple-element.30.refs_0_, ...), custom_call_target="tpu_custom_call" | custom-call | flops 3221225472 | bytes 16777216 | tf_op jit(solution)/shard_map/pallas_call | solution.py:386
  63.5 1.5 %collective-permute-done.2 = f32[136,128]{1,0:T(8,128)S(1)} collective-permute-done((f32[136,128]{1,0:T(8,128)S(1)}, f32[136,128]{1,0:T(8,128)S(1)}, u32[]{:S(2)}, u32[]{:S(2)}) %collective-permute-start.2) | collective-permute-done | bytes 69664 | tf_op jit(solution)/shard_map/ppermute | solution.py:393
  65.0 0.7 collective-permute-start.3
  65.8 5.4 %all-to-all-start.2 = ((f32[16,32,128]{2,1,0:T(8,128)}), f32[16,32,128]{2,1,0:T(8,128)S(1)}, u32[]{:S(2)}, u32[]{:S(2)}) async-start(f32[16,32,128]{2,1,0:T(8,128)} %shard_map.76), calls=%async_computation.2 | async-start | bytes 524288 | tf_op jit(solution)/shard_map/all_to_all | solution.py:395
  71.2 0.0 collective-permute-done.3
  71.2 1.2 %collective-permute-start.4 = (f32[136,128]{1,0:T(8,128)S(1)}, f32[136,128]{1,0:T(8,128)S(1)}, u32[]{:S(2)}, u32[]{:S(2)}) collective-permute-start(f32[136,128]{1,0:T(8,128)S(1)} %add.23.one_ref), channel_id=1, source_target_pairs={{0,3},{1,2},{2,1},{3,0},{4,7},{5,6},{6,5},{7,4},{8,11},{9,10},{10,... | collective-permute-start | bytes 208904 | tf_op jit(solution)/shard_map/ppermute | solution.py:397
  72.4 4.4 %collective-permute-done.4.two_ref = f32[136,128]{1,0:T(8,128)S(1)} collective-permute-done((f32[136,128]{1,0:T(8,128)S(1)}, f32[136,128]{1,0:T(8,128)S(1)}, u32[]{:S(2)}, u32[]{:S(2)}) %collective-permute-start.4) | collective-permute-done | bytes 69664 | tf_op jit(solution)/shard_map/ppermute | solution.py:397
  76.9 0.2 collective-permute-start.5
  77.0 4.2 %collective-permute-done.5.other_ref = f32[128,128]{1,0:T(8,128)S(1)} collective-permute-done((f32[128,128]{1,0:T(8,128)S(1)}, f32[128,128]{1,0:T(8,128)S(1)}, u32[]{:S(2)}, u32[]{:S(2)}) %collective-permute-start.5) | collective-permute-done | bytes 65568 | tf_op jit(solution)/shard_map/ppermute | solution.py:399
  81.2 0.7 shard_map.75
  81.9 0.0 all-to-all-done.2.image_ref
  81.9 0.0 collective-permute-start.6
  81.9 1.5 %collective-permute-done.6.other_ref = f32[16,32,128]{2,1,0:T(8,128)S(1)} collective-permute-done((f32[16,32,128]{2,1,0:T(8,128)S(1)}, f32[16,32,128]{2,1,0:T(8,128)S(1)}, u32[]{:S(2)}, u32[]{:S(2)}) %collective-permute-start.6) | collective-permute-done | bytes 262176 | tf_op jit(solution)/shard_map/ppermute | solution.py:402
  83.5 0.8 shard_map.78
  (6 shorter events, 0.1 us)
Async XLA Ops:
  27.3 3.5 %collective-permute-start = (f32[16,40,128]{2,1,0:T(8,128)S(1)}, f32[16,40,128]{2,1,0:T(8,128)S(1)}, u32[]{:S(2)}, u32[]{:S(2)}) collective-permute-start(f32[16,40,128]{2,1,0:T(8,128)S(1)} %get-tuple-element.27), channel_id=1, source_target_pairs={{0,8},{8,0},{1,9},{9,1},{2,10},{10,2},{3,11},{11,3},{4,12},{12,4},... | collective-permute-start | bytes 983048 | tf_op jit(solution)/shard_map/ppermute | solution.py:364
  55.8 1.3 %collective-permute-start.1 = (f32[16,128]{1,0:T(8,128)S(1)}, f32[16,128]{1,0:T(8,128)S(1)}, u32[]{:S(2)}, u32[]{:S(2)}) collective-permute-start(f32[16,128]{1,0:T(8,128)S(1)} %shard_map.70.after_ref.refs_1_), channel_id=1, source_target_pairs={{0,8},{8,0},{1,9},{9,1},{2,10},{10,2},{3,11},{11,3},{4,12},{12,4},... | collective-permute-start | bytes 24584 | tf_op jit(solution)/shard_map/ppermute | solution.py:371
  60.7 4.3 %collective-permute-start.2 = (f32[136,128]{1,0:T(8,128)S(1)}, f32[136,128]{1,0:T(8,128)S(1)}, u32[]{:S(2)}, u32[]{:S(2)}) collective-permute-start(f32[136,128]{1,0:T(8,128)S(1)} %get-tuple-element.29.after_ref), channel_id=1, source_target_pairs={{0,4},{1,5},{2,6},{3,7},{4,0},{5,1},{6,2},{7,3},{8,12},{9,13},{10,... | collective-permute-start | bytes 208904 | tf_op jit(solution)/shard_map/ppermute | solution.py:393
  65.0 6.2 %collective-permute-start.3 = (f32[136,128]{1,0:T(8,128)S(1)}, f32[136,128]{1,0:T(8,128)S(1)}, u32[]{:S(2)}, u32[]{:S(2)}) collective-permute-start(f32[136,128]{1,0:T(8,128)S(1)} %add.22.after_ref), channel_id=1, source_target_pairs={{0,1},{1,0},{2,3},{3,2},{4,5},{5,4},{6,7},{7,6},{8,9},{9,8},{10,11... | collective-permute-start | bytes 208904 | tf_op jit(solution)/shard_map/ppermute | solution.py:396
  65.8 16.1 %all-to-all-start.2 = ((f32[16,32,128]{2,1,0:T(8,128)}), f32[16,32,128]{2,1,0:T(8,128)S(1)}, u32[]{:S(2)}, u32[]{:S(2)}) async-start(f32[16,32,128]{2,1,0:T(8,128)} %shard_map.76), calls=%async_computation.2 | async-start | bytes 524288 | tf_op jit(solution)/shard_map/all_to_all | solution.py:395
  71.2 5.6 %collective-permute-start.4 = (f32[136,128]{1,0:T(8,128)S(1)}, f32[136,128]{1,0:T(8,128)S(1)}, u32[]{:S(2)}, u32[]{:S(2)}) collective-permute-start(f32[136,128]{1,0:T(8,128)S(1)} %add.23.one_ref), channel_id=1, source_target_pairs={{0,3},{1,2},{2,1},{3,0},{4,7},{5,6},{6,5},{7,4},{8,11},{9,10},{10,... | collective-permute-start | bytes 208904 | tf_op jit(solution)/shard_map/ppermute | solution.py:397
  76.9 4.4 %collective-permute-start.5 = (f32[128,128]{1,0:T(8,128)S(1)}, f32[128,128]{1,0:T(8,128)S(1)}, u32[]{:S(2)}, u32[]{:S(2)}) collective-permute-start(f32[128,128]{1,0:T(8,128)S(1)} %shard_map.74.mine_ref), channel_id=1, source_target_pairs={{0,4},{1,5},{2,6},{3,7},{4,0},{5,1},{6,2},{7,3},{8,12},{9,13},{10,... | collective-permute-start | bytes 196616 | tf_op jit(solution)/shard_map/ppermute | solution.py:399
  81.9 1.5 %collective-permute-start.6 = (f32[16,32,128]{2,1,0:T(8,128)S(1)}, f32[16,32,128]{2,1,0:T(8,128)S(1)}, u32[]{:S(2)}, u32[]{:S(2)}) collective-permute-start(f32[16,32,128]{2,1,0:T(8,128)S(1)} %shard_map.77.mine_ref), channel_id=1, source_target_pairs={{0,8},{8,0},{1,9},{9,1},{2,10},{10,2},{3,11},{11,3},{4,12},{12,4},... | collective-permute-start | bytes 786440 | tf_op jit(solution)/shard_map/ppermute | solution.py:402

commit v7 on v6

--- a/solution.py
+++ b/solution.py
@@ -157,10 +157,6 @@
 
 def core_of(me_ref):
     return me_ref[0] >> 3 & 1
-
-
-def side_of(me_ref):
-    return me_ref[0] >> 2 & 1
 
 
 def column_sums(log_n, first, me_ref, x_ref, y_ref, g_ref, from_ref, *refs):
@@ -241,7 +237,7 @@
         out_ref[d] = image
 
 
-def row_sides(log_n, me_ref, y_ref, mine_ref, other_ref, pot_ref, a_ref, v_ref, l_ref):
+def row_images(log_n, me_ref, x_ref, total_ref, after_ref, y_ref, mine_ref, other_ref, pot_ref, out_ref, a_ref, b_ref, v_ref, o_ref, l_ref, *t_refs):
     for part, ref in ((core_of(me_ref), mine_ref), (1 - core_of(me_ref), other_ref)):
         for q in range(ref.shape[0]):
             at = pl.ds(pl.multiple_of((part * ref.shape[0] + q) * LANES, LANES), LANES)
@@ -250,49 +246,29 @@
     y = y_ref[...]
     pot_ref[...] = jnp.sum(y * y, 0, keepdims=True) - LN * (logs + log_n)
     a_ref[...] = first_side(y, -logs).T
+    b_ref[...] = second_side(x_ref[...] * (2 * C2), LIFT - total_ref[...])
     v_ref[...] = coordinates(y)
-
-
-def row_images(log_n, own, me_ref, x_ref, total_ref, after_ref, *refs):
-    if own:
-        a_ref, v_ref, out_ref, b_ref, o_ref, *t_refs = refs
-    else:
-        y_ref, mine_ref, other_ref, pot_ref, out_ref, a_ref, v_ref, b_ref, o_ref, l_ref, *t_refs = refs
-        row_sides(log_n, me_ref, y_ref, mine_ref, other_ref, pot_ref, a_ref, v_ref, l_ref)
-    half = o_ref.shape[1]
-    side = side_of(me_ref) if own else 1 - side_of(me_ref)
-    cols = pl.ds(pl.multiple_of(side * half, half), half)
-    b_ref[...] = second_side(x_ref[:, cols] * (2 * C2), LIFT - total_ref[:, cols])
     weighted(a_ref, b_ref, v_ref, t_refs, o_ref)
-    tiles = half // LANES
+    tiles = o_ref.shape[1] // LANES
     for k in range(tiles):
         lanes = slice(k * LANES, (k + 1) * LANES)
         for r in range(0, K, 8):
             out_ref[r * tiles + 8 * k : r * tiles + 8 * k + 8, :] = o_ref[r : r + 8, lanes] + o_ref[K + r : K + r + 8, lanes]
         out_ref[K * tiles + k : K * tiles + k + 1, :] = o_ref[2 * K : 2 * K + 1, lanes]
-    out_ref[K * tiles + tiles :, :] = jnp.ones((out_ref.shape[0] - (K + 1) * tiles, LANES), F32)
+
+
+def add(one_ref, two_ref, out_ref):
+    out_ref[...] = one_ref[...] + two_ref[...]
 
 
 def add_divide(one_ref, two_ref, out_ref):
-    rows = out_ref.shape[0]
-    tiles = rows // K
-    mass = one_ref[rows : rows + 8, :] + two_ref[rows : rows + 8, :]
+    tiles = out_ref.shape[1] // LANES
+    mass = one_ref[K * tiles :, :] + two_ref[K * tiles :, :]
     for k in range(tiles):
         under = jnp.broadcast_to(mass[k : k + 1, :], (8, LANES))
         for r in range(0, K, 8):
             at = slice(r * tiles + 8 * k, r * tiles + 8 * k + 8)
-            out_ref[at, :] = (one_ref[at, :] + two_ref[at, :]) / under
-
-
-def lay_rows(me_ref, mine_ref, other_ref, out_ref, token_ref):
-    token_ref[...] = mine_ref[0:8, :]
-    half = out_ref.shape[1] // 2
-    tiles = half // LANES
-    for side, ref in ((side_of(me_ref), mine_ref), (1 - side_of(me_ref), other_ref)):
-        for k in range(tiles):
-            cols = pl.ds(pl.multiple_of(side * half + k * LANES, LANES), LANES)
-            for r in range(0, K, 8):
-                out_ref[r : r + 8, cols] = ref[r * tiles + 8 * k : r * tiles + 8 * k + 8, :]
+            out_ref[r : r + 8, k * LANES : (k + 1) * LANES] = (one_ref[at, :] + two_ref[at, :]) / under
 
 
 def hold(image_ref, after_ref, out_ref):
@@ -372,33 +348,23 @@
 
         (image,) = call(merge_chunk, "svv", [(pairs, K, LANES)], cost=work(ns * nt // 2, 2))(me, image, mine)
 
-        half = ns // 2
-        tall = (K * half) // LANES
-        sums = [((KD, half), BF), ((80, half), F32)]
-        log_n = math.log2(nt * n_tgt)
-        target_potential, sent, side, weights = call(
-            functools.partial(row_images, log_n, False),
+        tall = (K * ns) // LANES
+        target_potential, held = call(
+            functools.partial(row_images, math.log2(nt * n_tgt)),
             "svvhvvv",
-            [(1, nt), (tall + 8, LANES), ((nt, KD), BF), ((80, nt), BF)],
-            [*sums, ((1, nt), F32), BLOCK, BLOCK],
-            cost=work(half * nt, 2),
+            [(1, nt), (tall + rows, LANES)],
+            [((nt, KD), BF), ((KD, ns), BF), ((80, nt), BF), ((80, ns), F32), ((1, nt), F32), BLOCK, BLOCK],
+            cost=work(ns * nt, 2),
         )(me, x, total, image, y, mine, other)
-        (held,) = call(
-            functools.partial(row_images, log_n, True),
-            "svvvvv",
-            [(tall + 8, LANES)],
-            [*sums, BLOCK, BLOCK],
-            cost=work(half * nt, 2),
-        )(me, x, total, sent, side, weights)
-        held = held + lax.ppermute(sent, tgt, over)
         (image,) = call(hold, "hv", [image.shape], aliases={0: 0}, out="h")(image, held)
         image = lax.all_to_all(image, chips, 0, 0, tiled=True)
-        held = held + lax.ppermute(held, tgt, near)
-        (held,) = call(add_divide, "vv", [(tall, LANES)], cost=work(half * nt, 2))(held, lax.ppermute(held, tgt, far))
-        source_image, token = call(lay_rows, "svv", [(K, ns), (8, LANES)])(
-            me, held, lax.ppermute(held, tgt, over)
+        sizes = [held.shape]
+        (held,) = call(add, "vv", sizes, cost=work(ns * nt // 4, 2))(held, lax.ppermute(held, tgt, over))
+        (held,) = call(add, "vv", sizes, cost=work(ns * nt // 4, 2))(held, lax.ppermute(held, tgt, near))
+        (source_image,) = call(add_divide, "vv", [(K, ns)], cost=work(ns * nt // 4, 2))(
+            held, lax.ppermute(held, tgt, far)
         )
-        (image,) = call(hold, "vv", [image.shape], aliases={0: 0})(image, token)
+        (image,) = call(hold, "vv", [image.shape], aliases={0: 0})(image, held)
         (target_image,) = call(lay_columns, "svv", [(K, nt)])(me, image, lax.ppermute(image, "core", swap))
         return source_potential.reshape(ns), target_potential.reshape(nt), source_image, target_image
 

time: 85.8 us -> 84.9 us (0.990)
  waiting for transfers between devices: 12.1 us -> 10.7 us
    all_to_all x1, waiting for transfers between devices: 0.04 us -> 5.12 us  [shards(): image = lax.all_to_all(image, chips, 0, 0, tiled=True)]
    ppermute x1, waiting for transfers between devices: 4.43 us -> 0.01 us  [shards(): lax.ppermute(held, tgt, far)]
    ppermute x1, waiting for transfers between devices: 4.19 us -> 0.01 us  [shards(): lax.ppermute(held, tgt, over)]
    ppermute x2 -> x1, waiting for transfers between devices: 1.49 us -> 4.37 us  [shards(): lax.ppermute(held, tgt, near)]
  transfers between devices with their start and end apart: 8 -> 7, of which waited for: 5 -> 4; matrix products, arithmetic and copies ran while one was open for 0% -> 0% of each run, Pallas kernels for 9% -> 6%
where the time goes in v7:
time: 84.9 us; the launch traced here: 83.4 us
  blocking collectives  36.3 us (43%)
  Pallas kernels  27.5 us (32%)
  waiting for transfers between devices  10.7 us (13%)
  starting transfers between devices  8.16 us (10%)
    all_to_all x1, blocking collectives, shards(): image = lax.all_to_all(part, chips, 0, 0, tiled=True)  24.9 us
    all_to_all x1, blocking collectives, shards(): part = lax.all_to_all(part, tgt, 0, 0, tiled=True)  11.4 us
    pallas_call x1, Pallas kernels, shards(): call(row_logs, 'shhh', [(n_tgt, rows, LANES), x.shape, y.shape, g.shape],...  11.4 us
    pallas_call x1, Pallas kernels, shards(): call(functools.partial(row_images, math.log2(nt * n_tgt)), 'svvhvvv', [(1...  6.31 us
    all_to_all x1, starting transfers between devices, shards(): image = lax.all_to_all(image, chips, 0, 0, tiled=True)  6.01 us
    all_to_all x1, waiting for transfers between devices, shards(): image = lax.all_to_all(image, chips, 0, 0, tiled=True)  5.12 us
    ppermute x1, waiting for transfers between devices, shards(): lax.ppermute(held, tgt, near)  4.37 us
    pallas_call x1, Pallas kernels, shards(): call(functools.partial(column_sums, log_n, True), 'svvvv', [(1, ns), (1,...  3.86 us
  transfers between devices with their start and end apart: 7, of which 4 were waited for; matrix products, arithmetic and copies ran while one was open for 0% of the time, Pallas kernels for 6%

profile of v7, /device:TPU:32, one launch (start us, length us, event | category | flops | bytes accessed | tf_op | source)
XLA Modules:
  0.0 83.4 jit_solution(1486117443628991575)
XLA Ops:
  0.6 11.4 %shard_map.66 = (f32[8,8,128]{2,1,0:T(8,128)S(1)}, f32[32,1024]{1,0:T(8,128)S(1)}, f32[32,4096]{1,0:T(8,128)S(1)}, f32[1,4096]{1,0:T(1,128)S(1)}) custom-call(s32[1]{0:T(128)} %bitcast.me_ref, f32[32,1024]{1,0:T(8,128)} %x_hbm.1, f32[32,4096]{1,0:T(8,128)} %y_hbm.1, f32[1,4096]{1,0:T(1,128)} %bitcast.4), custom_call_target="tpu_custom_call" | custom-call | flops 2147483648 | bytes 33554432 | tf_op jit(solution)/shard_map/pallas_call | solution.py:321
  12.0 11.4 %all_to_all.15.from_ref = f32[8,8,128]{2,1,0:T(8,128)S(1)} all-to-all(f32[8,8,128]{2,1,0:T(8,128)S(1)} %get-tuple-element.18), channel_id=1, replica_groups=mesh['high'=2,'line'=8,'core'=2,'low'=2,'ring'=4] {'low','ring'}, dimensions={0} | all-to-all | bytes 65536 | tf_op jit(solution)/shard_map/all_to_all | solution.py:329
  23.4 3.9 %shard_map.67 = (f32[1,1024]{1,0:T(1,128)}, f32[1,1024]{1,0:T(1,128)S(1)}, f32[16,40,128]{2,1,0:T(8,128)S(1)}, bf16[1024,256]{1,0:T(8,128)(2,1)S(1)}, bf16[80,1024]{1,0:T(8,128)(2,1)S(1)}) custom-call(s32[1]{0:T(128)} %bitcast.me_ref, f32[32,1024]{1,0:T(8,128)S(1)} %get-tuple-element.15.x_ref, f32[32,4096]{1,0:T(8,128)S(1)} %get-tuple-element.16.y_ref, ...), custom_call_target="tpu_custom_call" | custom-call | flops 3221225472 | bytes 16777216 | tf_op jit(solution)/shard_map/pallas_call | solution.py:333
  27.3 0.0 collective-permute-start
  27.3 3.5 %shard_map.68.one_ref = f32[16,40,128]{2,1,0:T(8,128)S(1)} custom-call(s32[1]{0:T(128)} %bitcast.me_ref, f32[32,1024]{1,0:T(8,128)S(1)} %get-tuple-element.15.x_ref, f32[32,4096]{1,0:T(8,128)S(1)} %get-tuple-element.16.y_ref, f32[1,4096]{1,0:T(1,128)S(1)} %get-tuple-element.17.g_ref, f32[1,1024]{1,0:T(1,128)S(1)} %get-tuple-element.20.from_ref.total_ref, ...), custom_call_target="tpu_custom_call" | custom-call | flops 3221225472 | bytes 16777216 | tf_op jit(solution)/shard_map/pallas_call | solution.py:341
  30.8 0.0 collective-permute-done.two_ref
  30.8 0.1 shard_map.69
  30.9 24.9 %all_to_all.16.part_ref = f32[16,48,128]{2,1,0:T(8,128)S(1)} all-to-all(f32[16,48,128]{2,1,0:T(8,128)S(1)} %shard_map.69), channel_id=1, replica_groups=mesh['high'=2,'line'=8,'core'=2,'low'=2,'ring'=4] {'high','line'}, dimensions={0} | all-to-all | bytes 786432 | tf_op jit(solution)/shard_map/all_to_all | solution.py:345
  55.8 0.1 collective-permute-start.1
  55.9 0.8 shard_map.71.after_ref.image_ref
  56.7 0.4 collective-permute-done.1.other_ref
  57.1 6.3 %shard_map.72 = (f32[1,4096]{1,0:T(1,128)}, f32[264,128]{1,0:T(8,128)S(1)}) custom-call(s32[1]{0:T(128)} %bitcast.me_ref, f32[32,1024]{1,0:T(8,128)S(1)} %get-tuple-element.15.x_ref, f32[1,1024]{1,0:T(1,128)S(1)} %get-tuple-element.20.from_ref.total_ref, f32[16,32,128]{2,1,0:T(8,128)} %shard_map.71.after_ref.image_ref, ...), custom_call_target="tpu_custom_call" | custom-call | flops 6442450944 | bytes 33554432 | tf_op jit(solution)/shard_map/pallas_call | solution.py:352
  63.4 0.0 collective-permute-start.2
  63.4 6.0 %all-to-all-start.2 = ((f32[16,32,128]{2,1,0:T(8,128)}), f32[16,32,128]{2,1,0:T(8,128)S(1)}, u32[]{:S(2)}, u32[]{:S(2)}) async-start(f32[16,32,128]{2,1,0:T(8,128)} %shard_map.76), calls=%async_computation.2 | async-start | bytes 524288 | tf_op jit(solution)/shard_map/all_to_all | solution.py:360
  69.4 0.0 collective-permute-done.2.two_ref
  69.4 0.7 collective-permute-start.3
  70.2 4.4 %collective-permute-done.3.two_ref = f32[264,128]{1,0:T(8,128)S(1)} collective-permute-done((f32[264,128]{1,0:T(8,128)S(1)}, f32[264,128]{1,0:T(8,128)S(1)}, u32[]{:S(2)}, u32[]{:S(2)}) %collective-permute-start.3) | collective-permute-done | bytes 135200 | tf_op jit(solution)/shard_map/ppermute | solution.py:363
  74.6 1.3 %collective-permute-start.4 = (f32[264,128]{1,0:T(8,128)S(1)}, f32[264,128]{1,0:T(8,128)S(1)}, u32[]{:S(2)}, u32[]{:S(2)}) collective-permute-start(f32[264,128]{1,0:T(8,128)S(1)} %shard_map.74.one_ref.after_ref), channel_id=1, source_target_pairs={{0,3},{1,2},{2,1},{3,0},{4,7},{5,6},{6,5},{7,4},{8,11},{9,10},{10,... | collective-permute-start | bytes 405512 | tf_op jit(solution)/shard_map/ppermute | solution.py:365
  75.9 5.1 %all-to-all-done.2.image_ref = f32[16,32,128]{2,1,0:T(8,128)S(1)} async-done(((f32[16,32,128]{2,1,0:T(8,128)}), f32[16,32,128]{2,1,0:T(8,128)S(1)}, u32[]{:S(2)}, u32[]{:S(2)}) %all-to-all-start.2) | async-done | bytes 262176 | tf_op jit(solution)/shard_map/all_to_all | solution.py:360
  81.0 0.0 collective-permute-start.5
  81.0 0.0 collective-permute-done.4.two_ref
  81.0 0.7 shard_map.75
  81.7 0.8 %collective-permute-done.5.other_ref = f32[16,32,128]{2,1,0:T(8,128)S(1)} collective-permute-done((f32[16,32,128]{2,1,0:T(8,128)S(1)}, f32[16,32,128]{2,1,0:T(8,128)S(1)}, u32[]{:S(2)}, u32[]{:S(2)}) %collective-permute-start.5) | collective-permute-done | bytes 262176 | tf_op jit(solution)/shard_map/ppermute | solution.py:368
  82.5 0.8 shard_map.78
  (5 shorter events, 0.1 us)
Async XLA Ops:
  27.3 3.5 %collective-permute-start = (f32[16,40,128]{2,1,0:T(8,128)S(1)}, f32[16,40,128]{2,1,0:T(8,128)S(1)}, u32[]{:S(2)}, u32[]{:S(2)}) collective-permute-start(f32[16,40,128]{2,1,0:T(8,128)S(1)} %get-tuple-element.23), channel_id=1, source_target_pairs={{0,8},{8,0},{1,9},{9,1},{2,10},{10,2},{3,11},{11,3},{4,12},{12,4},... | collective-permute-start | bytes 983048 | tf_op jit(solution)/shard_map/ppermute | solution.py:340
  55.8 1.3 %collective-permute-start.1 = (f32[16,128]{1,0:T(8,128)S(1)}, f32[16,128]{1,0:T(8,128)S(1)}, u32[]{:S(2)}, u32[]{:S(2)}) collective-permute-start(f32[16,128]{1,0:T(8,128)S(1)} %shard_map.70.after_ref.mine_ref), channel_id=1, source_target_pairs={{0,8},{8,0},{1,9},{9,1},{2,10},{10,2},{3,11},{11,3},{4,12},{12,4},... | collective-permute-start | bytes 24584 | tf_op jit(solution)/shard_map/ppermute | solution.py:347
  63.4 6.0 %collective-permute-start.2 = (f32[264,128]{1,0:T(8,128)S(1)}, f32[264,128]{1,0:T(8,128)S(1)}, u32[]{:S(2)}, u32[]{:S(2)}) collective-permute-start(f32[264,128]{1,0:T(8,128)S(1)} %get-tuple-element.25.one_ref.after_ref), channel_id=1, source_target_pairs={{0,4},{1,5},{2,6},{3,7},{4,0},{5,1},{6,2},{7,3},{8,12},{9,13},{10,... | collective-permute-start | bytes 405512 | tf_op jit(solution)/shard_map/ppermute | solution.py:362
  63.4 17.6 %all-to-all-start.2 = ((f32[16,32,128]{2,1,0:T(8,128)}), f32[16,32,128]{2,1,0:T(8,128)S(1)}, u32[]{:S(2)}, u32[]{:S(2)}) async-start(f32[16,32,128]{2,1,0:T(8,128)} %shard_map.76), calls=%async_computation.2 | async-start | bytes 524288 | tf_op jit(solution)/shard_map/all_to_all | solution.py:360
  69.4 5.1 %collective-permute-start.3 = (f32[264,128]{1,0:T(8,128)S(1)}, f32[264,128]{1,0:T(8,128)S(1)}, u32[]{:S(2)}, u32[]{:S(2)}) collective-permute-start(f32[264,128]{1,0:T(8,128)S(1)} %shard_map.73.one_ref), channel_id=1, source_target_pairs={{0,1},{1,0},{2,3},{3,2},{4,5},{5,4},{6,7},{7,6},{8,9},{9,8},{10,11... | collective-permute-start | bytes 405512 | tf_op jit(solution)/shard_map/ppermute | solution.py:363
  74.6 6.5 %collective-permute-start.4 = (f32[264,128]{1,0:T(8,128)S(1)}, f32[264,128]{1,0:T(8,128)S(1)}, u32[]{:S(2)}, u32[]{:S(2)}) collective-permute-start(f32[264,128]{1,0:T(8,128)S(1)} %shard_map.74.one_ref.after_ref), channel_id=1, source_target_pairs={{0,3},{1,2},{2,1},{3,0},{4,7},{5,6},{6,5},{7,4},{8,11},{9,10},{10,... | collective-permute-start | bytes 405512 | tf_op jit(solution)/shard_map/ppermute | solution.py:365
  81.0 1.5 %collective-permute-start.5 = (f32[16,32,128]{2,1,0:T(8,128)S(1)}, f32[16,32,128]{2,1,0:T(8,128)S(1)}, u32[]{:S(2)}, u32[]{:S(2)}) collective-permute-start(f32[16,32,128]{2,1,0:T(8,128)S(1)} %shard_map.77.mine_ref), channel_id=1, source_target_pairs={{0,8},{8,0},{1,9},{9,1},{2,10},{10,2},{3,11},{11,3},{4,12},{12,4},... | collective-permute-start | bytes 786440 | tf_op jit(solution)/shard_map/ppermute | solution.py:368

commit v8 on v7

--- a/solution.py
+++ b/solution.py
@@ -21,7 +21,7 @@
 VM = pl.BlockSpec(memory_space=pltpu.VMEM)
 SM = pl.BlockSpec(memory_space=pltpu.SMEM)
 LANES = 128
-TALL, WIDE = 1024, 512
+TALL, WIDE = 1024, 256
 BLOCK = ((TALL, WIDE), F32)
 
 
@@ -186,15 +186,17 @@
     @pl.when(jnp.min(mass) < LEAST)
     def _():
         t_ref = t_refs[0]
-        wide = t_ref.shape[1]
+        tall, wide = t_ref.shape
         exact_logs(a_ref, b_ref, t_ref, l_ref)
         l_ref[...] += bound
         b_ref[6 * K : KD, :] = offsets(-l_ref[...], False)
 
         def column(c, _):
             at = pl.ds(pl.multiple_of(c * wide, wide), wide)
-            t_ref[...] = jnp.dot(a_ref[...], b_ref[:, at], preferred_element_type=F32)
-            o_ref[:, at] = by_coordinates(v_ref[...], jnp.exp2(t_ref[...]))
+            for r in range(0, a_ref.shape[0], tall):
+                t_ref[...] = jnp.dot(a_ref[r : r + tall, :], b_ref[:, at], preferred_element_type=F32)
+                part = by_coordinates(v_ref[:, r : r + tall], jnp.exp2(t_ref[...]))
+                o_ref[:, at] = part if r == 0 else o_ref[:, at] + part
             return 0
 
         lax.fori_loop(0, half // wide, column, 0)

time: 84.9 us -> 88 us (1.037)
  Pallas kernels: 27.5 us -> 30.5 us
    pallas_call x1, Pallas kernels: 11.4 us -> 15.4 us  [shards(): call(row_logs, 'shhh', [(n_tgt, rows, LANES), x.shape, y.shape, g.shape],...]
  transfers between devices with their start and end apart: 7 -> 7, of which waited for: 4 -> 4; matrix products, arithmetic and copies ran while one was open for 0% -> 0% of each run, Pallas kernels for 6% -> 5%
where the time goes in v8:
time: 88 us; the launch traced here: 86.5 us
  blocking collectives  36.3 us (41%)
  Pallas kernels  30.5 us (35%)
  waiting for transfers between devices  10.7 us (12%)
  starting transfers between devices  8.34 us (9%)
    all_to_all x1, blocking collectives, shards(): image = lax.all_to_all(part, chips, 0, 0, tiled=True)  24.9 us
    pallas_call x1, Pallas kernels, shards(): call(row_logs, 'shhh', [(n_tgt, rows, LANES), x.shape, y.shape, g.shape],...  15.4 us
    all_to_all x1, blocking collectives, shards(): part = lax.all_to_all(part, tgt, 0, 0, tiled=True)  11.4 us
    pallas_call x1, Pallas kernels, shards(): call(functools.partial(row_images, math.log2(nt * n_tgt)), 'svvhvvv', [(1...  6.08 us
    all_to_all x1, starting transfers between devices, shards(): image = lax.all_to_all(image, chips, 0, 0, tiled=True)  5.99 us
    all_to_all x1, waiting for transfers between devices, shards(): image = lax.all_to_all(image, chips, 0, 0, tiled=True)  5.11 us
    ppermute x1, waiting for transfers between devices, shards(): lax.ppermute(held, tgt, near)  4.37 us
    pallas_call x1, Pallas kernels, shards(): call(functools.partial(column_sums, log_n, True), 'svvvv', [(1, ns), (1,...  3.57 us
  transfers between devices with their start and end apart: 7, of which 4 were waited for; matrix products, arithmetic and copies ran while one was open for 0% of the time, Pallas kernels for 5%

profile of v8, /device:TPU:32, one launch (start us, length us, event | category | flops | bytes accessed | tf_op | source)
XLA Modules:
  0.0 86.5 jit_solution(16410497936289527490)
XLA Ops:
  0.6 15.4 %shard_map.66 = (f32[8,8,128]{2,1,0:T(8,128)S(1)}, f32[32,1024]{1,0:T(8,128)S(1)}, f32[32,4096]{1,0:T(8,128)S(1)}, f32[1,4096]{1,0:T(1,128)S(1)}) custom-call(s32[1]{0:T(128)} %bitcast.me_ref, f32[32,1024]{1,0:T(8,128)} %x_hbm.1, f32[32,4096]{1,0:T(8,128)} %y_hbm.1, f32[1,4096]{1,0:T(1,128)} %bitcast.4), custom_call_target="tpu_custom_call" | custom-call | flops 2147483648 | bytes 33554432 | tf_op jit(solution)/shard_map/pallas_call | solution.py:323
  16.1 11.4 %all_to_all.15.from_ref = f32[8,8,128]{2,1,0:T(8,128)S(1)} all-to-all(f32[8,8,128]{2,1,0:T(8,128)S(1)} %get-tuple-element.18), channel_id=1, replica_groups=mesh['high'=2,'line'=8,'core'=2,'low'=2,'ring'=4] {'low','ring'}, dimensions={0} | all-to-all | bytes 65536 | tf_op jit(solution)/shard_map/all_to_all | solution.py:331
  27.5 3.6 %shard_map.67 = (f32[1,1024]{1,0:T(1,128)}, f32[1,1024]{1,0:T(1,128)S(1)}, f32[16,40,128]{2,1,0:T(8,128)S(1)}, bf16[1024,256]{1,0:T(8,128)(2,1)S(1)}, bf16[80,1024]{1,0:T(8,128)(2,1)S(1)}) custom-call(s32[1]{0:T(128)} %bitcast.me_ref, f32[32,1024]{1,0:T(8,128)S(1)} %get-tuple-element.15.x_ref, f32[32,4096]{1,0:T(8,128)S(1)} %get-tuple-element.16.y_ref, ...), custom_call_target="tpu_custom_call" | custom-call | flops 3221225472 | bytes 16777216 | tf_op jit(solution)/shard_map/pallas_call | solution.py:335
  31.0 0.0 collective-permute-start
  31.0 2.9 %shard_map.68.one_ref = f32[16,40,128]{2,1,0:T(8,128)S(1)} custom-call(s32[1]{0:T(128)} %bitcast.me_ref, f32[32,1024]{1,0:T(8,128)S(1)} %get-tuple-element.15.x_ref, f32[32,4096]{1,0:T(8,128)S(1)} %get-tuple-element.16.y_ref, f32[1,4096]{1,0:T(1,128)S(1)} %get-tuple-element.17.g_ref, f32[1,1024]{1,0:T(1,128)S(1)} %get-tuple-element.20.from_ref.total_ref, ...), custom_call_target="tpu_custom_call" | custom-call | flops 3221225472 | bytes 16777216 | tf_op jit(solution)/shard_map/pallas_call | solution.py:343
  34.0 0.0 collective-permute-done.two_ref
  34.0 0.1 shard_map.69
  34.1 24.9 %all_to_all.16.part_ref = f32[16,48,128]{2,1,0:T(8,128)S(1)} all-to-all(f32[16,48,128]{2,1,0:T(8,128)S(1)} %shard_map.69), channel_id=1, replica_groups=mesh['high'=2,'line'=8,'core'=2,'low'=2,'ring'=4] {'high','line'}, dimensions={0} | all-to-all | bytes 786432 | tf_op jit(solution)/shard_map/all_to_all | solution.py:347
  59.0 0.3 collective-permute-start.1
  59.3 0.8 shard_map.71.after_ref.image_ref
  60.1 0.4 collective-permute-done.1.other_ref
  60.5 6.1 %shard_map.72 = (f32[1,4096]{1,0:T(1,128)}, f32[264,128]{1,0:T(8,128)S(1)}) custom-call(s32[1]{0:T(128)} %bitcast.me_ref, f32[32,1024]{1,0:T(8,128)S(1)} %get-tuple-element.15.x_ref, f32[1,1024]{1,0:T(1,128)S(1)} %get-tuple-element.20.from_ref.total_ref, f32[16,32,128]{2,1,0:T(8,128)} %shard_map.71.after_ref.image_ref, ...), custom_call_target="tpu_custom_call" | custom-call | flops 6442450944 | bytes 33554432 | tf_op jit(solution)/shard_map/pallas_call | solution.py:354
  66.5 0.0 collective-permute-start.2
  66.5 6.0 %all-to-all-start.2 = ((f32[16,32,128]{2,1,0:T(8,128)}), f32[16,32,128]{2,1,0:T(8,128)S(1)}, u32[]{:S(2)}, u32[]{:S(2)}) async-start(f32[16,32,128]{2,1,0:T(8,128)} %shard_map.76), calls=%async_computation.2 | async-start | bytes 524288 | tf_op jit(solution)/shard_map/all_to_all | solution.py:362
  72.5 0.0 collective-permute-done.2.two_ref
  72.6 0.7 collective-permute-start.3
  73.3 4.4 %collective-permute-done.3.two_ref = f32[264,128]{1,0:T(8,128)S(1)} collective-permute-done((f32[264,128]{1,0:T(8,128)S(1)}, f32[264,128]{1,0:T(8,128)S(1)}, u32[]{:S(2)}, u32[]{:S(2)}) %collective-permute-start.3) | collective-permute-done | bytes 135200 | tf_op jit(solution)/shard_map/ppermute | solution.py:365
  77.7 1.3 %collective-permute-start.4 = (f32[264,128]{1,0:T(8,128)S(1)}, f32[264,128]{1,0:T(8,128)S(1)}, u32[]{:S(2)}, u32[]{:S(2)}) collective-permute-start(f32[264,128]{1,0:T(8,128)S(1)} %shard_map.74.one_ref.after_ref), channel_id=1, source_target_pairs={{0,3},{1,2},{2,1},{3,0},{4,7},{5,6},{6,5},{7,4},{8,11},{9,10},{10,... | collective-permute-start | bytes 405512 | tf_op jit(solution)/shard_map/ppermute | solution.py:367
  79.0 5.1 %all-to-all-done.2.image_ref = f32[16,32,128]{2,1,0:T(8,128)S(1)} async-done(((f32[16,32,128]{2,1,0:T(8,128)}), f32[16,32,128]{2,1,0:T(8,128)S(1)}, u32[]{:S(2)}, u32[]{:S(2)}) %all-to-all-start.2) | async-done | bytes 262176 | tf_op jit(solution)/shard_map/all_to_all | solution.py:362
  84.1 0.0 collective-permute-start.5
  84.1 0.0 collective-permute-done.4.two_ref
  84.1 0.7 shard_map.75
  84.8 0.8 collective-permute-done.5.other_ref
  85.7 0.8 shard_map.78
  (5 shorter events, 0.1 us)
Async XLA Ops:
  31.0 2.9 %collective-permute-start = (f32[16,40,128]{2,1,0:T(8,128)S(1)}, f32[16,40,128]{2,1,0:T(8,128)S(1)}, u32[]{:S(2)}, u32[]{:S(2)}) collective-permute-start(f32[16,40,128]{2,1,0:T(8,128)S(1)} %get-tuple-element.23), channel_id=1, source_target_pairs={{0,8},{8,0},{1,9},{9,1},{2,10},{10,2},{3,11},{11,3},{4,12},{12,4},... | collective-permute-start | bytes 983048 | tf_op jit(solution)/shard_map/ppermute | solution.py:342
  59.0 1.4 %collective-permute-start.1 = (f32[16,128]{1,0:T(8,128)S(1)}, f32[16,128]{1,0:T(8,128)S(1)}, u32[]{:S(2)}, u32[]{:S(2)}) collective-permute-start(f32[16,128]{1,0:T(8,128)S(1)} %shard_map.70.after_ref.mine_ref), channel_id=1, source_target_pairs={{0,8},{8,0},{1,9},{9,1},{2,10},{10,2},{3,11},{11,3},{4,12},{12,4},... | collective-permute-start | bytes 24584 | tf_op jit(solution)/shard_map/ppermute | solution.py:349
  66.5 6.0 %collective-permute-start.2 = (f32[264,128]{1,0:T(8,128)S(1)}, f32[264,128]{1,0:T(8,128)S(1)}, u32[]{:S(2)}, u32[]{:S(2)}) collective-permute-start(f32[264,128]{1,0:T(8,128)S(1)} %get-tuple-element.25.one_ref.after_ref), channel_id=1, source_target_pairs={{0,4},{1,5},{2,6},{3,7},{4,0},{5,1},{6,2},{7,3},{8,12},{9,13},{10,... | collective-permute-start | bytes 405512 | tf_op jit(solution)/shard_map/ppermute | solution.py:364
  66.5 17.6 %all-to-all-start.2 = ((f32[16,32,128]{2,1,0:T(8,128)}), f32[16,32,128]{2,1,0:T(8,128)S(1)}, u32[]{:S(2)}, u32[]{:S(2)}) async-start(f32[16,32,128]{2,1,0:T(8,128)} %shard_map.76), calls=%async_computation.2 | async-start | bytes 524288 | tf_op jit(solution)/shard_map/all_to_all | solution.py:362
  72.6 5.1 %collective-permute-start.3 = (f32[264,128]{1,0:T(8,128)S(1)}, f32[264,128]{1,0:T(8,128)S(1)}, u32[]{:S(2)}, u32[]{:S(2)}) collective-permute-start(f32[264,128]{1,0:T(8,128)S(1)} %shard_map.73.one_ref), channel_id=1, source_target_pairs={{0,1},{1,0},{2,3},{3,2},{4,5},{5,4},{6,7},{7,6},{8,9},{9,8},{10,11... | collective-permute-start | bytes 405512 | tf_op jit(solution)/shard_map/ppermute | solution.py:365
  77.7 6.5 %collective-permute-start.4 = (f32[264,128]{1,0:T(8,128)S(1)}, f32[264,128]{1,0:T(8,128)S(1)}, u32[]{:S(2)}, u32[]{:S(2)}) collective-permute-start(f32[264,128]{1,0:T(8,128)S(1)} %shard_map.74.one_ref.after_ref), channel_id=1, source_target_pairs={{0,3},{1,2},{2,1},{3,0},{4,7},{5,6},{6,5},{7,4},{8,11},{9,10},{10,... | collective-permute-start | bytes 405512 | tf_op jit(solution)/shard_map/ppermute | solution.py:367
  84.1 1.5 %collective-permute-start.5 = (f32[16,32,128]{2,1,0:T(8,128)S(1)}, f32[16,32,128]{2,1,0:T(8,128)S(1)}, u32[]{:S(2)}, u32[]{:S(2)}) collective-permute-start(f32[16,32,128]{2,1,0:T(8,128)S(1)} %shard_map.77.mine_ref), channel_id=1, source_target_pairs={{0,8},{8,0},{1,9},{9,1},{2,10},{10,2},{3,11},{11,3},{4,12},{12,4},... | collective-permute-start | bytes 786440 | tf_op jit(solution)/shard_map/ppermute | solution.py:370

commit v9 on v8

--- a/solution.py
+++ b/solution.py
@@ -106,18 +106,12 @@
     lax.fori_loop(0, b_ref.shape[1] // wide, column, 0)
 
 
-def log_sums(a_ref, b_ref, t_refs, l_ref):
+def plain_sums(a_ref, b_ref, t_refs, l_ref):
     def use(t_ref, rows, cols):
         part = jnp.sum(jnp.exp2(t_ref[...]), 0, keepdims=True)
         l_ref[:, cols] = part if rows.start == 0 else l_ref[:, cols] + part
 
     blocks(a_ref, b_ref, t_refs, 0, use)
-    least = jnp.min(l_ref[...])
-    l_ref[...] = jnp.log2(l_ref[...])
-
-    @pl.when(least < LEAST)
-    def _():
-        exact_logs(a_ref, b_ref, t_refs[0], l_ref)
 
 
 def by_coordinates(v, p):
@@ -148,11 +142,21 @@
     bound = jnp.max(lift, 1, keepdims=True) + 2 * C2 * longest
     a_ref[...] = first_side(y, lift).T
     b_ref[...] = second_side(x * (2 * C2), -bound)
-    log_sums(a_ref, b_ref, t_refs, l_ref)
-    total = l_ref[...] + bound
-    for k in range(out_ref.shape[1]):
+    plain_sums(a_ref, b_ref, t_refs, l_ref)
+    sums = l_ref[...]
+
+    def finish(logs):
+        total = logs + bound
+        tile = jnp.concatenate([cut(total, k) for k in range(out_ref.shape[1])], 0)
         for d in range(out_ref.shape[0]):
-            out_ref[d, k : k + 1, :] = cut(total, k)
+            out_ref[d] = tile
+
+    finish(jnp.log2(sums))
+
+    @pl.when(jnp.min(sums) < LEAST)
+    def _():
+        exact_logs(a_ref, b_ref, t_refs[0], l_ref)
+        finish(l_ref[...])
 
 
 def core_of(me_ref):
@@ -181,7 +185,15 @@
     b_ref[...] = second_side(y, -bound)
     weighted(a_ref, b_ref, v_ref, t_refs, o_ref)
     mass = o_ref[2 * K : 2 * K + 1, :]
-    l_ref[...] = jnp.log2(mass) + bound
+
+    def finish(logs):
+        share = 1.0 / o_ref[2 * K : 2 * K + 1, :]
+        for q in range(out_ref.shape[0]):
+            at = slice(q * LANES, (q + 1) * LANES)
+            out_ref[q, 0:K, :] = (o_ref[0:K, at] + o_ref[K : 2 * K, at]) * share[:, at]
+            out_ref[q, K : K + 8, :] = jnp.broadcast_to(logs[:, at], (8, LANES))
+
+    finish(jnp.log2(mass) + bound)
 
     @pl.when(jnp.min(mass) < LEAST)
     def _():
@@ -200,11 +212,7 @@
             return 0
 
         lax.fori_loop(0, half // wide, column, 0)
-
-    for q in range(out_ref.shape[0]):
-        at = slice(q * LANES, (q + 1) * LANES)
-        out_ref[q, 0:K, :] = (o_ref[0:K, at] + o_ref[K : 2 * K, at]) / o_ref[2 * K : 2 * K + 1, at]
-        out_ref[q, K : K + 8, :] = jnp.broadcast_to(l_ref[:, at], (8, LANES))
+        finish(l_ref[...])
 
 
 def merge(logs, images):
@@ -361,10 +369,10 @@
         (image,) = call(hold, "hv", [image.shape], aliases={0: 0}, out="h")(image, held)
         image = lax.all_to_all(image, chips, 0, 0, tiled=True)
         sizes = [held.shape]
-        (held,) = call(add, "vv", sizes, cost=work(ns * nt // 4, 2))(held, lax.ppermute(held, tgt, over))
         (held,) = call(add, "vv", sizes, cost=work(ns * nt // 4, 2))(held, lax.ppermute(held, tgt, near))
+        (held,) = call(add, "vv", sizes, cost=work(ns * nt // 4, 2))(held, lax.ppermute(held, tgt, far))
         (source_image,) = call(add_divide, "vv", [(K, ns)], cost=work(ns * nt // 4, 2))(
-            held, lax.ppermute(held, tgt, far)
+            held, lax.ppermute(held, tgt, over)
         )
         (image,) = call(hold, "vv", [image.shape], aliases={0: 0})(image, held)
         (target_image,) = call(lay_columns, "svv", [(K, nt)])(me, image, lax.ppermute(image, "core", swap))

time: 88 us -> 88.1 us (level)
    ppermute x1, waiting for transfers between devices: 0.01 us -> 5.14 us  [shards(): lax.ppermute(held, tgt, far)]
    ppermute x1, waiting for transfers between devices: 4.37 us -> 0.01 us  [shards(): lax.ppermute(held, tgt, near)]
where the time goes in v9:
time: 88.1 us; the launch traced here: 86.6 us
  blocking collectives  36.3 us (41%)
  Pallas kernels  30.5 us (35%)
  waiting for transfers between devices  11.5 us (13%)
  starting transfers between devices  7.64 us (9%)
    all_to_all x1, blocking collectives, shards(): image = lax.all_to_all(part, chips, 0, 0, tiled=True)  24.9 us
    pallas_call x1, Pallas kernels, shards(): call(row_logs, 'shhh', [(n_tgt, rows, LANES), x.shape, y.shape, g.shape],...  15.4 us
    all_to_all x1, blocking collectives, shards(): part = lax.all_to_all(part, tgt, 0, 0, tiled=True)  11.4 us
    pallas_call x1, Pallas kernels, shards(): call(functools.partial(row_images, math.log2(nt * n_tgt)), 'svvhvvv', [(1...  6.06 us
    all_to_all x1, starting transfers between devices, shards(): image = lax.all_to_all(image, chips, 0, 0, tiled=True)  5.45 us
    ppermute x1, waiting for transfers between devices, shards(): lax.ppermute(held, tgt, far)  5.14 us
    all_to_all x1, waiting for transfers between devices, shards(): image = lax.all_to_all(image, chips, 0, 0, tiled=True)  5.14 us
    pallas_call x1, Pallas kernels, shards(): call(functools.partial(column_sums, log_n, True), 'svvvv', [(1, ns), (1,...  3.6 us
  transfers between devices with their start and end apart: 7, of which 4 were waited for; matrix products, arithmetic and copies ran while one was open for 0% of the time, Pallas kernels for 5%

profile of v9, /device:TPU:32, one launch (start us, length us, event | category | flops | bytes accessed | tf_op | source)
XLA Modules:
  0.0 86.6 jit_solution(17478792011099392889)
XLA Ops:
  0.6 15.4 %shard_map.66 = (f32[8,8,128]{2,1,0:T(8,128)S(1)}, f32[32,1024]{1,0:T(8,128)S(1)}, f32[32,4096]{1,0:T(8,128)S(1)}, f32[1,4096]{1,0:T(1,128)S(1)}) custom-call(s32[1]{0:T(128)} %bitcast.me_ref, f32[32,1024]{1,0:T(8,128)} %x_hbm.1, f32[32,4096]{1,0:T(8,128)} %y_hbm.1, f32[1,4096]{1,0:T(1,128)} %bitcast.4), custom_call_target="tpu_custom_call" | custom-call | flops 2147483648 | bytes 33554432 | tf_op jit(solution)/shard_map/pallas_call | solution.py:331
  16.1 11.4 %all_to_all.15.from_ref = f32[8,8,128]{2,1,0:T(8,128)S(1)} all-to-all(f32[8,8,128]{2,1,0:T(8,128)S(1)} %get-tuple-element.18), channel_id=1, replica_groups=mesh['high'=2,'line'=8,'core'=2,'low'=2,'ring'=4] {'low','ring'}, dimensions={0} | all-to-all | bytes 65536 | tf_op jit(solution)/shard_map/all_to_all | solution.py:339
  27.4 3.6 %shard_map.67 = (f32[1,1024]{1,0:T(1,128)}, f32[1,1024]{1,0:T(1,128)S(1)}, f32[16,40,128]{2,1,0:T(8,128)S(1)}, bf16[1024,256]{1,0:T(8,128)(2,1)S(1)}, bf16[80,1024]{1,0:T(8,128)(2,1)S(1)}) custom-call(s32[1]{0:T(128)} %bitcast.me_ref, f32[32,1024]{1,0:T(8,128)S(1)} %get-tuple-element.15.x_ref, f32[32,4096]{1,0:T(8,128)S(1)} %get-tuple-element.16.y_ref, ...), custom_call_target="tpu_custom_call" | custom-call | flops 3221225472 | bytes 16777216 | tf_op jit(solution)/shard_map/pallas_call | solution.py:343
  31.0 0.0 collective-permute-start
  31.0 2.9 %shard_map.68.one_ref = f32[16,40,128]{2,1,0:T(8,128)S(1)} custom-call(s32[1]{0:T(128)} %bitcast.me_ref, f32[32,1024]{1,0:T(8,128)S(1)} %get-tuple-element.15.x_ref, f32[32,4096]{1,0:T(8,128)S(1)} %get-tuple-element.16.y_ref, f32[1,4096]{1,0:T(1,128)S(1)} %get-tuple-element.17.g_ref, f32[1,1024]{1,0:T(1,128)S(1)} %get-tuple-element.20.from_ref.total_ref, ...), custom_call_target="tpu_custom_call" | custom-call | flops 3221225472 | bytes 16777216 | tf_op jit(solution)/shard_map/pallas_call | solution.py:351
  34.0 0.0 collective-permute-done.two_ref
  34.0 0.1 shard_map.69
  34.1 24.9 %all_to_all.16.part_ref = f32[16,48,128]{2,1,0:T(8,128)S(1)} all-to-all(f32[16,48,128]{2,1,0:T(8,128)S(1)} %shard_map.69), channel_id=1, replica_groups=mesh['high'=2,'line'=8,'core'=2,'low'=2,'ring'=4] {'high','line'}, dimensions={0} | all-to-all | bytes 786432 | tf_op jit(solution)/shard_map/all_to_all | solution.py:355
  59.0 0.3 collective-permute-start.1
  59.3 0.8 shard_map.71.after_ref.image_ref
  60.1 0.4 collective-permute-done.1.other_ref
  60.5 6.1 %shard_map.72 = (f32[1,4096]{1,0:T(1,128)}, f32[264,128]{1,0:T(8,128)S(1)}) custom-call(s32[1]{0:T(128)} %bitcast.me_ref, f32[32,1024]{1,0:T(8,128)S(1)} %get-tuple-element.15.x_ref, f32[1,1024]{1,0:T(1,128)S(1)} %get-tuple-element.20.from_ref.total_ref, f32[16,32,128]{2,1,0:T(8,128)} %shard_map.71.after_ref.image_ref, ...), custom_call_target="tpu_custom_call" | custom-call | flops 6442450944 | bytes 33554432 | tf_op jit(solution)/shard_map/pallas_call | solution.py:362
  66.5 0.6 collective-permute-start.2
  67.2 5.4 %all-to-all-start.2 = ((f32[16,32,128]{2,1,0:T(8,128)}), f32[16,32,128]{2,1,0:T(8,128)S(1)}, u32[]{:S(2)}, u32[]{:S(2)}) async-start(f32[16,32,128]{2,1,0:T(8,128)} %shard_map.76), calls=%async_computation.2 | async-start | bytes 524288 | tf_op jit(solution)/shard_map/all_to_all | solution.py:370
  72.6 0.0 collective-permute-done.2.two_ref
  72.6 1.2 %collective-permute-start.3 = (f32[264,128]{1,0:T(8,128)S(1)}, f32[264,128]{1,0:T(8,128)S(1)}, u32[]{:S(2)}, u32[]{:S(2)}) collective-permute-start(f32[264,128]{1,0:T(8,128)S(1)} %shard_map.73.one_ref), channel_id=1, source_target_pairs={{0,3},{1,2},{2,1},{3,0},{4,7},{5,6},{6,5},{7,4},{8,11},{9,10},{10,... | collective-permute-start | bytes 405512 | tf_op jit(solution)/shard_map/ppermute | solution.py:373
  73.8 5.1 %collective-permute-done.3.two_ref = f32[264,128]{1,0:T(8,128)S(1)} collective-permute-done((f32[264,128]{1,0:T(8,128)S(1)}, f32[264,128]{1,0:T(8,128)S(1)}, u32[]{:S(2)}, u32[]{:S(2)}) %collective-permute-start.3) | collective-permute-done | bytes 135200 | tf_op jit(solution)/shard_map/ppermute | solution.py:373
  79.0 0.1 collective-permute-start.4
  79.1 5.1 %all-to-all-done.2.image_ref = f32[16,32,128]{2,1,0:T(8,128)S(1)} async-done(((f32[16,32,128]{2,1,0:T(8,128)}), f32[16,32,128]{2,1,0:T(8,128)S(1)}, u32[]{:S(2)}, u32[]{:S(2)}) %all-to-all-start.2) | async-done | bytes 262176 | tf_op jit(solution)/shard_map/all_to_all | solution.py:370
  84.2 0.0 collective-permute-start.5
  84.2 0.0 collective-permute-done.4.two_ref
  84.2 0.7 shard_map.75
  84.9 0.8 collective-permute-done.5.other_ref
  85.8 0.8 shard_map.78
  (5 shorter events, 0.1 us)
Async XLA Ops:
  31.0 2.9 %collective-permute-start = (f32[16,40,128]{2,1,0:T(8,128)S(1)}, f32[16,40,128]{2,1,0:T(8,128)S(1)}, u32[]{:S(2)}, u32[]{:S(2)}) collective-permute-start(f32[16,40,128]{2,1,0:T(8,128)S(1)} %get-tuple-element.23), channel_id=1, source_target_pairs={{0,8},{8,0},{1,9},{9,1},{2,10},{10,2},{3,11},{11,3},{4,12},{12,4},... | collective-permute-start | bytes 983048 | tf_op jit(solution)/shard_map/ppermute | solution.py:350
  59.0 1.4 %collective-permute-start.1 = (f32[16,128]{1,0:T(8,128)S(1)}, f32[16,128]{1,0:T(8,128)S(1)}, u32[]{:S(2)}, u32[]{:S(2)}) collective-permute-start(f32[16,128]{1,0:T(8,128)S(1)} %shard_map.70.after_ref.mine_ref), channel_id=1, source_target_pairs={{0,8},{8,0},{1,9},{9,1},{2,10},{10,2},{3,11},{11,3},{4,12},{12,4},... | collective-permute-start | bytes 24584 | tf_op jit(solution)/shard_map/ppermute | solution.py:357
  66.5 6.1 %collective-permute-start.2 = (f32[264,128]{1,0:T(8,128)S(1)}, f32[264,128]{1,0:T(8,128)S(1)}, u32[]{:S(2)}, u32[]{:S(2)}) collective-permute-start(f32[264,128]{1,0:T(8,128)S(1)} %get-tuple-element.25.one_ref.after_ref), channel_id=1, source_target_pairs={{0,1},{1,0},{2,3},{3,2},{4,5},{5,4},{6,7},{7,6},{8,9},{9,8},{10,11... | collective-permute-start | bytes 405512 | tf_op jit(solution)/shard_map/ppermute | solution.py:372
  67.2 17.0 %all-to-all-start.2 = ((f32[16,32,128]{2,1,0:T(8,128)}), f32[16,32,128]{2,1,0:T(8,128)S(1)}, u32[]{:S(2)}, u32[]{:S(2)}) async-start(f32[16,32,128]{2,1,0:T(8,128)} %shard_map.76), calls=%async_computation.2 | async-start | bytes 524288 | tf_op jit(solution)/shard_map/all_to_all | solution.py:370
  72.6 6.3 %collective-permute-start.3 = (f32[264,128]{1,0:T(8,128)S(1)}, f32[264,128]{1,0:T(8,128)S(1)}, u32[]{:S(2)}, u32[]{:S(2)}) collective-permute-start(f32[264,128]{1,0:T(8,128)S(1)} %shard_map.73.one_ref), channel_id=1, source_target_pairs={{0,3},{1,2},{2,1},{3,0},{4,7},{5,6},{6,5},{7,4},{8,11},{9,10},{10,... | collective-permute-start | bytes 405512 | tf_op jit(solution)/shard_map/ppermute | solution.py:373
  79.0 5.2 %collective-permute-start.4 = (f32[264,128]{1,0:T(8,128)S(1)}, f32[264,128]{1,0:T(8,128)S(1)}, u32[]{:S(2)}, u32[]{:S(2)}) collective-permute-start(f32[264,128]{1,0:T(8,128)S(1)} %shard_map.74.one_ref.after_ref), channel_id=1, source_target_pairs={{0,4},{1,5},{2,6},{3,7},{4,0},{5,1},{6,2},{7,3},{8,12},{9,13},{10,... | collective-permute-start | bytes 405512 | tf_op jit(solution)/shard_map/ppermute | solution.py:375
  84.2 1.5 %collective-permute-start.5 = (f32[16,32,128]{2,1,0:T(8,128)S(1)}, f32[16,32,128]{2,1,0:T(8,128)S(1)}, u32[]{:S(2)}, u32[]{:S(2)}) collective-permute-start(f32[16,32,128]{2,1,0:T(8,128)S(1)} %shard_map.77.mine_ref), channel_id=1, source_target_pairs={{0,8},{8,0},{1,9},{9,1},{2,10},{10,2},{3,11},{11,3},{4,12},{12,4},... | collective-permute-start | bytes 786440 | tf_op jit(solution)/shard_map/ppermute | solution.py:378

commit v10 on v9

--- a/solution.py
+++ b/solution.py
@@ -271,7 +271,9 @@
     out_ref[...] = one_ref[...] + two_ref[...]
 
 
-def add_divide(one_ref, two_ref, out_ref):
+def add_divide(one_ref, two_ref, src_ref, tgt_ref, out_ref, src_out_ref, tgt_out_ref):
+    src_out_ref[...] = src_ref[...]
+    tgt_out_ref[...] = tgt_ref[...]
     tiles = out_ref.shape[1] // LANES
     mass = one_ref[K * tiles :, :] + two_ref[K * tiles :, :]
     for k in range(tiles):
@@ -371,9 +373,9 @@
         sizes = [held.shape]
         (held,) = call(add, "vv", sizes, cost=work(ns * nt // 4, 2))(held, lax.ppermute(held, tgt, near))
         (held,) = call(add, "vv", sizes, cost=work(ns * nt // 4, 2))(held, lax.ppermute(held, tgt, far))
-        (source_image,) = call(add_divide, "vv", [(K, ns)], cost=work(ns * nt // 4, 2))(
-            held, lax.ppermute(held, tgt, over)
-        )
+        source_image, source_potential, target_potential = call(
+            add_divide, "vvvv", [(K, ns), (1, ns), (1, nt)], cost=work(ns * nt // 4, 2)
+        )(held, lax.ppermute(held, tgt, over), source_potential, target_potential)
         (image,) = call(hold, "vv", [image.shape], aliases={0: 0})(image, held)
         (target_image,) = call(lay_columns, "svv", [(K, nt)])(me, image, lax.ppermute(image, "core", swap))
         return source_potential.reshape(ns), target_potential.reshape(nt), source_image, target_image

time: 88.1 us -> 87.1 us (0.989)
  Pallas kernels: 30.5 us -> 29.3 us
where the time goes in v10:
time: 87.1 us; the launch traced here: 85.6 us
  blocking collectives  36.3 us (42%)
  Pallas kernels  29.3 us (34%)
  waiting for transfers between devices  11.5 us (13%)
  starting transfers between devices  7.78 us (9%)
    all_to_all x1, blocking collectives, shards(): image = lax.all_to_all(part, chips, 0, 0, tiled=True)  24.9 us
    pallas_call x1, Pallas kernels, shards(): call(row_logs, 'shhh', [(n_tgt, rows, LANES), x.shape, y.shape, g.shape],...  15.4 us
    all_to_all x1, blocking collectives, shards(): part = lax.all_to_all(part, tgt, 0, 0, tiled=True)  11.4 us
    pallas_call x1, Pallas kernels, shards(): call(functools.partial(row_images, math.log2(nt * n_tgt)), 'svvhvvv', [(1...  5.46 us
    all_to_all x1, starting transfers between devices, shards(): image = lax.all_to_all(image, chips, 0, 0, tiled=True)  5.43 us
    ppermute x1, waiting for transfers between devices, shards(): lax.ppermute(held, tgt, far)  5.15 us
    all_to_all x1, waiting for transfers between devices, shards(): image = lax.all_to_all(image, chips, 0, 0, tiled=True)  5.13 us
    pallas_call x1, Pallas kernels, shards(): call(functools.partial(column_sums, log_n, True), 'svvvv', [(1, ns), (1,...  3.01 us
  transfers between devices with their start and end apart: 7, of which 4 were waited for; matrix products, arithmetic and copies ran while one was open for 0% of the time, Pallas kernels for 5%

profile of v10, /device:TPU:32, one launch (start us, length us, event | category | flops | bytes accessed | tf_op | source)
XLA Modules:
  0.0 85.6 jit_solution(11260303410905626499)
XLA Ops:
  0.6 15.4 %shard_map.66 = (f32[8,8,128]{2,1,0:T(8,128)S(1)}, f32[32,1024]{1,0:T(8,128)S(1)}, f32[32,4096]{1,0:T(8,128)S(1)}, f32[1,4096]{1,0:T(1,128)S(1)}) custom-call(s32[1]{0:T(128)} %bitcast.me_ref, f32[32,1024]{1,0:T(8,128)} %x_hbm.1, f32[32,4096]{1,0:T(8,128)} %y_hbm.1, f32[1,4096]{1,0:T(1,128)} %bitcast.4), custom_call_target="tpu_custom_call" | custom-call | flops 2147483648 | bytes 33554432 | tf_op jit(solution)/shard_map/pallas_call | solution.py:333
  16.1 11.4 %all_to_all.15.from_ref = f32[8,8,128]{2,1,0:T(8,128)S(1)} all-to-all(f32[8,8,128]{2,1,0:T(8,128)S(1)} %get-tuple-element.21), channel_id=1, replica_groups=mesh['high'=2,'line'=8,'core'=2,'low'=2,'ring'=4] {'low','ring'}, dimensions={0} | all-to-all | bytes 65536 | tf_op jit(solution)/shard_map/all_to_all | solution.py:341
  27.4 3.0 %shard_map.67 = (f32[1,1024]{1,0:T(1,128)S(1)}, f32[1,1024]{1,0:T(1,128)S(1)}, f32[16,40,128]{2,1,0:T(8,128)S(1)}, bf16[1024,256]{1,0:T(8,128)(2,1)S(1)}, bf16[80,1024]{1,0:T(8,128)(2,1)S(1)}) custom-call(s32[1]{0:T(128)} %bitcast.me_ref, f32[32,1024]{1,0:T(8,128)S(1)} %get-tuple-element.18.x_ref, f32[32,4096]{1,0:T(8,128)S(1)} %get-tuple-element.19.y_ref, ...), custom_call_target="tpu_custom_call" | custom-call | flops 3221225472 | bytes 16777216 | tf_op jit(solution)/shard_map/pallas_call | solution.py:345
  30.5 0.1 collective-permute-start
  30.6 2.9 %shard_map.68.one_ref = f32[16,40,128]{2,1,0:T(8,128)S(1)} custom-call(s32[1]{0:T(128)} %bitcast.me_ref, f32[32,1024]{1,0:T(8,128)S(1)} %get-tuple-element.18.x_ref, f32[32,4096]{1,0:T(8,128)S(1)} %get-tuple-element.19.y_ref, f32[1,4096]{1,0:T(1,128)S(1)} %get-tuple-element.20.g_ref, f32[1,1024]{1,0:T(1,128)S(1)} %get-tuple-element.22.from_ref.total_ref, ...), custom_call_target="tpu_custom_call" | custom-call | flops 3221225472 | bytes 16777216 | tf_op jit(solution)/shard_map/pallas_call | solution.py:353
  33.5 0.0 collective-permute-done.two_ref
  33.5 0.1 shard_map.69
  33.6 24.9 %all_to_all.16.part_ref = f32[16,48,128]{2,1,0:T(8,128)S(1)} all-to-all(f32[16,48,128]{2,1,0:T(8,128)S(1)} %shard_map.69), channel_id=1, replica_groups=mesh['high'=2,'line'=8,'core'=2,'low'=2,'ring'=4] {'high','line'}, dimensions={0} | all-to-all | bytes 786432 | tf_op jit(solution)/shard_map/all_to_all | solution.py:357
  58.5 0.3 collective-permute-start.1
  58.8 0.8 shard_map.71.after_ref.image_ref
  59.6 0.4 collective-permute-done.1.other_ref
  60.0 5.5 %shard_map.72 = (f32[1,4096]{1,0:T(1,128)S(1)}, f32[264,128]{1,0:T(8,128)S(1)}) custom-call(s32[1]{0:T(128)} %bitcast.me_ref, f32[32,1024]{1,0:T(8,128)S(1)} %get-tuple-element.18.x_ref, f32[1,1024]{1,0:T(1,128)S(1)} %get-tuple-element.22.from_ref.total_ref, f32[16,32,128]{2,1,0:T(8,128)} %shard_map.71.after_ref.image_ref, ...), custom_call_target="tpu_custom_call" | custom-call | flops 6442450944 | bytes 33554432 | tf_op jit(solution)/shard_map/pallas_call | solution.py:364
  65.4 0.7 collective-permute-start.2
  66.2 5.4 %all-to-all-start.2 = ((f32[16,32,128]{2,1,0:T(8,128)}), f32[16,32,128]{2,1,0:T(8,128)S(1)}, u32[]{:S(2)}, u32[]{:S(2)}) async-start(f32[16,32,128]{2,1,0:T(8,128)} %shard_map.76), calls=%async_computation.2 | async-start | bytes 524288 | tf_op jit(solution)/shard_map/all_to_all | solution.py:372
  71.6 0.0 collective-permute-done.2.two_ref
  71.6 1.2 %collective-permute-start.3 = (f32[264,128]{1,0:T(8,128)S(1)}, f32[264,128]{1,0:T(8,128)S(1)}, u32[]{:S(2)}, u32[]{:S(2)}) collective-permute-start(f32[264,128]{1,0:T(8,128)S(1)} %shard_map.73.one_ref), channel_id=1, source_target_pairs={{0,3},{1,2},{2,1},{3,0},{4,7},{5,6},{6,5},{7,4},{8,11},{9,10},{10,... | collective-permute-start | bytes 405512 | tf_op jit(solution)/shard_map/ppermute | solution.py:375
  72.8 5.1 %collective-permute-done.3.two_ref = f32[264,128]{1,0:T(8,128)S(1)} collective-permute-done((f32[264,128]{1,0:T(8,128)S(1)}, f32[264,128]{1,0:T(8,128)S(1)}, u32[]{:S(2)}, u32[]{:S(2)}) %collective-permute-start.3) | collective-permute-done | bytes 135200 | tf_op jit(solution)/shard_map/ppermute | solution.py:375
  78.0 0.1 collective-permute-start.4
  78.1 5.1 %all-to-all-done.2.image_ref = f32[16,32,128]{2,1,0:T(8,128)S(1)} async-done(((f32[16,32,128]{2,1,0:T(8,128)}), f32[16,32,128]{2,1,0:T(8,128)S(1)}, u32[]{:S(2)}, u32[]{:S(2)}) %all-to-all-start.2) | async-done | bytes 262176 | tf_op jit(solution)/shard_map/all_to_all | solution.py:372
  83.2 0.0 collective-permute-start.5
  83.2 0.0 collective-permute-done.4.two_ref
  83.2 0.7 shard_map.75
  83.9 0.8 collective-permute-done.5.other_ref
  84.7 0.8 shard_map.78
  (5 shorter events, 0.1 us)
Async XLA Ops:
  30.5 3.0 %collective-permute-start = (f32[16,40,128]{2,1,0:T(8,128)S(1)}, f32[16,40,128]{2,1,0:T(8,128)S(1)}, u32[]{:S(2)}, u32[]{:S(2)}) collective-permute-start(f32[16,40,128]{2,1,0:T(8,128)S(1)} %get-tuple-element.25), channel_id=1, source_target_pairs={{0,8},{8,0},{1,9},{9,1},{2,10},{10,2},{3,11},{11,3},{4,12},{12,4},... | collective-permute-start | bytes 983048 | tf_op jit(solution)/shard_map/ppermute | solution.py:352
  58.5 1.4 %collective-permute-start.1 = (f32[16,128]{1,0:T(8,128)S(1)}, f32[16,128]{1,0:T(8,128)S(1)}, u32[]{:S(2)}, u32[]{:S(2)}) collective-permute-start(f32[16,128]{1,0:T(8,128)S(1)} %shard_map.70.after_ref.mine_ref), channel_id=1, source_target_pairs={{0,8},{8,0},{1,9},{9,1},{2,10},{10,2},{3,11},{11,3},{4,12},{12,4},... | collective-permute-start | bytes 24584 | tf_op jit(solution)/shard_map/ppermute | solution.py:359
  65.4 6.2 %collective-permute-start.2 = (f32[264,128]{1,0:T(8,128)S(1)}, f32[264,128]{1,0:T(8,128)S(1)}, u32[]{:S(2)}, u32[]{:S(2)}) collective-permute-start(f32[264,128]{1,0:T(8,128)S(1)} %get-tuple-element.26.one_ref.after_ref), channel_id=1, source_target_pairs={{0,1},{1,0},{2,3},{3,2},{4,5},{5,4},{6,7},{7,6},{8,9},{9,8},{10,11... | collective-permute-start | bytes 405512 | tf_op jit(solution)/shard_map/ppermute | solution.py:374
  66.2 17.0 %all-to-all-start.2 = ((f32[16,32,128]{2,1,0:T(8,128)}), f32[16,32,128]{2,1,0:T(8,128)S(1)}, u32[]{:S(2)}, u32[]{:S(2)}) async-start(f32[16,32,128]{2,1,0:T(8,128)} %shard_map.76), calls=%async_computation.2 | async-start | bytes 524288 | tf_op jit(solution)/shard_map/all_to_all | solution.py:372
  71.6 6.3 %collective-permute-start.3 = (f32[264,128]{1,0:T(8,128)S(1)}, f32[264,128]{1,0:T(8,128)S(1)}, u32[]{:S(2)}, u32[]{:S(2)}) collective-permute-start(f32[264,128]{1,0:T(8,128)S(1)} %shard_map.73.one_ref), channel_id=1, source_target_pairs={{0,3},{1,2},{2,1},{3,0},{4,7},{5,6},{6,5},{7,4},{8,11},{9,10},{10,... | collective-permute-start | bytes 405512 | tf_op jit(solution)/shard_map/ppermute | solution.py:375
  78.0 5.2 %collective-permute-start.4 = (f32[264,128]{1,0:T(8,128)S(1)}, f32[264,128]{1,0:T(8,128)S(1)}, u32[]{:S(2)}, u32[]{:S(2)}) collective-permute-start(f32[264,128]{1,0:T(8,128)S(1)} %shard_map.74.one_ref.after_ref), channel_id=1, source_target_pairs={{0,4},{1,5},{2,6},{3,7},{4,0},{5,1},{6,2},{7,3},{8,12},{9,13},{10,... | collective-permute-start | bytes 405512 | tf_op jit(solution)/shard_map/ppermute | solution.py:378
  83.2 1.5 %collective-permute-start.5 = (f32[16,32,128]{2,1,0:T(8,128)S(1)}, f32[16,32,128]{2,1,0:T(8,128)S(1)}, u32[]{:S(2)}, u32[]{:S(2)}) collective-permute-start(f32[16,32,128]{2,1,0:T(8,128)S(1)} %shard_map.77.mine_ref), channel_id=1, source_target_pairs={{0,8},{8,0},{1,9},{9,1},{2,10},{10,2},{3,11},{11,3},{4,12},{12,4},... | collective-permute-start | bytes 786440 | tf_op jit(solution)/shard_map/ppermute | solution.py:380
